TPU v7x, 32 devices: a whole 2x2x4 slice. The times are simulated.
32 devices in a mesh: tm: 16 (over z, y, x), head: 2 (over core).
Axes of the slice: x: 2, y: 2, z: 4, core: 2. Of those that a mesh axis runs over, the one named last changes fastest.
Arguments:
- series: bfloat16 [16, 16384, 512], P(None, 'tm'), may hold values from -6 to 6
- modes: int32 [128], replicated, may hold values from 1 to 8191, as said below
- query_weight: bfloat16 [512, 512], P(None, 'head'), may hold values from -0.25 to 0.25
- mix_weight: float32 [128, 8, 64, 128], P('tm', 'head'), may hold values from -0.5 to 0.5
- out_weight: bfloat16 [512, 512], P(None, 'head'), may hold values from -0.25 to 0.25
Outputs:
- output: bfloat16 [16, 16384, 512], P(None, 'tm', 'head')
Inputs may be any that keep to these rules, and one draw needn't show every extreme that they name: `modes`: distinct mode numbers; both 1 and one less than half of 16384 are among them.
All inputs are finite; a program needn't handle non-finite values.
Results may differ from a plain program's by a relative error of at most 0.0075.
Values may be sent and summed in bfloat16 or wider, within the bound.
No kernel may reach another device: no remote copies, remote signals or barrier semaphores. Data moves between devices by JAX's collectives and lax.ppermute only.
A program may use at most 128 MiB of HBM per device.

v0:
```python
import math

import jax
import jax.numpy as jnp
from jax import lax
from jax.sharding import PartitionSpec as P

two_pi = 2.0 * math.pi


def wave_tables(mode_list, first_time, time_count, series_length):
    time_index = first_time + lax.iota(jnp.int32, time_count)
    phases = time_index[:, None] * mode_list[None, :] % series_length
    angles = phases.astype(jnp.float32) * (two_pi / series_length)
    return (jnp.cos(angles).astype(jnp.bfloat16), jnp.sin(angles).astype(jnp.bfloat16))


def body(series, modes, query_weight, mix_weight, out_weight):
    series_count, shard_rows, model_width = series.shape
    group_width = query_weight.shape[1]
    mode_total = modes.shape[0]
    own_modes = mix_weight.shape[0]
    heads_here = mix_weight.shape[1]
    head_size = mix_weight.shape[2]
    series_length = lax.axis_size("tm") * shard_rows
    first_time = lax.axis_index("tm") * shard_rows
    forward_scale = 1.0 / math.sqrt(series_length)
    inverse_scale = 1.0 / math.sqrt(mode_total)
    queries = jnp.dot(
        series.reshape(series_count * shard_rows, model_width),
        query_weight,
        preferred_element_type=jnp.float32,
    )
    queries = queries.astype(jnp.bfloat16).reshape(series_count, shard_rows, group_width)
    cosine, sine_part = wave_tables(modes, first_time, shard_rows, series_length)
    real_part = jnp.einsum("tm,btf->mbf", cosine, queries, preferred_element_type=jnp.float32)
    imag_part = jnp.einsum("tm,btf->mbf", sine_part, queries, preferred_element_type=jnp.float32)
    summed_all = lax.psum(jnp.stack([real_part, -imag_part], axis=1) * forward_scale, "tm")
    spectrum = lax.dynamic_slice_in_dim(summed_all, lax.axis_index("tm") * own_modes, own_modes, 0)
    spec_parts = spectrum.reshape(own_modes, 2, series_count, heads_here, head_size)
    from_real = jnp.einsum(
        "mbhi,mhio->mbho", spec_parts[:, 0], mix_weight, precision=lax.Precision.HIGHEST
    )
    from_imag = jnp.einsum(
        "mbhi,mhio->mbho", spec_parts[:, 1], mix_weight, precision=lax.Precision.HIGHEST
    )
    mixed_real = from_real[..., :head_size] - from_imag[..., head_size:]
    mixed_imag = from_real[..., head_size:] + from_imag[..., :head_size]
    mixed_spectra = jnp.stack([mixed_real, mixed_imag], axis=1).reshape(
        own_modes, 2, series_count, group_width
    )
    mixed_spectra = mixed_spectra.astype(jnp.bfloat16)
    cosine, sine_part = wave_tables(modes, first_time, shard_rows, series_length)
    wave_table = jnp.concatenate([cosine, -sine_part], axis=1)
    by_mode = lax.all_gather(mixed_spectra, "tm", axis=0, tiled=True)
    all_spectra = lax.all_gather(by_mode, "head", axis=3, tiled=True)
    stacked = jnp.concatenate([all_spectra[:, 0], all_spectra[:, 1]], axis=0)
    summed = jnp.einsum("tk,kbf->btf", wave_table, stacked, preferred_element_type=jnp.float32)
    restored = (summed * inverse_scale).astype(jnp.bfloat16)
    output = jnp.dot(
        restored.reshape(series_count * shard_rows, model_width),
        out_weight,
        preferred_element_type=jnp.float32,
    )
    return output.astype(jnp.bfloat16).reshape(series_count, shard_rows, group_width)


def solution(mesh):
    in_specs = (
        P(None, "tm", None),
        P(),
        P(None, "head"),
        P("tm", "head", None, None),
        P(None, "head"),
    )
    out_specs = P(None, "tm", "head")
    return jax.shard_map(body, mesh=mesh, in_specs=in_specs, out_specs=out_specs, check_vma=False)
```

profile of v0, /device:TPU:0, one launch (start us, length us, event | category | flops | bytes accessed | tf_op | source)
XLA Modules:
  0.0 330.8 jit_solution(13637485986639025161)
XLA Ops:
  6.6 10.4 %convolution_convert_fusion.1 = bf16[16384,256]{1,0:T(8,128)(2,1)S(1)} fusion(bf16[16384,512]{1,0:T(8,128)(2,1)} %bitcast.52, bf16[512,256]{1,0:T(8,128)(2,1)} %param.7), kind=kOutput, calls=%fused_computation.2 | convolution fusion | flops 4299161600 | bytes 25427968 | tf_op jit(solution)/shard_map/dot_general | solution.py:29
  17.0 3.0 negate_bitcast_fusion
  20.0 3.0 convolution_bitcast_fusion
  23.0 2.4 maximum_multiply_fusion
  25.4 0.2 all-gather.3.cloned.1.call-start
  25.6 170.8 %all-reduce.2.cloned.1.call-done = f32[128,2,16,256]{3,0,2,1:T(8,128)} async-done(((f32[128,2,16,256]{3,0,2,1:T(8,128)}), f32[128,2,16,256]{3,0,2,1:T(8,128)}) %all-reduce.2.cloned.1.call-update) | async-done | bytes 4194320 | tf_op jit(solution)/shard_map/psum | solution.py:38
  196.4 1.0 constant_dynamic-slice_fusion
  197.4 0.2 reshape.35
  197.7 1.2 convolution_bitcast_fusion.2
  198.9 1.2 convolution_bitcast_fusion.1
  200.0 0.2 fusion.10
  200.2 0.1 copy.23
  200.3 0.1 stack.21
  200.5 0.1 stack.22
  200.7 0.7 pad_maximum_fusion
  201.4 59.7 %all-gather.3.cloned.1.call-done = bf16[128,2,16,256]{3,2,1,0:T(8,128)(2,1)} async-done(((bf16[8,2,16,256]{3,2,1,0:T(8,128)(2,1)}), bf16[128,2,16,256]{3,2,1,0:T(8,128)(2,1)}) %all-gather.3.cloned.1.call-update) | async-done | bytes 2097168 | tf_op jit(solution)/shard_map/all_gather | solution.py:55
  261.1 4.5 %copy.27 = bf16[128,2,16,256]{0,3,2,1:T(8,128)(2,1)} copy(bf16[128,2,16,256]{3,2,1,0:T(8,128)(2,1)} %all-gather.3.cloned.1.call-done) | data formatting | bytes 4194304 | tf_op jit(solution)/shard_map/all_gather | solution.py:55
  265.7 2.3 fusion.13
  268.0 2.3 cosine_convert_fusion
  270.2 7.9 %all-gather.5.cloned.1.call-done = bf16[128,2,16,512]{0,3,2,1:T(8,128)(2,1)} async-done(((bf16[128,2,16,256]{0,3,2,1:T(8,128)(2,1)}), bf16[128,2,16,512]{0,3,2,1:T(8,128)(2,1)}) %all-gather.5.cloned.1.call-update) | async-done | bytes 4194320 | tf_op jit(solution)/shard_map/all_gather | solution.py:56
  278.2 2.5 slice_bitcast_fusion.1
  280.7 8.1 %fusion = bf16[16,1024,512]{1,2,0:T(8,128)(2,1)} fusion(bf16[128,16,512]{0,2,1:T(8,128)(2,1)S(1)} %get-tuple-element.6, bf16[128,16,512]{0,2,1:T(8,128)(2,1)S(1)} %get-tuple-element.5, bf16[1024,128]{1,0:T(8,128)(2,1)S(1)} %fusion.13, bf16[1024,128]{1,0:T(8,128)(2,1)S(1)} %cosine_convert_fusion), kind=kOutput, calls=%fused_computation.3 | convolution fusion | flops 4321181696 | bytes 21495808 | tf_op jit(solution)/shard_map/tk,kbf->btf/dot_general | solution.py:58
  288.8 21.6 %copy.28 = bf16[16,1024,512]{2,1,0:T(8,128)(2,1)} copy(bf16[16,1024,512]{1,2,0:T(8,128)(2,1)} %fusion) | data formatting | bytes 33554432 | tf_op jit(solution)/shard_map/convert_element_type | solution.py:59
  310.5 13.8 %convolution_convert_fusion = bf16[16384,256]{1,0:T(8,128)(2,1)} fusion(bf16[16384,512]{1,0:T(8,128)(2,1)} %bitcast.49, bf16[512,256]{1,0:T(8,128)(2,1)S(1)} %copy-done.3), kind=kOutput, calls=%fused_computation.1 | convolution fusion | flops 4299161600 | bytes 25427968 | tf_op jit(solution)/shard_map/dot_general | solution.py:60
  (16 shorter events, 0.2 us)
Async XLA Ops:
  6.5 191.2 %copy-start = (f32[8,4,64,128]{3,2,1,0:T(8,128)S(1)}, f32[8,4,64,128]{3,2,1,0:T(8,128)}, u32[]{:S(2)}) copy-start(f32[8,4,64,128]{3,2,1,0:T(8,128)} %param.8) | copy-start | bytes 3145732
  6.5 189.9 %all-reduce.2.cloned.1.call-start = ((), (), s32[]{:S(2)}) async-start(), calls=%async_computation | async-start | bytes 8388608 | tf_op jit(solution)/shard_map/psum | solution.py:38
  6.5 10.4 %copy-start.2 = (s32[128]{0:T(128)S(1)}, s32[128]{0:T(128)}, u32[]{:S(2)}) copy-start(s32[128]{0:T(128)} %param.6) | copy-start | bytes 1540
  25.4 235.7 %all-gather.3.cloned.1.call-start = ((), (), s32[]{:S(2)}) async-start(), calls=%async_computation.1 | async-start | bytes 2228224 | tf_op jit(solution)/shard_map/all_gather | solution.py:55
  201.4 76.8 %all-gather.5.cloned.1.call-start = ((), (), s32[]{:S(2)}) async-start(), calls=%async_computation.2 | async-start | bytes 6291456 | tf_op jit(solution)/shard_map/all_gather | solution.py:56
  288.8 21.6 %copy-start.3 = (bf16[512,256]{1,0:T(8,128)(2,1)S(1)}, bf16[512,256]{1,0:T(8,128)(2,1)}, u32[]{:S(2)}) copy-start(bf16[512,256]{1,0:T(8,128)(2,1)} %param.9) | copy-start | bytes 786436
  310.5 13.8 %copy-start.1 = (f32[8,4,64,128]{3,2,1,0:T(8,128)S(1)}, f32[8,4,64,128]{3,2,1,0:T(8,128)}, u32[]{:S(2)}) copy-start(f32[8,4,64,128]{3,2,1,0:T(8,128)} %param.8) | copy-start | bytes 3145732
Sparse Core Ops, SparseCore 0:
  25.5 170.8 all-reduce.1
  201.5 59.6 all-gather.2
  265.8 12.3 all-gather.4
where the time goes:
time: 332 us; the launch traced here: 331 us
  waiting for transfers between devices  239 us (72%)
  matrix products  40.7 us (12%)
  local copies, waits for them, and re-layouts  30.3 us (9%)
  between operations  13.2 us (4%)
  other arithmetic  7.83 us (2%)
    psum x1, waiting for transfers between devices, body(): lax.psum(jnp.stack([real_part, -imag_part], axis=1) * forward_scale, 'tm')  171 us
    all_gather x1, waiting for transfers between devices, body(): by_mode = lax.all_gather(mixed_spectra, 'tm', axis=0, tiled=True)  59.7 us
    convert_element_type x1, local copies, waits for them, and re-layouts, body(): restored = (summed * inverse_scale).astype(jnp.bfloat16)  21.6 us
    dot_general x1, matrix products, body(): jnp.dot(restored.reshape(series_count * shard_rows, model_width), out_wei...  13.8 us
    dot_general x1, matrix products, body(): jnp.dot(series.reshape(series_count * shard_rows, model_width), query_wei...  10.4 us
    dot_general x1, matrix products, body(): jnp.einsum('tk,kbf->btf', wave_table, stacked, preferred_element_type=jnp...  8.15 us
    all_gather x1, waiting for transfers between devices, body(): all_spectra = lax.all_gather(by_mode, 'head', axis=3, tiled=True)  7.92 us
  transfers between devices with their start and end apart: 3, of which 3 were waited for; matrix products, arithmetic and copies ran while one was open for 1% of the time, Pallas kernels for 0%

commit v1 on v0

v1 whole, which is shorter than its diff:
```python
import functools
import math

import jax
import jax.numpy as jnp
from jax import lax
from jax.experimental import pallas as pl
from jax.experimental.pallas import tpu as pltpu
from jax.sharding import PartitionSpec as P

f32 = jnp.float32
bf16 = jnp.bfloat16
two_pi = 2.0 * math.pi


def row_modes(place, modes_row, rows, own_modes, series_length):
    lanes = modes_row.shape[1]
    row = lax.broadcasted_iota(jnp.int32, (rows, lanes), 0)
    lane = lax.broadcasted_iota(jnp.int32, (rows, lanes), 1)
    block_rows = 2 * own_modes
    far = rows // block_rows // 4
    block = row // block_rows
    inside = row - block * block_rows
    quarter = block // far
    relative = (quarter // 2) + 2 * (quarter % 2) + 4 * (block % far)
    imaginary = inside // own_modes
    wanted = (place ^ relative) * own_modes + inside - imaginary * own_modes
    picked = jnp.where(lane == wanted, modes_row.astype(f32), 0.0)
    mode = jnp.sum(picked, axis=1, keepdims=True).astype(jnp.int32)
    return mode, imaginary[:, :1] * (series_length // 4)


def wave(phases, series_length):
    turns = phases.astype(f32) * (1.0 / series_length)
    quarters = jnp.floor(turns * 4.0 + 0.5)
    angle = (turns - quarters * 0.25) * two_pi
    square = angle * angle
    cosine = 1.0 + square * (-0.5 + square * (1 / 24 + square * (-1 / 720 + square * (1 / 40320))))
    sine = angle * (1.0 + square * (-1 / 6 + square * (1 / 120 + square * (-1 / 5040))))
    which = quarters.astype(jnp.int32)
    size = jnp.where(which & 1 == 0, cosine, sine)
    return jnp.where((which == 1) | (which == 2), -size, size)


def forward_kernel(first, own_modes, series_length, place_ref, *refs):
    if first:
        modes_ref, series_ref, send_ref, keep_ref, table_ref = refs
        rows, time_count = table_ref.shape

        @pl.when(pl.program_id(0) == 0)
        def _():
            place = place_ref[0]
            mode, shift = row_modes(place, modes_ref[...], rows, own_modes, series_length)
            step = 16
            for start in range(0, rows, step):
                time_index = place * time_count + lax.broadcasted_iota(jnp.int32, (step, time_count), 1)
                phases = time_index * mode[start:start + step] + shift[start:start + step]
                phases = phases & (series_length - 1)
                table_ref[start:start + step, :] = wave(phases, series_length).astype(bf16)
    else:
        table_ref, series_ref, send_ref, keep_ref = refs
    part = jnp.dot(table_ref[...], series_ref[0], preferred_element_type=f32)
    q = part.shape[0] // 4
    if first:
        send_ref[0] = part[2 * q:].astype(bf16)
        keep_ref[0] = part[:2 * q]
    else:
        send_ref[0, :q] = part[q:2 * q].astype(bf16)
        send_ref[0, q:] = part[3 * q:].astype(bf16)
        keep_ref[0, :q] = part[:q]
        keep_ref[0, q:] = part[2 * q:3 * q]


def forward(first, series, place, extra, count, half, own_modes, series_length, rows):
    _, time_count, width = series.shape
    offset = 0 if first else count
    series_spec = pl.BlockSpec((1, time_count, width), lambda b, p: (p[1] * half + offset + b, 0, 0))
    table_spec = pl.BlockSpec((rows, time_count), lambda b, p: (0, 0))
    part_spec = pl.BlockSpec((1, rows // 2, width), lambda b, p: (b, 0, 0))
    outs = [jax.ShapeDtypeStruct((count, rows // 2, width), bf16), jax.ShapeDtypeStruct((count, rows // 2, width), f32)]
    out_specs = [part_spec, part_spec]
    if first:
        in_specs = [pl.BlockSpec(extra.shape, lambda b, p: (0, 0)), series_spec]
        outs.append(jax.ShapeDtypeStruct((rows, time_count), bf16))
        out_specs.append(table_spec)
    else:
        in_specs = [table_spec, series_spec]
    return pl.pallas_call(
        functools.partial(forward_kernel, first, own_modes, series_length),
        out_shape=outs,
        grid_spec=pltpu.PrefetchScalarGridSpec(num_scalar_prefetch=1, grid=(count,), in_specs=in_specs, out_specs=out_specs),
        compiler_params=pltpu.CompilerParams(vmem_limit_bytes=24 * 2**20),
        cost_estimate=pl.CostEstimate(
            flops=2 * count * rows * time_count * width,
            bytes_accessed=count * (time_count * width * 2 + rows * width * 3),
            transcendentals=0,
        ),
        name="forward_first" if first else "forward_second",
    )(place, extra, series)


def split_rows(value):
    high = value.astype(bf16)
    low = (value - high.astype(f32)).astype(bf16)
    return jnp.concatenate([high, low], axis=0)


def fold_rows(value):
    half = value.shape[0] // 2
    return value[:half] + value[half:]


def mix_kernel(scale, own_modes, arrivals, own_ref, *refs):
    arrived = refs[:arrivals]
    query_ref, mix_ref, out_weight_ref, here_ref, there_ref = refs[arrivals:]
    total = own_ref[...]
    for ref in arrived:
        total = total + ref[...].astype(f32)
    total = total * scale
    count, _, width = total.shape
    rows = count * own_modes
    heads = mix_ref.shape[0]
    spectrum = jnp.concatenate(
        [total[:, :own_modes].reshape(rows, width), total[:, own_modes:].reshape(rows, width)], axis=0
    )
    queries = fold_rows(jnp.dot(split_rows(spectrum), query_ref[...], preferred_element_type=f32))
    lower = lax.broadcasted_iota(jnp.int32, (rows, 128), 1) < 64
    row_mode = lax.broadcasted_iota(jnp.int32, (2 * rows, 128), 0) % own_modes
    mixed_real, mixed_imag = [], []
    for pair in range(heads // 2):
        columns = slice(pair * 128, pair * 128 + 128)
        real, imag = queries[:rows, columns], queries[rows:, columns]
        both = [
            jnp.where(lower, real, pltpu.roll(imag, 64, 1)),
            jnp.where(lower, pltpu.roll(real, 64, 1), imag),
        ]
        mixed = []
        for which in range(2):
            pieces = split_rows(both[which])
            zero = jnp.zeros_like(pieces)
            spread = jnp.concatenate([jnp.where(row_mode == k, pieces, zero) for k in range(own_modes)], axis=1)
            mixed.append(fold_rows(jnp.dot(spread, mix_ref[2 * pair + which], preferred_element_type=f32)))
        mixed_real.append(jnp.where(lower, mixed[0], pltpu.roll(mixed[1], 64, 1)))
        mixed_imag.append(jnp.where(lower, pltpu.roll(mixed[0], 64, 1), mixed[1]))
    mixed = jnp.concatenate([jnp.concatenate(mixed_real, axis=1), jnp.concatenate(mixed_imag, axis=1)], axis=0)
    result = fold_rows(jnp.dot(split_rows(mixed), out_weight_ref[...], preferred_element_type=f32)).astype(bf16)
    here = here_ref.shape[2]
    both = jnp.concatenate(
        [result[:rows].reshape(count, own_modes, width), result[rows:].reshape(count, own_modes, width)], axis=1
    )
    here_ref[...] = both[:, :, :here]
    there_ref[...] = both[:, :, here:]


def mix(own, arrived, query_full, mix_full, out_full, scale, own_modes):
    count, block_rows, width = own.shape
    here = width // 2
    heads = mix_full.shape[0]
    if own_modes % 8 == 0:
        shape = jax.ShapeDtypeStruct((count, block_rows, here), bf16)
        return pl.pallas_call(
            functools.partial(mix_kernel, scale, own_modes, len(arrived)),
            out_shape=[shape, shape],
            compiler_params=pltpu.CompilerParams(vmem_limit_bytes=32 * 2**20),
            cost_estimate=pl.CostEstimate(flops=3 * 10**9, bytes_accessed=4 * 2**20, transcendentals=0),
            name="mix_modes",
        )(own, *arrived, query_full, mix_full, out_full)
    total = (own + sum(piece.astype(f32) for piece in arrived)) * scale
    queries = jnp.einsum("brf,fg->brg", total, query_full.astype(f32), precision=lax.Precision.HIGHEST)
    queries = queries.reshape(count, 2, own_modes, heads, 64)
    weights = mix_full.reshape(heads, own_modes, 2, 64, 2, 64).astype(f32)
    mixed = jnp.einsum("brmhi,hmriso->bsmho", queries, weights, precision=lax.Precision.HIGHEST)
    mixed = mixed.reshape(count, block_rows, width)
    result = jnp.einsum("brf,fg->brg", mixed, out_full.astype(f32), precision=lax.Precision.HIGHEST).astype(bf16)
    return result[:, :, :here], result[:, :, here:]


def inverse_kernel(scale, aliased, place_ref, table_ref, *refs):
    pieces, out_ref = refs[:4], refs[-1]
    spectra = jnp.concatenate([piece[0] for piece in pieces], axis=0)
    result = jnp.dot(table_ref[...], spectra, preferred_element_type=f32) * scale
    out_ref[0] = result.astype(bf16)


def inverse(place, table, pieces, previous, series_count, half, offset, scale):
    time_count, rows = table.shape
    count, quarter, width = pieces[0].shape
    own = count // 2
    piece_spec = pl.BlockSpec((1, quarter, width), lambda b, p: (b, 0, 0))
    in_specs = [pl.BlockSpec((time_count, rows), lambda b, p: (0, 0))] + [piece_spec] * 4
    args = [place, table, *pieces]
    aliases = {}
    if previous is not None:
        in_specs.append(pl.BlockSpec(memory_space=pl.ANY))
        aliases = {len(args): 0}
        args.append(previous)
    return pl.pallas_call(
        functools.partial(inverse_kernel, scale, previous is not None),
        out_shape=jax.ShapeDtypeStruct((series_count, time_count, width), bf16),
        grid_spec=pltpu.PrefetchScalarGridSpec(
            num_scalar_prefetch=1,
            grid=(count,),
            in_specs=in_specs,
            out_specs=pl.BlockSpec(
                (1, time_count, width), lambda b, p: ((p[1] ^ (b // own)) * half + offset + b % own, 0, 0)
            ),
        ),
        input_output_aliases=aliases,
        compiler_params=pltpu.CompilerParams(vmem_limit_bytes=24 * 2**20),
        cost_estimate=pl.CostEstimate(
            flops=2 * count * time_count * rows * width,
            bytes_accessed=count * (time_count * width * 2 + rows * width * 2),
            transcendentals=0,
        ),
        name="inverse_second" if previous is not None else "inverse_first",
    )(*args)


def to_device(value, mask, size):
    return lax.ppermute(value, "tm", [(i, i ^ mask) for i in range(size)])


def to_core(value):
    return lax.ppermute(value, "head", [(0, 1), (1, 0)])


def reduce_scatter(send, keep, masks, size, block_rows):
    q = keep.shape[1] // 2
    arrived = to_device(send, masks[0], size)
    onward = (keep[:, q:] + arrived[:, q:].astype(f32)).astype(bf16)
    second = to_device(onward, masks[1], size)
    total = keep[:, :q] + arrived[:, :q].astype(f32) + second.astype(f32)
    pieces = []
    for far in range(1, q // block_rows):
        part = total[:, far * block_rows:(far + 1) * block_rows].astype(bf16)
        pieces.append(to_device(part, 4 * far, size))
    return total[:, :block_rows], pieces


def gather(block, swapped, size):
    far = [block] + [to_device(block, 4 * z, size) for z in range(1, size // 4)]
    own = jnp.concatenate(far, axis=1)
    by_x = to_device(own, 1, size)
    by_y = to_device(own, 2, size)
    by_both = to_device(by_x, 2, size) if swapped else to_device(by_y, 1, size)
    return [own, by_y, by_x, by_both]


def body(series, modes, query_weight, mix_weight, out_weight):
    series_count, shard_rows, width = series.shape
    own_modes, heads_here, head_size, _ = mix_weight.shape
    mode_total = modes.shape[0]
    size = lax.axis_size("tm")
    series_length = size * shard_rows
    rows = 2 * mode_total
    half = series_count // 2
    count = half // 2
    core = lax.axis_index("head")
    place = jnp.stack([lax.axis_index("tm"), core]).astype(jnp.int32)

    send_a, keep_a, table = forward(
        True, series, place, modes[None, :], count, half, own_modes, series_length, rows
    )
    send_b, keep_b = forward(False, series, place, table, count, half, own_modes, series_length, rows)

    real, imag = mix_weight[..., :head_size], mix_weight[..., head_size:]
    mix_here = jnp.concatenate(
        [jnp.concatenate([real, imag], axis=-1), jnp.concatenate([-imag, real], axis=-1)], axis=2
    ).astype(bf16)
    mix_here = jnp.swapaxes(mix_here, 0, 1).reshape(heads_here, own_modes * 2 * head_size, 2 * head_size)
    mix_full = jnp.concatenate([mix_here, to_core(mix_here)], axis=0)
    query_full = jnp.concatenate([query_weight, to_core(query_weight)], axis=1)
    out_full = jnp.concatenate([out_weight, to_core(out_weight)], axis=1)
    out_full = jnp.where(core == 0, out_full, jnp.roll(out_full, width // 2, axis=0))
    table_back = table.T

    block_rows = 2 * own_modes
    scale = 1.0 / math.sqrt(series_length)
    back_scale = 1.0 / math.sqrt(mode_total)
    total_a = reduce_scatter(send_a, keep_a, (1, 2), size, block_rows)
    total_b = reduce_scatter(send_b, keep_b, (2, 1), size, block_rows)
    gathered = []
    for part, (own, arrived) in enumerate((total_a, total_b)):
        here, there = mix(own, arrived, query_full, mix_full, out_full, scale, own_modes)
        block = jnp.concatenate([here, to_core(there)], axis=0)
        gathered.append(gather(block, part == 1, size))
    output = inverse(place, table_back, gathered[0], None, series_count, half, 0, back_scale)
    return inverse(place, table_back, gathered[1], output, series_count, half, count, back_scale)


def solution(mesh):
    in_specs = (
        P(None, "tm", None),
        P(),
        P(None, "head"),
        P("tm", "head", None, None),
        P(None, "head"),
    )
    out_specs = P(None, "tm", "head")
    return jax.shard_map(body, mesh=mesh, in_specs=in_specs, out_specs=out_specs, check_vma=False)
```

time: 332 us -> 103 us (0.31)
  waiting for transfers between devices: 239 us -> 29.1 us
  matrix products: 40.7 us -> 0 us
  starting transfers between devices: 0.27 us -> 35 us
  local copies, waits for them, and re-layouts: 30.3 us -> 10.1 us
  Pallas kernels: 0 us -> 19.6 us
  between operations: 13.2 us -> 0.29 us
    psum x1 -> x0, waiting for transfers between devices: 171 us -> none  [body(): lax.psum(jnp.stack([real_part, -imag_part], axis=1) * forward_scale, 'tm')]
    all_gather x2 -> x0, waiting for transfers between devices: 67.7 us -> none  [the longest x1 59.7 us: body(): by_mode = lax.all_gather(mixed_spectra, 'tm', axis=0, tiled=True)]
    dot_general x7 -> x0, matrix products: 40.7 us -> none  [the longest x1 13.8 us: body(): jnp.dot(restored.reshape(series_count * shard_rows, model_width), out_wei...]
    ppermute x0 -> x27, starting transfers between devices: none -> 35 us  [the longest x22 33.9 us: to_device(): return lax.ppermute(value, 'tm', [(i, i ^ mask) for i in range(size)])]
    ppermute x0 -> x27, waiting for transfers between devices: none -> 29.1 us  [the longest x22 29.1 us: to_device(): return lax.ppermute(value, 'tm', [(i, i ^ mask) for i in range(size)])]
    convert_element_type x1 -> x0, local copies, waits for them, and re-layouts: 21.6 us -> none  [body(): restored = (summed * inverse_scale).astype(jnp.bfloat16)]
    pallas_call x0 -> x6, Pallas kernels: none -> 19.6 us  [the longest x2 10.6 us: inverse(): pl.pallas_call(functools.partial(inverse_kernel, scale, previous is not N...]
    unnamed x8 -> x14, local copies, waits for them, and re-layouts: 0.02 us -> 6.78 us
  transfers between devices with their start and end apart: 3 -> 27, of which waited for: 3 -> 11; matrix products, arithmetic and copies ran while one was open for 1% -> 12% of each run, Pallas kernels for 0% -> 14%
where the time goes in v1:
time: 103 us; the launch traced here: 102 us
  starting transfers between devices  35 us (34%)
  waiting for transfers between devices  29.1 us (28%)
  Pallas kernels  19.6 us (19%)
  local copies, waits for them, and re-layouts  10.1 us (10%)
  other arithmetic  8.17 us (8%)
    ppermute x22, starting transfers between devices, to_device(): return lax.ppermute(value, 'tm', [(i, i ^ mask) for i in range(size)])  33.9 us
    ppermute x22, waiting for transfers between devices, to_device(): return lax.ppermute(value, 'tm', [(i, i ^ mask) for i in range(size)])  29.1 us
    pallas_call x2, Pallas kernels, inverse(): pl.pallas_call(functools.partial(inverse_kernel, scale, previous is not N...  10.6 us
    pallas_call x2, Pallas kernels, forward(): pl.pallas_call(functools.partial(forward_kernel, first, own_modes, series...  7.08 us
    unnamed x14, local copies, waits for them, and re-layouts  6.78 us
    another operation x4, other arithmetic  3.78 us
    convert_element_type x2, other arithmetic, reduce_scatter(): onward = (keep[:, q:] + arrived[:, q:].astype(f32)).astype(bf16)  2.07 us
  transfers between devices with their start and end apart: 27, of which 11 were waited for; matrix products, arithmetic and copies ran while one was open for 12% of the time, Pallas kernels for 14%

profile of v1, /device:TPU:0, one launch (start us, length us, event | category | flops | bytes accessed | tf_op | source)
XLA Modules:
  0.0 102.3 jit_solution(13043992694466884922)
XLA Ops:
  4.1 5.8 %copy-done = bf16[16,1024,512]{2,1,0:T(8,128)(2,1)S(1)} copy-done((bf16[16,1024,512]{2,1,0:T(8,128)(2,1)S(1)}, bf16[16,1024,512]{2,1,0:T(8,128)(2,1)}, u32[]{:S(2)}) %copy-start) | copy-done | bytes 16777240
  9.9 4.7 %forward_first.1 = (bf16[4,128,512]{2,1,0:T(8,128)(2,1)}, f32[4,128,512]{2,1,0:T(8,128)S(1)}, bf16[256,1024]{1,0:T(8,128)(2,1)S(1)}) custom-call(s32[2]{0:T(128)S(1)} %pad_add_fusion.place_ref, s32[1,128]{1,0:T(1,128)S(1)} %bitcast.10, bf16[16,1024,512]{2,1,0:T(8,128)(2,1)S(1)} %copy-done), custom_call_target="tpu_custom_call" | custom-call | flops 1073741824 | bytes 5767168 | tf_op jit(solution)/shard_map/forward_first/pallas_call | solution.py:88
  14.6 2.5 %collective-permute-start.15 = (bf16[4,128,512]{2,1,0:T(8,128)(2,1)}, bf16[4,128,512]{2,1,0:T(8,128)(2,1)}, u32[]{:S(2)}, u32[]{:S(2)}) collective-permute-start(bf16[4,128,512]{2,1,0:T(8,128)(2,1)} %get-tuple-element.20), channel_id=1, source_target_pairs={{0,2},{2,0},{4,6},{6,4},{8,10},{10,8},{12,14},{14,12},{16,18},{18,... | collective-permute-start | bytes 1572872 | tf_op jit(solution)/shard_map/ppermute | solution.py:220
  17.2 2.3 %forward_second.1 = (bf16[4,128,512]{2,1,0:T(8,128)(2,1)S(1)}, f32[4,128,512]{2,1,0:T(8,128)S(1)}) custom-call(s32[2]{0:T(128)S(1)} %pad_add_fusion.place_ref, bf16[256,1024]{1,0:T(8,128)(2,1)S(1)} %get-tuple-element.14.refs_0_, bf16[16,1024,512]{2,1,0:T(8,128)(2,1)S(1)} %copy-done.1), custom_call_target="tpu_custom_call" | custom-call | flops 1073741824 | bytes 5767168 | tf_op jit(solution)/shard_map/forward_second/pallas_call | solution.py:88
  19.5 1.6 %collective-permute-start = (bf16[4,128,512]{2,1,0:T(8,128)(2,1)S(1)}, bf16[4,128,512]{2,1,0:T(8,128)(2,1)}, u32[]{:S(2)}, u32[]{:S(2)}) collective-permute-start(bf16[4,128,512]{2,1,0:T(8,128)(2,1)S(1)} %get-tuple-element.16), channel_id=1, source_target_pairs={{0,4},{2,6},{4,0},{6,2},{8,12},{10,14},{12,8},{14,10},{16,20},{18,... | collective-permute-start | bytes 1572872 | tf_op jit(solution)/shard_map/ppermute | solution.py:220
  23.3 6.7 %collective-permute-done.15 = bf16[4,128,512]{2,1,0:T(8,128)(2,1)} collective-permute-done((bf16[4,128,512]{2,1,0:T(8,128)(2,1)}, bf16[4,128,512]{2,1,0:T(8,128)(2,1)}, u32[]{:S(2)}, u32[]{:S(2)}) %collective-permute-start.15) | collective-permute-done | bytes 524320 | tf_op jit(solution)/shard_map/ppermute | solution.py:220
  31.1 1.8 %collective-permute-start.16 = (bf16[4,64,512]{2,1,0:T(8,128)(2,1)S(1)}, bf16[4,64,512]{2,1,0:T(8,128)(2,1)S(1)}, u32[]{:S(2)}, u32[]{:S(2)}) collective-permute-start(bf16[4,64,512]{2,1,0:T(8,128)(2,1)S(1)} %add_convert_fusion), channel_id=1, source_target_pairs={{0,4},{2,6},{4,0},{6,2},{8,12},{10,14},{12,8},{14,10},{16,20},{18,... | collective-permute-start | bytes 786440 | tf_op jit(solution)/shard_map/ppermute | solution.py:220
  34.9 1.6 %collective-permute-start.1 = (bf16[4,64,512]{2,1,0:T(8,128)(2,1)S(1)}, bf16[4,64,512]{2,1,0:T(8,128)(2,1)S(1)}, u32[]{:S(2)}, u32[]{:S(2)}) collective-permute-start(bf16[4,64,512]{2,1,0:T(8,128)(2,1)S(1)} %add_convert_fusion.1), channel_id=1, source_target_pairs={{0,2},{2,0},{4,6},{6,4},{8,10},{10,8},{12,14},{14,12},{16,18},{18,... | collective-permute-start | bytes 786440 | tf_op jit(solution)/shard_map/ppermute | solution.py:220
  36.5 2.7 %collective-permute-done.16 = bf16[4,64,512]{2,1,0:T(8,128)(2,1)S(1)} collective-permute-done((bf16[4,64,512]{2,1,0:T(8,128)(2,1)S(1)}, bf16[4,64,512]{2,1,0:T(8,128)(2,1)S(1)}, u32[]{:S(2)}, u32[]{:S(2)}) %collective-permute-start.16) | collective-permute-done | bytes 262176 | tf_op jit(solution)/shard_map/ppermute | solution.py:220
  40.3 3.7 %collective-permute-start.19 = (bf16[4,16,512]{2,1,0:T(8,128)(2,1)S(1)}, bf16[4,16,512]{2,1,0:T(8,128)(2,1)S(1)}, u32[]{:S(2)}, u32[]{:S(2)}) collective-permute-start(bf16[4,16,512]{2,1,0:T(8,128)(2,1)S(1)} %get-tuple-element.29), channel_id=1, source_target_pairs={{0,24},{2,26},{4,28},{6,30},{8,16},{10,18},{12,20},{14,22},{16,8},... | collective-permute-start | bytes 196616 | tf_op jit(solution)/shard_map/ppermute | solution.py:220
  45.9 3.7 %collective-permute-start.4 = (bf16[4,16,512]{2,1,0:T(8,128)(2,1)S(1)}, bf16[4,16,512]{2,1,0:T(8,128)(2,1)S(1)}, u32[]{:S(2)}, u32[]{:S(2)}) collective-permute-start(bf16[4,16,512]{2,1,0:T(8,128)(2,1)S(1)} %get-tuple-element.32), channel_id=1, source_target_pairs={{0,24},{2,26},{4,28},{6,30},{8,16},{10,18},{12,20},{14,22},{16,8},... | collective-permute-start | bytes 196616 | tf_op jit(solution)/shard_map/ppermute | solution.py:220
  49.7 1.7 %pad_maximum_fusion.refs_4_ = bf16[8,1024,128]{2,1,0:T(8,128)(2,1)S(1)} fusion(bf16[4,1024,128]{2,1,0:T(8,128)(2,1)} %collective-permute-done.6, bf16[4,1024,128]{2,1,0:T(8,128)(2,1)} %bitcast.5), kind=kLoop, calls=%fused_computation | loop fusion | flops 1048576 | bytes 4194304 | tf_op jit(solution)/shard_map/concatenate | solution.py:271
  56.9 2.4 %collective-permute-start.23 = (bf16[8,16,256]{2,1,0:T(8,128)(2,1)S(1)}, bf16[8,16,256]{2,1,0:T(8,128)(2,1)S(1)}, u32[]{:S(2)}, u32[]{:S(2)}) collective-permute-start(bf16[8,16,256]{2,1,0:T(8,128)(2,1)S(1)} %constant_dynamic-update-slice_fusion.6), channel_id=1, source_target_pairs={{0,24},{2,26},{4,28},{6,30},{8,16},{10,18},{12,20},{14,22},{16,8},... | collective-permute-start | bytes 196616 | tf_op jit(solution)/shard_map/ppermute | solution.py:220
  61.3 2.4 %collective-permute-start.11 = (bf16[8,16,256]{2,1,0:T(8,128)(2,1)S(1)}, bf16[8,16,256]{2,1,0:T(8,128)(2,1)S(1)}, u32[]{:S(2)}, u32[]{:S(2)}) collective-permute-start(bf16[8,16,256]{2,1,0:T(8,128)(2,1)S(1)} %constant_dynamic-update-slice_fusion.4), channel_id=1, source_target_pairs={{0,24},{2,26},{4,28},{6,30},{8,16},{10,18},{12,20},{14,22},{16,8},... | collective-permute-start | bytes 196616 | tf_op jit(solution)/shard_map/ppermute | solution.py:220
  63.7 2.4 %collective-permute-start.9 = (bf16[8,16,256]{2,1,0:T(8,128)(2,1)S(1)}, bf16[8,16,256]{2,1,0:T(8,128)(2,1)S(1)}, u32[]{:S(2)}, u32[]{:S(2)}) collective-permute-start(bf16[8,16,256]{2,1,0:T(8,128)(2,1)S(1)} %constant_dynamic-update-slice_fusion.4), channel_id=1, source_target_pairs={{0,8},{2,10},{4,12},{6,14},{8,0},{10,2},{12,4},{14,6},{16,24},{18,... | collective-permute-start | bytes 196616 | tf_op jit(solution)/shard_map/ppermute | solution.py:220
  66.1 3.7 %collective-permute-done.22 = bf16[8,16,256]{2,1,0:T(8,128)(2,1)S(1)} collective-permute-done((bf16[8,16,256]{2,1,0:T(8,128)(2,1)S(1)}, bf16[8,16,256]{2,1,0:T(8,128)(2,1)S(1)}, u32[]{:S(2)}, u32[]{:S(2)}) %collective-permute-start.22) | collective-permute-done | bytes 65568 | tf_op jit(solution)/shard_map/ppermute | solution.py:220
  69.8 1.6 %collective-permute-start.24 = (bf16[8,64,256]{2,1,0:T(8,128)(2,1)S(1)}, bf16[8,64,256]{2,1,0:T(8,128)(2,1)S(1)}, u32[]{:S(2)}, u32[]{:S(2)}) collective-permute-start(bf16[8,64,256]{2,1,0:T(8,128)(2,1)S(1)} %pad_maximum_fusion.2.refs_0_), channel_id=1, source_target_pairs={{0,4},{2,6},{4,0},{6,2},{8,12},{10,14},{12,8},{14,10},{16,20},{18,... | collective-permute-start | bytes 786440 | tf_op jit(solution)/shard_map/ppermute | solution.py:220
  72.4 1.6 %collective-permute-start.13 = (bf16[8,64,256]{2,1,0:T(8,128)(2,1)S(1)}, bf16[8,64,256]{2,1,0:T(8,128)(2,1)S(1)}, u32[]{:S(2)}, u32[]{:S(2)}) collective-permute-start(bf16[8,64,256]{2,1,0:T(8,128)(2,1)S(1)} %pad_maximum_fusion.1.refs_0_), channel_id=1, source_target_pairs={{0,2},{2,0},{4,6},{6,4},{8,10},{10,8},{12,14},{14,12},{16,18},{18,... | collective-permute-start | bytes 786440 | tf_op jit(solution)/shard_map/ppermute | solution.py:220
  74.5 3.2 %collective-permute-done.24.refs_1_ = bf16[8,64,256]{2,1,0:T(8,128)(2,1)S(1)} collective-permute-done((bf16[8,64,256]{2,1,0:T(8,128)(2,1)S(1)}, bf16[8,64,256]{2,1,0:T(8,128)(2,1)S(1)}, u32[]{:S(2)}, u32[]{:S(2)}) %collective-permute-start.24) | collective-permute-done | bytes 262176 | tf_op jit(solution)/shard_map/ppermute | solution.py:220
  79.1 1.5 %collective-permute-start.12 = (bf16[8,64,256]{2,1,0:T(8,128)(2,1)S(1)}, bf16[8,64,256]{2,1,0:T(8,128)(2,1)S(1)}, u32[]{:S(2)}, u32[]{:S(2)}) collective-permute-start(bf16[8,64,256]{2,1,0:T(8,128)(2,1)S(1)} %pad_maximum_fusion.1.refs_0_), channel_id=1, source_target_pairs={{0,4},{2,6},{4,0},{6,2},{8,12},{10,14},{12,8},{14,10},{16,20},{18,... | collective-permute-start | bytes 786440 | tf_op jit(solution)/shard_map/ppermute | solution.py:220
  83.3 3.9 %collective-permute-done.25.refs_2_ = bf16[8,64,256]{2,1,0:T(8,128)(2,1)S(1)} collective-permute-done((bf16[8,64,256]{2,1,0:T(8,128)(2,1)S(1)}, bf16[8,64,256]{2,1,0:T(8,128)(2,1)S(1)}, u32[]{:S(2)}, u32[]{:S(2)}) %collective-permute-start.25) | collective-permute-done | bytes 262176 | tf_op jit(solution)/shard_map/ppermute | solution.py:220
  87.2 4.5 %collective-permute-done.26.refs_3_ = bf16[8,64,256]{2,1,0:T(8,128)(2,1)S(1)} collective-permute-done((bf16[8,64,256]{2,1,0:T(8,128)(2,1)S(1)}, bf16[8,64,256]{2,1,0:T(8,128)(2,1)S(1)}, u32[]{:S(2)}, u32[]{:S(2)}) %collective-permute-start.26) | collective-permute-done | bytes 262176 | tf_op jit(solution)/shard_map/ppermute | solution.py:220
  91.7 5.3 %inverse_first.1.refs_4_ = bf16[16,1024,256]{2,1,0:T(8,128)(2,1)} custom-call(s32[2]{0:T(128)S(1)} %pad_add_fusion.place_ref, bf16[1024,256]{1,0:T(8,128)(2,1)S(1)} %bitcast.8, bf16[8,64,256]{2,1,0:T(8,128)(2,1)S(1)} %pad_maximum_fusion.2.refs_0_, bf16[8,64,256]{2,1,0:T(8,128)(2,1)S(1)} %collective-permute-done.24.refs_1_, ...), custom_call_target="tpu_custom_call" | custom-call | flops 1073741824 | bytes 5242880 | tf_op jit(solution)/shard_map/inverse_first/pallas_call | solution.py:197
  97.0 5.3 %inverse_second.1 = bf16[16,1024,256]{2,1,0:T(8,128)(2,1)} custom-call(s32[2]{0:T(128)S(1)} %pad_add_fusion.place_ref, bf16[1024,256]{1,0:T(8,128)(2,1)S(1)} %bitcast.9, bf16[8,64,256]{2,1,0:T(8,128)(2,1)S(1)} %pad_maximum_fusion.1.refs_0_, bf16[8,64,256]{2,1,0:T(8,128)(2,1)S(1)} %collective-permute-done.12.refs_1_, ...), custom_call_target="tpu_custom_call", output_to_operand_aliasing={{}: (6, {})} | custom-call | flops 1073741824 | bytes 5242880 | tf_op jit(solution)/shard_map/inverse_second/pallas_call | solution.py:197
  (73 shorter events, 25.4 us)
Async XLA Ops:
  0.0 32.9 %collective-permute-start.5 = (bf16[512,256]{1,0:T(8,128)(2,1)}, bf16[512,256]{1,0:T(8,128)(2,1)}, u32[]{:S(2)}, u32[]{:S(2)}) collective-permute-start(bf16[512,256]{1,0:T(8,128)(2,1)} %param.7), channel_id=1, source_target_pairs={{0,1},{1,0},{2,3},{3,2},{4,5},{5,4},{6,7},{7,6},{8,9},{9,8},{10,11... | collective-permute-start | bytes 786440 | tf_op jit(solution)/shard_map/ppermute | solution.py:224
  0.5 21.7 %collective-permute-start.7 = (bf16[512,256]{1,0:T(8,128)(2,1)}, bf16[512,256]{1,0:T(8,128)(2,1)}, u32[]{:S(2)}, u32[]{:S(2)}) collective-permute-start(bf16[512,256]{1,0:T(8,128)(2,1)} %param.9), channel_id=1, source_target_pairs={{0,1},{1,0},{2,3},{3,2},{4,5},{5,4},{6,7},{7,6},{8,9},{9,8},{10,11... | collective-permute-start | bytes 786440 | tf_op jit(solution)/shard_map/ppermute | solution.py:224
  3.6 46.0 %collective-permute-start.6 = (bf16[4,1024,128]{2,1,0:T(8,128)(2,1)}, bf16[4,1024,128]{2,1,0:T(8,128)(2,1)}, u32[]{:S(2)}, u32[]{:S(2)}) collective-permute-start(bf16[4,1024,128]{2,1,0:T(8,128)(2,1)} %bitcast.5), channel_id=1, source_target_pairs={{0,1},{1,0},{2,3},{3,2},{4,5},{5,4},{6,7},{7,6},{8,9},{9,8},{10,11... | collective-permute-start | bytes 3145736 | tf_op jit(solution)/shard_map/ppermute | solution.py:224
  14.6 15.4 %collective-permute-start.15 = (bf16[4,128,512]{2,1,0:T(8,128)(2,1)}, bf16[4,128,512]{2,1,0:T(8,128)(2,1)}, u32[]{:S(2)}, u32[]{:S(2)}) collective-permute-start(bf16[4,128,512]{2,1,0:T(8,128)(2,1)} %get-tuple-element.20), channel_id=1, source_target_pairs={{0,2},{2,0},{4,6},{6,4},{8,10},{10,8},{12,14},{14,12},{16,18},{18,... | collective-permute-start | bytes 1572872 | tf_op jit(solution)/shard_map/ppermute | solution.py:220
  19.5 14.3 %collective-permute-start = (bf16[4,128,512]{2,1,0:T(8,128)(2,1)S(1)}, bf16[4,128,512]{2,1,0:T(8,128)(2,1)}, u32[]{:S(2)}, u32[]{:S(2)}) collective-permute-start(bf16[4,128,512]{2,1,0:T(8,128)(2,1)S(1)} %get-tuple-element.16), channel_id=1, source_target_pairs={{0,4},{2,6},{4,0},{6,2},{8,12},{10,14},{12,8},{14,10},{16,20},{18,... | collective-permute-start | bytes 1572872 | tf_op jit(solution)/shard_map/ppermute | solution.py:220
  31.1 8.2 %collective-permute-start.16 = (bf16[4,64,512]{2,1,0:T(8,128)(2,1)S(1)}, bf16[4,64,512]{2,1,0:T(8,128)(2,1)S(1)}, u32[]{:S(2)}, u32[]{:S(2)}) collective-permute-start(bf16[4,64,512]{2,1,0:T(8,128)(2,1)S(1)} %add_convert_fusion), channel_id=1, source_target_pairs={{0,4},{2,6},{4,0},{6,2},{8,12},{10,14},{12,8},{14,10},{16,20},{18,... | collective-permute-start | bytes 786440 | tf_op jit(solution)/shard_map/ppermute | solution.py:220
  34.9 9.9 %collective-permute-start.1 = (bf16[4,64,512]{2,1,0:T(8,128)(2,1)S(1)}, bf16[4,64,512]{2,1,0:T(8,128)(2,1)S(1)}, u32[]{:S(2)}, u32[]{:S(2)}) collective-permute-start(bf16[4,64,512]{2,1,0:T(8,128)(2,1)S(1)} %add_convert_fusion.1), channel_id=1, source_target_pairs={{0,2},{2,0},{4,6},{6,4},{8,10},{10,8},{12,14},{14,12},{16,18},{18,... | collective-permute-start | bytes 786440 | tf_op jit(solution)/shard_map/ppermute | solution.py:220
  40.3 11.1 %collective-permute-start.19 = (bf16[4,16,512]{2,1,0:T(8,128)(2,1)S(1)}, bf16[4,16,512]{2,1,0:T(8,128)(2,1)S(1)}, u32[]{:S(2)}, u32[]{:S(2)}) collective-permute-start(bf16[4,16,512]{2,1,0:T(8,128)(2,1)S(1)} %get-tuple-element.29), channel_id=1, source_target_pairs={{0,24},{2,26},{4,28},{6,30},{8,16},{10,18},{12,20},{14,22},{16,8},... | collective-permute-start | bytes 196616 | tf_op jit(solution)/shard_map/ppermute | solution.py:220
  44.0 8.3 %collective-permute-start.18 = (bf16[4,16,512]{2,1,0:T(8,128)(2,1)S(1)}, bf16[4,16,512]{2,1,0:T(8,128)(2,1)S(1)}, u32[]{:S(2)}, u32[]{:S(2)}) collective-permute-start(bf16[4,16,512]{2,1,0:T(8,128)(2,1)S(1)} %get-tuple-element.30), channel_id=1, source_target_pairs={{0,16},{2,18},{4,20},{6,22},{8,24},{10,26},{12,28},{14,30},{16,0},... | collective-permute-start | bytes 196616 | tf_op jit(solution)/shard_map/ppermute | solution.py:220
  44.0 8.3 %collective-permute-start.17 = (bf16[4,16,512]{2,1,0:T(8,128)(2,1)S(1)}, bf16[4,16,512]{2,1,0:T(8,128)(2,1)S(1)}, u32[]{:S(2)}, u32[]{:S(2)}) collective-permute-start(bf16[4,16,512]{2,1,0:T(8,128)(2,1)S(1)} %get-tuple-element.31), channel_id=1, source_target_pairs={{0,8},{2,10},{4,12},{6,14},{8,0},{10,2},{12,4},{14,6},{16,24},{18,... | collective-permute-start | bytes 196616 | tf_op jit(solution)/shard_map/ppermute | solution.py:220
  45.9 7.5 %collective-permute-start.4 = (bf16[4,16,512]{2,1,0:T(8,128)(2,1)S(1)}, bf16[4,16,512]{2,1,0:T(8,128)(2,1)S(1)}, u32[]{:S(2)}, u32[]{:S(2)}) collective-permute-start(bf16[4,16,512]{2,1,0:T(8,128)(2,1)S(1)} %get-tuple-element.32), channel_id=1, source_target_pairs={{0,24},{2,26},{4,28},{6,30},{8,16},{10,18},{12,20},{14,22},{16,8},... | collective-permute-start | bytes 196616 | tf_op jit(solution)/shard_map/ppermute | solution.py:220
  49.6 5.2 %collective-permute-start.3 = (bf16[4,16,512]{2,1,0:T(8,128)(2,1)S(1)}, bf16[4,16,512]{2,1,0:T(8,128)(2,1)S(1)}, u32[]{:S(2)}, u32[]{:S(2)}) collective-permute-start(bf16[4,16,512]{2,1,0:T(8,128)(2,1)S(1)} %get-tuple-element.33), channel_id=1, source_target_pairs={{0,16},{2,18},{4,20},{6,22},{8,24},{10,26},{12,28},{14,30},{16,0},... | collective-permute-start | bytes 196616 | tf_op jit(solution)/shard_map/ppermute | solution.py:220
  56.9 6.8 %collective-permute-start.23 = (bf16[8,16,256]{2,1,0:T(8,128)(2,1)S(1)}, bf16[8,16,256]{2,1,0:T(8,128)(2,1)S(1)}, u32[]{:S(2)}, u32[]{:S(2)}) collective-permute-start(bf16[8,16,256]{2,1,0:T(8,128)(2,1)S(1)} %constant_dynamic-update-slice_fusion.6), channel_id=1, source_target_pairs={{0,24},{2,26},{4,28},{6,30},{8,16},{10,18},{12,20},{14,22},{16,8},... | collective-permute-start | bytes 196616 | tf_op jit(solution)/shard_map/ppermute | solution.py:220
  59.3 10.5 %collective-permute-start.22 = (bf16[8,16,256]{2,1,0:T(8,128)(2,1)S(1)}, bf16[8,16,256]{2,1,0:T(8,128)(2,1)S(1)}, u32[]{:S(2)}, u32[]{:S(2)}) collective-permute-start(bf16[8,16,256]{2,1,0:T(8,128)(2,1)S(1)} %constant_dynamic-update-slice_fusion.6), channel_id=1, source_target_pairs={{0,16},{2,18},{4,20},{6,22},{8,24},{10,26},{12,28},{14,30},{16,0},... | collective-permute-start | bytes 196616 | tf_op jit(solution)/shard_map/ppermute | solution.py:220
  59.9 9.9 %collective-permute-start.21 = (bf16[8,16,256]{2,1,0:T(8,128)(2,1)S(1)}, bf16[8,16,256]{2,1,0:T(8,128)(2,1)S(1)}, u32[]{:S(2)}, u32[]{:S(2)}) collective-permute-start(bf16[8,16,256]{2,1,0:T(8,128)(2,1)S(1)} %constant_dynamic-update-slice_fusion.6), channel_id=1, source_target_pairs={{0,8},{2,10},{4,12},{6,14},{8,0},{10,2},{12,4},{14,6},{16,24},{18,... | collective-permute-start | bytes 196616 | tf_op jit(solution)/shard_map/ppermute | solution.py:220
  61.3 10.1 %collective-permute-start.11 = (bf16[8,16,256]{2,1,0:T(8,128)(2,1)S(1)}, bf16[8,16,256]{2,1,0:T(8,128)(2,1)S(1)}, u32[]{:S(2)}, u32[]{:S(2)}) collective-permute-start(bf16[8,16,256]{2,1,0:T(8,128)(2,1)S(1)} %constant_dynamic-update-slice_fusion.4), channel_id=1, source_target_pairs={{0,24},{2,26},{4,28},{6,30},{8,16},{10,18},{12,20},{14,22},{16,8},... | collective-permute-start | bytes 196616 | tf_op jit(solution)/shard_map/ppermute | solution.py:220
  63.7 8.7 %collective-permute-start.10 = (bf16[8,16,256]{2,1,0:T(8,128)(2,1)S(1)}, bf16[8,16,256]{2,1,0:T(8,128)(2,1)S(1)}, u32[]{:S(2)}, u32[]{:S(2)}) collective-permute-start(bf16[8,16,256]{2,1,0:T(8,128)(2,1)S(1)} %constant_dynamic-update-slice_fusion.4), channel_id=1, source_target_pairs={{0,16},{2,18},{4,20},{6,22},{8,24},{10,26},{12,28},{14,30},{16,0},... | collective-permute-start | bytes 196616 | tf_op jit(solution)/shard_map/ppermute | solution.py:220
  63.7 8.7 %collective-permute-start.9 = (bf16[8,16,256]{2,1,0:T(8,128)(2,1)S(1)}, bf16[8,16,256]{2,1,0:T(8,128)(2,1)S(1)}, u32[]{:S(2)}, u32[]{:S(2)}) collective-permute-start(bf16[8,16,256]{2,1,0:T(8,128)(2,1)S(1)} %constant_dynamic-update-slice_fusion.4), channel_id=1, source_target_pairs={{0,8},{2,10},{4,12},{6,14},{8,0},{10,2},{12,4},{14,6},{16,24},{18,... | collective-permute-start | bytes 196616 | tf_op jit(solution)/shard_map/ppermute | solution.py:220
  69.8 7.8 %collective-permute-start.24 = (bf16[8,64,256]{2,1,0:T(8,128)(2,1)S(1)}, bf16[8,64,256]{2,1,0:T(8,128)(2,1)S(1)}, u32[]{:S(2)}, u32[]{:S(2)}) collective-permute-start(bf16[8,64,256]{2,1,0:T(8,128)(2,1)S(1)} %pad_maximum_fusion.2.refs_0_), channel_id=1, source_target_pairs={{0,4},{2,6},{4,0},{6,2},{8,12},{10,14},{12,8},{14,10},{16,20},{18,... | collective-permute-start | bytes 786440 | tf_op jit(solution)/shard_map/ppermute | solution.py:220
  72.4 9.3 %collective-permute-start.13 = (bf16[8,64,256]{2,1,0:T(8,128)(2,1)S(1)}, bf16[8,64,256]{2,1,0:T(8,128)(2,1)S(1)}, u32[]{:S(2)}, u32[]{:S(2)}) collective-permute-start(bf16[8,64,256]{2,1,0:T(8,128)(2,1)S(1)} %pad_maximum_fusion.1.refs_0_), channel_id=1, source_target_pairs={{0,2},{2,0},{4,6},{6,4},{8,10},{10,8},{12,14},{14,12},{16,18},{18,... | collective-permute-start | bytes 786440 | tf_op jit(solution)/shard_map/ppermute | solution.py:220
  73.9 13.3 %collective-permute-start.25 = (bf16[8,64,256]{2,1,0:T(8,128)(2,1)S(1)}, bf16[8,64,256]{2,1,0:T(8,128)(2,1)S(1)}, u32[]{:S(2)}, u32[]{:S(2)}) collective-permute-start(bf16[8,64,256]{2,1,0:T(8,128)(2,1)S(1)} %pad_maximum_fusion.2.refs_0_), channel_id=1, source_target_pairs={{0,2},{2,0},{4,6},{6,4},{8,10},{10,8},{12,14},{14,12},{16,18},{18,... | collective-permute-start | bytes 786440 | tf_op jit(solution)/shard_map/ppermute | solution.py:220
  77.6 14.1 %collective-permute-start.26 = (bf16[8,64,256]{2,1,0:T(8,128)(2,1)S(1)}, bf16[8,64,256]{2,1,0:T(8,128)(2,1)S(1)}, u32[]{:S(2)}, u32[]{:S(2)}) collective-permute-start(bf16[8,64,256]{2,1,0:T(8,128)(2,1)S(1)} %collective-permute-done.24.refs_1_), channel_id=1, source_target_pairs={{0,2},{2,0},{4,6},{6,4},{8,10},{10,8},{12,14},{14,12},{16,18},{18,... | collective-permute-start | bytes 786440 | tf_op jit(solution)/shard_map/ppermute | solution.py:220
  79.1 17.9 %collective-permute-start.12 = (bf16[8,64,256]{2,1,0:T(8,128)(2,1)S(1)}, bf16[8,64,256]{2,1,0:T(8,128)(2,1)S(1)}, u32[]{:S(2)}, u32[]{:S(2)}) collective-permute-start(bf16[8,64,256]{2,1,0:T(8,128)(2,1)S(1)} %pad_maximum_fusion.1.refs_0_), channel_id=1, source_target_pairs={{0,4},{2,6},{4,0},{6,2},{8,12},{10,14},{12,8},{14,10},{16,20},{18,... | collective-permute-start | bytes 786440 | tf_op jit(solution)/shard_map/ppermute | solution.py:220
  81.6 15.4 %collective-permute-start.14 = (bf16[8,64,256]{2,1,0:T(8,128)(2,1)S(1)}, bf16[8,64,256]{2,1,0:T(8,128)(2,1)S(1)}, u32[]{:S(2)}, u32[]{:S(2)}) collective-permute-start(bf16[8,64,256]{2,1,0:T(8,128)(2,1)S(1)} %collective-permute-done.13.refs_2_), channel_id=1, source_target_pairs={{0,4},{2,6},{4,0},{6,2},{8,12},{10,14},{12,8},{14,10},{16,20},{18,... | collective-permute-start | bytes 786440 | tf_op jit(solution)/shard_map/ppermute | solution.py:220
  (8 other events, 34.2 us)

commit v2 on v1

--- a/solution.py
+++ b/solution.py
@@ -13,7 +13,7 @@
 two_pi = 2.0 * math.pi
 
 
-def row_modes(place, modes_row, rows, own_modes, series_length):
+def row_modes(place, core, modes_row, rows, own_modes, series_length):
     lanes = modes_row.shape[1]
     row = lax.broadcasted_iota(jnp.int32, (rows, lanes), 0)
     lane = lax.broadcasted_iota(jnp.int32, (rows, lanes), 1)
@@ -22,7 +22,7 @@
     block = row // block_rows
     inside = row - block * block_rows
     quarter = block // far
-    relative = (quarter // 2) + 2 * (quarter % 2) + 4 * (block % far)
+    relative = (quarter // 2) * (1 + core) + (quarter % 2) * (2 - core) + 4 * (block % far)
     imaginary = inside // own_modes
     wanted = (place ^ relative) * own_modes + inside - imaginary * own_modes
     picked = jnp.where(lane == wanted, modes_row.astype(f32), 0.0)
@@ -38,58 +38,60 @@
     cosine = 1.0 + square * (-0.5 + square * (1 / 24 + square * (-1 / 720 + square * (1 / 40320))))
     sine = angle * (1.0 + square * (-1 / 6 + square * (1 / 120 + square * (-1 / 5040))))
     which = quarters.astype(jnp.int32)
-    size = jnp.where(which & 1 == 0, cosine, sine)
-    return jnp.where((which == 1) | (which == 2), -size, size)
-
-
-def forward_kernel(first, own_modes, series_length, place_ref, *refs):
+    odd = which & 1 == 1
+    cos_size = jnp.where(odd, sine, cosine)
+    sin_size = jnp.where(odd, cosine, sine)
+    cos_flip = (which == 1) | (which == 2)
+    sin_flip = (which == 2) | (which == 3)
+    return jnp.where(cos_flip, -cos_size, cos_size), jnp.where(sin_flip, -sin_size, sin_size)
+
+
+def fill_table(place_ref, modes_ref, table_ref, own_modes, series_length):
+    rows, time_count = table_ref.shape
+    place = place_ref[0]
+    mode, shift = row_modes(place, place_ref[1], modes_ref[...], rows, own_modes, series_length)
+    lane = lax.broadcasted_iota(jnp.int32, (rows, 128), 1)
+    last = series_length - 1
+    cos_a, sin_a = wave((mode * (place * time_count + lane * 128) + shift) & last, series_length)
+    cos_b, sin_b = wave((mode * lane) & last, series_length)
+    for piece in range(time_count // 128):
+        value = cos_a[:, piece:piece + 1] * cos_b - sin_a[:, piece:piece + 1] * sin_b
+        table_ref[:, piece * 128:piece * 128 + 128] = value.astype(bf16)
+
+
+def forward_kernel(first, count, half, own_modes, series_length, place_ref, extra_ref, series_ref, *refs):
     if first:
-        modes_ref, series_ref, send_ref, keep_ref, table_ref = refs
-        rows, time_count = table_ref.shape
-
-        @pl.when(pl.program_id(0) == 0)
-        def _():
-            place = place_ref[0]
-            mode, shift = row_modes(place, modes_ref[...], rows, own_modes, series_length)
-            step = 16
-            for start in range(0, rows, step):
-                time_index = place * time_count + lax.broadcasted_iota(jnp.int32, (step, time_count), 1)
-                phases = time_index * mode[start:start + step] + shift[start:start + step]
-                phases = phases & (series_length - 1)
-                table_ref[start:start + step, :] = wave(phases, series_length).astype(bf16)
+        send_ref, keep_ref, table_ref, held, sems = refs
     else:
-        table_ref, series_ref, send_ref, keep_ref = refs
-    part = jnp.dot(table_ref[...], series_ref[0], preferred_element_type=f32)
-    q = part.shape[0] // 4
+        send_ref, keep_ref, held, sems = refs
+        table_ref = extra_ref
+    base = place_ref[1] * half + (0 if first else count)
+    copies = [pltpu.make_async_copy(series_ref.at[base + b], held.at[b], sems.at[b]) for b in range(count)]
+    for copy in copies:
+        copy.start()
     if first:
-        send_ref[0] = part[2 * q:].astype(bf16)
-        keep_ref[0] = part[:2 * q]
-    else:
-        send_ref[0, :q] = part[q:2 * q].astype(bf16)
-        send_ref[0, q:] = part[3 * q:].astype(bf16)
-        keep_ref[0, :q] = part[:q]
-        keep_ref[0, q:] = part[2 * q:3 * q]
+        fill_table(place_ref, extra_ref, table_ref, own_modes, series_length)
+    middle = table_ref.shape[0] // 2
+    for b in range(count):
+        copies[b].wait()
+        part = jnp.dot(table_ref[...], held[b], preferred_element_type=f32)
+        send_ref[b] = part[middle:].astype(bf16)
+        keep_ref[b] = part[:middle]
 
 
 def forward(first, series, place, extra, count, half, own_modes, series_length, rows):
     _, time_count, width = series.shape
-    offset = 0 if first else count
-    series_spec = pl.BlockSpec((1, time_count, width), lambda b, p: (p[1] * half + offset + b, 0, 0))
-    table_spec = pl.BlockSpec((rows, time_count), lambda b, p: (0, 0))
-    part_spec = pl.BlockSpec((1, rows // 2, width), lambda b, p: (b, 0, 0))
+    whole = pl.BlockSpec(memory_space=pltpu.VMEM)
     outs = [jax.ShapeDtypeStruct((count, rows // 2, width), bf16), jax.ShapeDtypeStruct((count, rows // 2, width), f32)]
-    out_specs = [part_spec, part_spec]
     if first:
-        in_specs = [pl.BlockSpec(extra.shape, lambda b, p: (0, 0)), series_spec]
         outs.append(jax.ShapeDtypeStruct((rows, time_count), bf16))
-        out_specs.append(table_spec)
-    else:
-        in_specs = [table_spec, series_spec]
     return pl.pallas_call(
-        functools.partial(forward_kernel, first, own_modes, series_length),
+        functools.partial(forward_kernel, first, count, half, own_modes, series_length),
         out_shape=outs,
-        grid_spec=pltpu.PrefetchScalarGridSpec(num_scalar_prefetch=1, grid=(count,), in_specs=in_specs, out_specs=out_specs),
-        compiler_params=pltpu.CompilerParams(vmem_limit_bytes=24 * 2**20),
+        in_specs=[pl.BlockSpec(memory_space=pltpu.SMEM), whole, pl.BlockSpec(memory_space=pltpu.HBM)],
+        out_specs=[whole] * len(outs),
+        scratch_shapes=[pltpu.VMEM((count, time_count, width), bf16), pltpu.SemaphoreType.DMA((count,))],
+        compiler_params=pltpu.CompilerParams(vmem_limit_bytes=50 * 2**20),
         cost_estimate=pl.CostEstimate(
             flops=2 * count * rows * time_count * width,
             bytes_accessed=count * (time_count * width * 2 + rows * width * 3),
@@ -175,75 +177,82 @@
     return result[:, :, :here], result[:, :, here:]
 
 
-def inverse_kernel(scale, aliased, place_ref, table_ref, *refs):
-    pieces, out_ref = refs[:4], refs[-1]
-    spectra = jnp.concatenate([piece[0] for piece in pieces], axis=0)
-    result = jnp.dot(table_ref[...], spectra, preferred_element_type=f32) * scale
-    out_ref[0] = result.astype(bf16)
+def inverse_kernel(scale, half, offset, place_ref, table_ref, *refs):
+    pieces, (out_ref, held, sems) = refs[:4], refs[-3:]
+    count = held.shape[0]
+    own = count // 2
+    copies = []
+    for b in range(count):
+        spectra = jnp.concatenate([piece[b] for piece in pieces], axis=0)
+        result = jnp.dot(table_ref[...], spectra, preferred_element_type=f32) * scale
+        held[b] = result.astype(bf16)
+        index = (place_ref[1] ^ (b // own)) * half + offset + b % own
+        copies.append(pltpu.make_async_copy(held.at[b], out_ref.at[index], sems.at[b]))
+        copies[-1].start()
+    for copy in copies:
+        copy.wait()
 
 
 def inverse(place, table, pieces, previous, series_count, half, offset, scale):
     time_count, rows = table.shape
-    count, quarter, width = pieces[0].shape
-    own = count // 2
-    piece_spec = pl.BlockSpec((1, quarter, width), lambda b, p: (b, 0, 0))
-    in_specs = [pl.BlockSpec((time_count, rows), lambda b, p: (0, 0))] + [piece_spec] * 4
+    count, _, width = pieces[0].shape
+    whole = pl.BlockSpec(memory_space=pltpu.VMEM)
+    in_specs = [pl.BlockSpec(memory_space=pltpu.SMEM)] + [whole] * 5
     args = [place, table, *pieces]
     aliases = {}
     if previous is not None:
-        in_specs.append(pl.BlockSpec(memory_space=pl.ANY))
+        in_specs.append(pl.BlockSpec(memory_space=pltpu.HBM))
         aliases = {len(args): 0}
         args.append(previous)
     return pl.pallas_call(
-        functools.partial(inverse_kernel, scale, previous is not None),
+        functools.partial(inverse_kernel, scale, half, offset),
         out_shape=jax.ShapeDtypeStruct((series_count, time_count, width), bf16),
-        grid_spec=pltpu.PrefetchScalarGridSpec(
-            num_scalar_prefetch=1,
-            grid=(count,),
-            in_specs=in_specs,
-            out_specs=pl.BlockSpec(
-                (1, time_count, width), lambda b, p: ((p[1] ^ (b // own)) * half + offset + b % own, 0, 0)
-            ),
-        ),
+        in_specs=in_specs,
+        out_specs=pl.BlockSpec(memory_space=pltpu.HBM),
+        scratch_shapes=[pltpu.VMEM((count, time_count, width), bf16), pltpu.SemaphoreType.DMA((count,))],
         input_output_aliases=aliases,
-        compiler_params=pltpu.CompilerParams(vmem_limit_bytes=24 * 2**20),
+        compiler_params=pltpu.CompilerParams(vmem_limit_bytes=32 * 2**20),
         cost_estimate=pl.CostEstimate(
             flops=2 * count * time_count * rows * width,
             bytes_accessed=count * (time_count * width * 2 + rows * width * 2),
             transcendentals=0,
         ),
-        name="inverse_second" if previous is not None else "inverse_first",
+        name="inverse_first" if previous is None else "inverse_second",
     )(*args)
 
 
-def to_device(value, mask, size):
-    return lax.ppermute(value, "tm", [(i, i ^ mask) for i in range(size)])
+def to_devices(value, masks, size):
+    pairs = [(2 * i + c, 2 * (i ^ masks[c]) + c) for i in range(size) for c in range(2)]
+    return lax.ppermute(value, ("tm", "head"), pairs)
+
+
+going_first, going_second = (1, 2), (2, 1)
 
 
 def to_core(value):
     return lax.ppermute(value, "head", [(0, 1), (1, 0)])
 
 
-def reduce_scatter(send, keep, masks, size, block_rows):
+def reduce_scatter(send, keep, size, block_rows):
     q = keep.shape[1] // 2
-    arrived = to_device(send, masks[0], size)
+    arrived = to_devices(send, going_first, size)
     onward = (keep[:, q:] + arrived[:, q:].astype(f32)).astype(bf16)
-    second = to_device(onward, masks[1], size)
+    second = to_devices(onward, going_second, size)
     total = keep[:, :q] + arrived[:, :q].astype(f32) + second.astype(f32)
     pieces = []
     for far in range(1, q // block_rows):
         part = total[:, far * block_rows:(far + 1) * block_rows].astype(bf16)
-        pieces.append(to_device(part, 4 * far, size))
+        pieces.append(to_devices(part, (4 * far, 4 * far), size))
     return total[:, :block_rows], pieces
 
 
-def gather(block, swapped, size):
-    far = [block] + [to_device(block, 4 * z, size) for z in range(1, size // 4)]
+def gather(block, size):
+    far = [block] + [to_devices(block, (4 * z, 4 * z), size) for z in range(1, size // 4)]
     own = jnp.concatenate(far, axis=1)
-    by_x = to_device(own, 1, size)
-    by_y = to_device(own, 2, size)
-    by_both = to_device(by_x, 2, size) if swapped else to_device(by_y, 1, size)
-    return [own, by_y, by_x, by_both]
+    by_second = to_devices(own, going_second, size)
+    by_first = to_devices(own, going_first, size)
+    by_both = to_devices(by_second, going_first, size)
+    return [own, by_second, by_first, by_both]
 
 
 def body(series, modes, query_weight, mix_weight, out_weight):
@@ -262,6 +271,7 @@
         True, series, place, modes[None, :], count, half, own_modes, series_length, rows
     )
     send_b, keep_b = forward(False, series, place, table, count, half, own_modes, series_length, rows)
+    table, query_weight, mix_weight, out_weight = lax.optimization_barrier((table, query_weight, mix_weight, out_weight))
 
     real, imag = mix_weight[..., :head_size], mix_weight[..., head_size:]
     mix_here = jnp.concatenate(
@@ -277,13 +287,13 @@
     block_rows = 2 * own_modes
     scale = 1.0 / math.sqrt(series_length)
     back_scale = 1.0 / math.sqrt(mode_total)
-    total_a = reduce_scatter(send_a, keep_a, (1, 2), size, block_rows)
-    total_b = reduce_scatter(send_b, keep_b, (2, 1), size, block_rows)
+    total_a = reduce_scatter(send_a, keep_a, size, block_rows)
+    total_b = reduce_scatter(send_b, keep_b, size, block_rows)
     gathered = []
-    for part, (own, arrived) in enumerate((total_a, total_b)):
+    for own, arrived in (total_a, total_b):
         here, there = mix(own, arrived, query_full, mix_full, out_full, scale, own_modes)
         block = jnp.concatenate([here, to_core(there)], axis=0)
-        gathered.append(gather(block, part == 1, size))
+        gathered.append(gather(block, size))
     output = inverse(place, table_back, gathered[0], None, series_count, half, 0, back_scale)
     return inverse(place, table_back, gathered[1], output, series_count, half, count, back_scale)
 

time: 103 us -> 82.7 us (0.80)
  waiting for transfers between devices: 29.1 us -> 22.9 us
  local copies, waits for them, and re-layouts: 10.1 us -> 4.93 us
  starting transfers between devices: 35 us -> 31.2 us
  Pallas kernels: 19.6 us -> 16 us
  other arithmetic: 8.17 us -> 6.89 us
    ppermute x22, waiting for transfers between devices: 29.1 us -> 22.9 us  [to_devices(): return lax.ppermute(value, ('tm', 'head'), pairs)]
    unnamed x14 -> x10, local copies, waits for them, and re-layouts: 6.78 us -> 1.66 us
    pallas_call x4, Pallas kernels: 17.7 us -> 14 us  [the longest x2 7.92 us: forward(): pl.pallas_call(functools.partial(forward_kernel, first, count, half, own_...]
    ppermute x22, starting transfers between devices: 33.9 us -> 30.5 us  [to_devices(): return lax.ppermute(value, ('tm', 'head'), pairs)]
    another operation x4, other arithmetic: 3.78 us -> 2.55 us
  transfers between devices with their start and end apart: 27 -> 27, of which waited for: 11 -> 9; matrix products, arithmetic and copies ran while one was open for 12% -> 13% of each run, Pallas kernels for 14% -> 11%
where the time goes in v2:
time: 82.7 us; the launch traced here: 82.2 us
  starting transfers between devices  31.2 us (38%)
  waiting for transfers between devices  22.9 us (28%)
  Pallas kernels  16 us (19%)
  other arithmetic  6.89 us (8%)
  local copies, waits for them, and re-layouts  4.93 us (6%)
    ppermute x22, starting transfers between devices, to_devices(): return lax.ppermute(value, ('tm', 'head'), pairs)  30.5 us
    ppermute x22, waiting for transfers between devices, to_devices(): return lax.ppermute(value, ('tm', 'head'), pairs)  22.9 us
    pallas_call x2, Pallas kernels, forward(): pl.pallas_call(functools.partial(forward_kernel, first, count, half, own_...  7.92 us
    pallas_call x2, Pallas kernels, inverse(): pl.pallas_call(functools.partial(inverse_kernel, scale, half, offset), ou...  6.09 us
    another operation x4, other arithmetic  2.55 us
    convert_element_type x2, other arithmetic, reduce_scatter(): onward = (keep[:, q:] + arrived[:, q:].astype(f32)).astype(bf16)  2.05 us
    pallas_call x2, Pallas kernels, mix(): pl.pallas_call(functools.partial(mix_kernel, scale, own_modes, len(arrive...  1.94 us
    concatenate x1, other arithmetic, body(): mix_full = jnp.concatenate([mix_here, to_core(mix_here)], axis=0)  1.72 us
  transfers between devices with their start and end apart: 27, of which 9 were waited for; matrix products, arithmetic and copies ran while one was open for 13% of the time, Pallas kernels for 11%

profile of v2, /device:TPU:0, one launch (start us, length us, event | category | flops | bytes accessed | tf_op | source)
XLA Modules:
  0.0 82.2 jit_solution(5797036743890066438)
XLA Ops:
  0.7 3.6 %forward_first.1 = (bf16[4,128,512]{2,1,0:T(8,128)(2,1)S(1)}, f32[4,128,512]{2,1,0:T(8,128)S(1)}, bf16[256,1024]{1,0:T(8,128)(2,1)S(1)}) custom-call(s32[2]{0:T(128)S(1)} %pad_add_fusion.place_ref, s32[1,128]{1,0:T(1,128)S(1)} %bitcast.10, bf16[16,1024,512]{2,1,0:T(8,128)(2,1)} %series_ref.3), custom_call_target="tpu_custom_call" | custom-call | flops 1073741824 | bytes 5767168 | tf_op jit(solution)/shard_map/forward_first/pallas_call | solution.py:88
  4.9 2.9 %collective-permute-start.15 = (bf16[4,128,512]{2,1,0:T(8,128)(2,1)S(1)}, bf16[4,128,512]{2,1,0:T(8,128)(2,1)}, u32[]{:S(2)}, u32[]{:S(2)}) collective-permute-start(bf16[4,128,512]{2,1,0:T(8,128)(2,1)S(1)} %get-tuple-element.28), channel_id=1, source_target_pairs={{0,2},{1,5},{2,0},{3,7},{4,6},{5,1},{6,4},{7,3},{8,10},{9,13},{10,... | collective-permute-start | bytes 1572872 | tf_op jit(solution)/shard_map/ppermute | solution.py:226
  9.6 4.4 %forward_second.1 = (bf16[4,128,512]{2,1,0:T(8,128)(2,1)}, f32[4,128,512]{2,1,0:T(8,128)S(1)}) custom-call(s32[2]{0:T(128)S(1)} %pad_add_fusion.place_ref, bf16[256,1024]{1,0:T(8,128)(2,1)S(1)} %get-tuple-element.19.extra_ref, bf16[16,1024,512]{2,1,0:T(8,128)(2,1)} %series_ref.3), custom_call_target="tpu_custom_call" | custom-call | flops 1073741824 | bytes 5767168 | tf_op jit(solution)/shard_map/forward_second/pallas_call | solution.py:88
  14.0 1.4 %collective-permute-start = (bf16[4,128,512]{2,1,0:T(8,128)(2,1)}, bf16[4,128,512]{2,1,0:T(8,128)(2,1)}, u32[]{:S(2)}, u32[]{:S(2)}) collective-permute-start(bf16[4,128,512]{2,1,0:T(8,128)(2,1)} %get-tuple-element.21), channel_id=1, source_target_pairs={{0,2},{1,5},{2,0},{3,7},{4,6},{5,1},{6,4},{7,3},{8,10},{9,13},{10,... | collective-permute-start | bytes 1572872 | tf_op jit(solution)/shard_map/ppermute | solution.py:226
  20.4 4.9 %collective-permute-done = bf16[4,128,512]{2,1,0:T(8,128)(2,1)} collective-permute-done((bf16[4,128,512]{2,1,0:T(8,128)(2,1)}, bf16[4,128,512]{2,1,0:T(8,128)(2,1)}, u32[]{:S(2)}, u32[]{:S(2)}) %collective-permute-start) | collective-permute-done | bytes 524320 | tf_op jit(solution)/shard_map/ppermute | solution.py:226
  26.3 2.6 %collective-permute-start.1 = (bf16[4,64,512]{2,1,0:T(8,128)(2,1)S(1)}, bf16[4,64,512]{2,1,0:T(8,128)(2,1)S(1)}, u32[]{:S(2)}, u32[]{:S(2)}) collective-permute-start(bf16[4,64,512]{2,1,0:T(8,128)(2,1)S(1)} %add_convert_fusion.1), channel_id=1, source_target_pairs={{0,4},{1,3},{2,6},{3,1},{4,0},{5,7},{6,2},{7,5},{8,12},{9,11},{10,... | collective-permute-start | bytes 786440 | tf_op jit(solution)/shard_map/ppermute | solution.py:226
  28.9 1.1 %fusion = (bf16[4,64,512]{2,1,0:T(8,128)(2,1)S(1)}, f32[4,64,512]{2,1,0:T(8,128)S(1)}) fusion(bf16[4,64,512]{2,1,0:T(8,128)(2,1)S(1)} %collective-permute-done.16, bf16[4,128,512]{2,1,0:T(8,128)(2,1)} %collective-permute-done.15, f32[4,128,512]{2,1,0:T(8,128)S(1)} %get-tuple-element.27), kind=kLoop, calls=%fused_computation.19 | loop fusion | flops 655360 | bytes 1835008 | tf_op jit(solution)/shard_map/convert.2
  30.0 3.7 %collective-permute-start.19 = (bf16[4,16,512]{2,1,0:T(8,128)(2,1)S(1)}, bf16[4,16,512]{2,1,0:T(8,128)(2,1)S(1)}, u32[]{:S(2)}, u32[]{:S(2)}) collective-permute-start(bf16[4,16,512]{2,1,0:T(8,128)(2,1)S(1)} %get-tuple-element.37), channel_id=1, source_target_pairs={{0,24},{1,25},{2,26},{3,27},{4,28},{5,29},{6,30},{7,31},{8,16},{9,... | collective-permute-start | bytes 196616 | tf_op jit(solution)/shard_map/ppermute | solution.py:226
  34.5 1.1 %fusion.1 = (bf16[4,64,512]{2,1,0:T(8,128)(2,1)S(1)}, f32[4,64,512]{2,1,0:T(8,128)S(1)}) fusion(bf16[4,64,512]{2,1,0:T(8,128)(2,1)S(1)} %collective-permute-done.1, bf16[4,128,512]{2,1,0:T(8,128)(2,1)} %collective-permute-done, f32[4,128,512]{2,1,0:T(8,128)S(1)} %get-tuple-element.20), kind=kLoop, calls=%fused_computation.20 | loop fusion | flops 655360 | bytes 1835008 | tf_op jit(solution)/shard_map/convert.10
  35.6 3.7 %collective-permute-start.4 = (bf16[4,16,512]{2,1,0:T(8,128)(2,1)S(1)}, bf16[4,16,512]{2,1,0:T(8,128)(2,1)S(1)}, u32[]{:S(2)}, u32[]{:S(2)}) collective-permute-start(bf16[4,16,512]{2,1,0:T(8,128)(2,1)S(1)} %get-tuple-element.40), channel_id=1, source_target_pairs={{0,24},{1,25},{2,26},{3,27},{4,28},{5,29},{6,30},{7,31},{8,16},{9,... | collective-permute-start | bytes 196616 | tf_op jit(solution)/shard_map/ppermute | solution.py:226
  39.3 1.7 %pad_maximum_fusion.refs_4_ = bf16[8,1024,128]{2,1,0:T(8,128)(2,1)S(1)} fusion(bf16[4,1024,128]{2,1,0:T(8,128)(2,1)} %collective-permute-done.6, bf16[4,1024,128]{2,1,0:T(8,128)(2,1)} %bitcast.5), kind=kLoop, calls=%fused_computation | loop fusion | flops 1048576 | bytes 4194304 | tf_op jit(solution)/shard_map/concatenate | solution.py:281
  43.0 1.5 %collective-permute-done.3.refs_1_ = bf16[4,16,512]{2,1,0:T(8,128)(2,1)S(1)} collective-permute-done((bf16[4,16,512]{2,1,0:T(8,128)(2,1)S(1)}, bf16[4,16,512]{2,1,0:T(8,128)(2,1)S(1)}, u32[]{:S(2)}, u32[]{:S(2)}) %collective-permute-start.3) | collective-permute-done | bytes 65568 | tf_op jit(solution)/shard_map/ppermute | solution.py:226
  46.5 2.4 %collective-permute-start.23 = (bf16[8,16,256]{2,1,0:T(8,128)(2,1)S(1)}, bf16[8,16,256]{2,1,0:T(8,128)(2,1)S(1)}, u32[]{:S(2)}, u32[]{:S(2)}) collective-permute-start(bf16[8,16,256]{2,1,0:T(8,128)(2,1)S(1)} %constant_dynamic-update-slice_fusion.6), channel_id=1, source_target_pairs={{0,24},{1,25},{2,26},{3,27},{4,28},{5,29},{6,30},{7,31},{8,16},{9,... | collective-permute-start | bytes 196616 | tf_op jit(solution)/shard_map/ppermute | solution.py:226
  49.5 1.4 %collective-permute-start.21 = (bf16[8,16,256]{2,1,0:T(8,128)(2,1)S(1)}, bf16[8,16,256]{2,1,0:T(8,128)(2,1)S(1)}, u32[]{:S(2)}, u32[]{:S(2)}) collective-permute-start(bf16[8,16,256]{2,1,0:T(8,128)(2,1)S(1)} %constant_dynamic-update-slice_fusion.6), channel_id=1, source_target_pairs={{0,8},{1,9},{2,10},{3,11},{4,12},{5,13},{6,14},{7,15},{8,0},{9,1},... | collective-permute-start | bytes 196616 | tf_op jit(solution)/shard_map/ppermute | solution.py:226
  51.0 2.4 %collective-permute-start.11 = (bf16[8,16,256]{2,1,0:T(8,128)(2,1)S(1)}, bf16[8,16,256]{2,1,0:T(8,128)(2,1)S(1)}, u32[]{:S(2)}, u32[]{:S(2)}) collective-permute-start(bf16[8,16,256]{2,1,0:T(8,128)(2,1)S(1)} %constant_dynamic-update-slice_fusion.4), channel_id=1, source_target_pairs={{0,24},{1,25},{2,26},{3,27},{4,28},{5,29},{6,30},{7,31},{8,16},{9,... | collective-permute-start | bytes 196616 | tf_op jit(solution)/shard_map/ppermute | solution.py:226
  53.3 2.4 %collective-permute-start.9 = (bf16[8,16,256]{2,1,0:T(8,128)(2,1)S(1)}, bf16[8,16,256]{2,1,0:T(8,128)(2,1)S(1)}, u32[]{:S(2)}, u32[]{:S(2)}) collective-permute-start(bf16[8,16,256]{2,1,0:T(8,128)(2,1)S(1)} %constant_dynamic-update-slice_fusion.4), channel_id=1, source_target_pairs={{0,8},{1,9},{2,10},{3,11},{4,12},{5,13},{6,14},{7,15},{8,0},{9,1},... | collective-permute-start | bytes 196616 | tf_op jit(solution)/shard_map/ppermute | solution.py:226
  55.7 3.7 %collective-permute-done.22 = bf16[8,16,256]{2,1,0:T(8,128)(2,1)S(1)} collective-permute-done((bf16[8,16,256]{2,1,0:T(8,128)(2,1)S(1)}, bf16[8,16,256]{2,1,0:T(8,128)(2,1)S(1)}, u32[]{:S(2)}, u32[]{:S(2)}) %collective-permute-start.22) | collective-permute-done | bytes 65568 | tf_op jit(solution)/shard_map/ppermute | solution.py:226
  60.3 1.6 %collective-permute-done.10 = bf16[8,16,256]{2,1,0:T(8,128)(2,1)S(1)} collective-permute-done((bf16[8,16,256]{2,1,0:T(8,128)(2,1)S(1)}, bf16[8,16,256]{2,1,0:T(8,128)(2,1)S(1)}, u32[]{:S(2)}, u32[]{:S(2)}) %collective-permute-start.10) | collective-permute-done | bytes 65568 | tf_op jit(solution)/shard_map/ppermute | solution.py:226
  63.7 3.5 %collective-permute-done.24.refs_1_ = bf16[8,64,256]{2,1,0:T(8,128)(2,1)S(1)} collective-permute-done((bf16[8,64,256]{2,1,0:T(8,128)(2,1)S(1)}, bf16[8,64,256]{2,1,0:T(8,128)(2,1)S(1)}, u32[]{:S(2)}, u32[]{:S(2)}) %collective-permute-start.24) | collective-permute-done | bytes 262176 | tf_op jit(solution)/shard_map/ppermute | solution.py:226
  67.1 2.0 %collective-permute-start.13 = (bf16[8,64,256]{2,1,0:T(8,128)(2,1)S(1)}, bf16[8,64,256]{2,1,0:T(8,128)(2,1)S(1)}, u32[]{:S(2)}, u32[]{:S(2)}) collective-permute-start(bf16[8,64,256]{2,1,0:T(8,128)(2,1)S(1)} %pad_maximum_fusion.1.refs_0_), channel_id=1, source_target_pairs={{0,2},{1,5},{2,0},{3,7},{4,6},{5,1},{6,4},{7,3},{8,10},{9,13},{10,... | collective-permute-start | bytes 786440 | tf_op jit(solution)/shard_map/ppermute | solution.py:226
  69.2 3.6 %collective-permute-done.12.refs_1_ = bf16[8,64,256]{2,1,0:T(8,128)(2,1)S(1)} collective-permute-done((bf16[8,64,256]{2,1,0:T(8,128)(2,1)S(1)}, bf16[8,64,256]{2,1,0:T(8,128)(2,1)S(1)}, u32[]{:S(2)}, u32[]{:S(2)}) %collective-permute-start.12) | collective-permute-done | bytes 262176 | tf_op jit(solution)/shard_map/ppermute | solution.py:226
  73.5 3.0 %inverse_first.1.refs_4_ = bf16[16,1024,256]{2,1,0:T(8,128)(2,1)} custom-call(s32[2]{0:T(128)S(1)} %pad_add_fusion.place_ref, bf16[1024,256]{1,0:T(8,128)(2,1)S(1)} %bitcast.8, bf16[8,64,256]{2,1,0:T(8,128)(2,1)S(1)} %pad_maximum_fusion.2.refs_0_, bf16[8,64,256]{2,1,0:T(8,128)(2,1)S(1)} %collective-permute-done.24.refs_1_, ...), custom_call_target="tpu_custom_call" | custom-call | flops 1073741824 | bytes 5242880 | tf_op jit(solution)/shard_map/inverse_first/pallas_call | solution.py:207
  76.6 2.6 %collective-permute-done.14.refs_3_ = bf16[8,64,256]{2,1,0:T(8,128)(2,1)S(1)} collective-permute-done((bf16[8,64,256]{2,1,0:T(8,128)(2,1)S(1)}, bf16[8,64,256]{2,1,0:T(8,128)(2,1)S(1)}, u32[]{:S(2)}, u32[]{:S(2)}) %collective-permute-start.14) | collective-permute-done | bytes 262176 | tf_op jit(solution)/shard_map/ppermute | solution.py:226
  79.1 3.0 %inverse_second.1 = bf16[16,1024,256]{2,1,0:T(8,128)(2,1)} custom-call(s32[2]{0:T(128)S(1)} %pad_add_fusion.place_ref, bf16[1024,256]{1,0:T(8,128)(2,1)S(1)} %bitcast.9, bf16[8,64,256]{2,1,0:T(8,128)(2,1)S(1)} %pad_maximum_fusion.1.refs_0_, bf16[8,64,256]{2,1,0:T(8,128)(2,1)S(1)} %collective-permute-done.12.refs_1_, ...), custom_call_target="tpu_custom_call", output_to_operand_aliasing={{}: (6, {})} | custom-call | flops 1073741824 | bytes 5242880 | tf_op jit(solution)/shard_map/inverse_second/pallas_call | solution.py:207
  (69 shorter events, 17.8 us)
Async XLA Ops:
  4.3 15.1 %collective-permute-start.5 = (bf16[512,256]{1,0:T(8,128)(2,1)}, bf16[512,256]{1,0:T(8,128)(2,1)}, u32[]{:S(2)}, u32[]{:S(2)}) collective-permute-start(bf16[512,256]{1,0:T(8,128)(2,1)} %param.7), channel_id=1, source_target_pairs={{0,1},{1,0},{2,3},{3,2},{4,5},{5,4},{6,7},{7,6},{8,9},{9,8},{10,11... | collective-permute-start | bytes 786440 | tf_op jit(solution)/shard_map/ppermute | solution.py:233
  4.8 11.6 %collective-permute-start.7 = (bf16[512,256]{1,0:T(8,128)(2,1)S(1)}, bf16[512,256]{1,0:T(8,128)(2,1)}, u32[]{:S(2)}, u32[]{:S(2)}) collective-permute-start(bf16[512,256]{1,0:T(8,128)(2,1)S(1)} %copy-done.2), channel_id=1, source_target_pairs={{0,1},{1,0},{2,3},{3,2},{4,5},{5,4},{6,7},{7,6},{8,9},{9,8},{10,11... | collective-permute-start | bytes 786440 | tf_op jit(solution)/shard_map/ppermute | solution.py:233
  4.9 12.7 %collective-permute-start.15 = (bf16[4,128,512]{2,1,0:T(8,128)(2,1)S(1)}, bf16[4,128,512]{2,1,0:T(8,128)(2,1)}, u32[]{:S(2)}, u32[]{:S(2)}) collective-permute-start(bf16[4,128,512]{2,1,0:T(8,128)(2,1)S(1)} %get-tuple-element.28), channel_id=1, source_target_pairs={{0,2},{1,5},{2,0},{3,7},{4,6},{5,1},{6,4},{7,3},{8,10},{9,13},{10,... | collective-permute-start | bytes 1572872 | tf_op jit(solution)/shard_map/ppermute | solution.py:226
  9.6 29.6 %collective-permute-start.6 = (bf16[4,1024,128]{2,1,0:T(8,128)(2,1)}, bf16[4,1024,128]{2,1,0:T(8,128)(2,1)}, u32[]{:S(2)}, u32[]{:S(2)}) collective-permute-start(bf16[4,1024,128]{2,1,0:T(8,128)(2,1)} %bitcast.5), channel_id=1, source_target_pairs={{0,1},{1,0},{2,3},{3,2},{4,5},{5,4},{6,7},{7,6},{8,9},{9,8},{10,11... | collective-permute-start | bytes 3145736 | tf_op jit(solution)/shard_map/ppermute | solution.py:233
  14.0 11.3 %collective-permute-start = (bf16[4,128,512]{2,1,0:T(8,128)(2,1)}, bf16[4,128,512]{2,1,0:T(8,128)(2,1)}, u32[]{:S(2)}, u32[]{:S(2)}) collective-permute-start(bf16[4,128,512]{2,1,0:T(8,128)(2,1)} %get-tuple-element.21), channel_id=1, source_target_pairs={{0,2},{1,5},{2,0},{3,7},{4,6},{5,1},{6,4},{7,3},{8,10},{9,13},{10,... | collective-permute-start | bytes 1572872 | tf_op jit(solution)/shard_map/ppermute | solution.py:226
  18.6 10.3 %collective-permute-start.16 = (bf16[4,64,512]{2,1,0:T(8,128)(2,1)S(1)}, bf16[4,64,512]{2,1,0:T(8,128)(2,1)S(1)}, u32[]{:S(2)}, u32[]{:S(2)}) collective-permute-start(bf16[4,64,512]{2,1,0:T(8,128)(2,1)S(1)} %add_convert_fusion), channel_id=1, source_target_pairs={{0,4},{1,3},{2,6},{3,1},{4,0},{5,7},{6,2},{7,5},{8,12},{9,11},{10,... | collective-permute-start | bytes 786440 | tf_op jit(solution)/shard_map/ppermute | solution.py:226
  26.3 8.2 %collective-permute-start.1 = (bf16[4,64,512]{2,1,0:T(8,128)(2,1)S(1)}, bf16[4,64,512]{2,1,0:T(8,128)(2,1)S(1)}, u32[]{:S(2)}, u32[]{:S(2)}) collective-permute-start(bf16[4,64,512]{2,1,0:T(8,128)(2,1)S(1)} %add_convert_fusion.1), channel_id=1, source_target_pairs={{0,4},{1,3},{2,6},{3,1},{4,0},{5,7},{6,2},{7,5},{8,12},{9,11},{10,... | collective-permute-start | bytes 786440 | tf_op jit(solution)/shard_map/ppermute | solution.py:226
  30.0 11.1 %collective-permute-start.19 = (bf16[4,16,512]{2,1,0:T(8,128)(2,1)S(1)}, bf16[4,16,512]{2,1,0:T(8,128)(2,1)S(1)}, u32[]{:S(2)}, u32[]{:S(2)}) collective-permute-start(bf16[4,16,512]{2,1,0:T(8,128)(2,1)S(1)} %get-tuple-element.37), channel_id=1, source_target_pairs={{0,24},{1,25},{2,26},{3,27},{4,28},{5,29},{6,30},{7,31},{8,16},{9,... | collective-permute-start | bytes 196616 | tf_op jit(solution)/shard_map/ppermute | solution.py:226
  33.7 8.3 %collective-permute-start.18 = (bf16[4,16,512]{2,1,0:T(8,128)(2,1)S(1)}, bf16[4,16,512]{2,1,0:T(8,128)(2,1)S(1)}, u32[]{:S(2)}, u32[]{:S(2)}) collective-permute-start(bf16[4,16,512]{2,1,0:T(8,128)(2,1)S(1)} %get-tuple-element.38), channel_id=1, source_target_pairs={{0,16},{1,17},{2,18},{3,19},{4,20},{5,21},{6,22},{7,23},{8,24},{9,... | collective-permute-start | bytes 196616 | tf_op jit(solution)/shard_map/ppermute | solution.py:226
  33.7 8.3 %collective-permute-start.17 = (bf16[4,16,512]{2,1,0:T(8,128)(2,1)S(1)}, bf16[4,16,512]{2,1,0:T(8,128)(2,1)S(1)}, u32[]{:S(2)}, u32[]{:S(2)}) collective-permute-start(bf16[4,16,512]{2,1,0:T(8,128)(2,1)S(1)} %get-tuple-element.39), channel_id=1, source_target_pairs={{0,8},{1,9},{2,10},{3,11},{4,12},{5,13},{6,14},{7,15},{8,0},{9,1},... | collective-permute-start | bytes 196616 | tf_op jit(solution)/shard_map/ppermute | solution.py:226
  35.6 7.4 %collective-permute-start.4 = (bf16[4,16,512]{2,1,0:T(8,128)(2,1)S(1)}, bf16[4,16,512]{2,1,0:T(8,128)(2,1)S(1)}, u32[]{:S(2)}, u32[]{:S(2)}) collective-permute-start(bf16[4,16,512]{2,1,0:T(8,128)(2,1)S(1)} %get-tuple-element.40), channel_id=1, source_target_pairs={{0,24},{1,25},{2,26},{3,27},{4,28},{5,29},{6,30},{7,31},{8,16},{9,... | collective-permute-start | bytes 196616 | tf_op jit(solution)/shard_map/ppermute | solution.py:226
  39.3 5.2 %collective-permute-start.3 = (bf16[4,16,512]{2,1,0:T(8,128)(2,1)S(1)}, bf16[4,16,512]{2,1,0:T(8,128)(2,1)S(1)}, u32[]{:S(2)}, u32[]{:S(2)}) collective-permute-start(bf16[4,16,512]{2,1,0:T(8,128)(2,1)S(1)} %get-tuple-element.41), channel_id=1, source_target_pairs={{0,16},{1,17},{2,18},{3,19},{4,20},{5,21},{6,22},{7,23},{8,24},{9,... | collective-permute-start | bytes 196616 | tf_op jit(solution)/shard_map/ppermute | solution.py:226
  46.5 6.8 %collective-permute-start.23 = (bf16[8,16,256]{2,1,0:T(8,128)(2,1)S(1)}, bf16[8,16,256]{2,1,0:T(8,128)(2,1)S(1)}, u32[]{:S(2)}, u32[]{:S(2)}) collective-permute-start(bf16[8,16,256]{2,1,0:T(8,128)(2,1)S(1)} %constant_dynamic-update-slice_fusion.6), channel_id=1, source_target_pairs={{0,24},{1,25},{2,26},{3,27},{4,28},{5,29},{6,30},{7,31},{8,16},{9,... | collective-permute-start | bytes 196616 | tf_op jit(solution)/shard_map/ppermute | solution.py:226
  48.9 10.5 %collective-permute-start.22 = (bf16[8,16,256]{2,1,0:T(8,128)(2,1)S(1)}, bf16[8,16,256]{2,1,0:T(8,128)(2,1)S(1)}, u32[]{:S(2)}, u32[]{:S(2)}) collective-permute-start(bf16[8,16,256]{2,1,0:T(8,128)(2,1)S(1)} %constant_dynamic-update-slice_fusion.6), channel_id=1, source_target_pairs={{0,16},{1,17},{2,18},{3,19},{4,20},{5,21},{6,22},{7,23},{8,24},{9,... | collective-permute-start | bytes 196616 | tf_op jit(solution)/shard_map/ppermute | solution.py:226
  49.5 9.9 %collective-permute-start.21 = (bf16[8,16,256]{2,1,0:T(8,128)(2,1)S(1)}, bf16[8,16,256]{2,1,0:T(8,128)(2,1)S(1)}, u32[]{:S(2)}, u32[]{:S(2)}) collective-permute-start(bf16[8,16,256]{2,1,0:T(8,128)(2,1)S(1)} %constant_dynamic-update-slice_fusion.6), channel_id=1, source_target_pairs={{0,8},{1,9},{2,10},{3,11},{4,12},{5,13},{6,14},{7,15},{8,0},{9,1},... | collective-permute-start | bytes 196616 | tf_op jit(solution)/shard_map/ppermute | solution.py:226
  51.0 9.4 %collective-permute-start.11 = (bf16[8,16,256]{2,1,0:T(8,128)(2,1)S(1)}, bf16[8,16,256]{2,1,0:T(8,128)(2,1)S(1)}, u32[]{:S(2)}, u32[]{:S(2)}) collective-permute-start(bf16[8,16,256]{2,1,0:T(8,128)(2,1)S(1)} %constant_dynamic-update-slice_fusion.4), channel_id=1, source_target_pairs={{0,24},{1,25},{2,26},{3,27},{4,28},{5,29},{6,30},{7,31},{8,16},{9,... | collective-permute-start | bytes 196616 | tf_op jit(solution)/shard_map/ppermute | solution.py:226
  53.3 8.7 %collective-permute-start.10 = (bf16[8,16,256]{2,1,0:T(8,128)(2,1)S(1)}, bf16[8,16,256]{2,1,0:T(8,128)(2,1)S(1)}, u32[]{:S(2)}, u32[]{:S(2)}) collective-permute-start(bf16[8,16,256]{2,1,0:T(8,128)(2,1)S(1)} %constant_dynamic-update-slice_fusion.4), channel_id=1, source_target_pairs={{0,16},{1,17},{2,18},{3,19},{4,20},{5,21},{6,22},{7,23},{8,24},{9,... | collective-permute-start | bytes 196616 | tf_op jit(solution)/shard_map/ppermute | solution.py:226
  53.3 8.7 %collective-permute-start.9 = (bf16[8,16,256]{2,1,0:T(8,128)(2,1)S(1)}, bf16[8,16,256]{2,1,0:T(8,128)(2,1)S(1)}, u32[]{:S(2)}, u32[]{:S(2)}) collective-permute-start(bf16[8,16,256]{2,1,0:T(8,128)(2,1)S(1)} %constant_dynamic-update-slice_fusion.4), channel_id=1, source_target_pairs={{0,8},{1,9},{2,10},{3,11},{4,12},{5,13},{6,14},{7,15},{8,0},{9,1},... | collective-permute-start | bytes 196616 | tf_op jit(solution)/shard_map/ppermute | solution.py:226
  59.5 7.7 %collective-permute-start.24 = (bf16[8,64,256]{2,1,0:T(8,128)(2,1)S(1)}, bf16[8,64,256]{2,1,0:T(8,128)(2,1)S(1)}, u32[]{:S(2)}, u32[]{:S(2)}) collective-permute-start(bf16[8,64,256]{2,1,0:T(8,128)(2,1)S(1)} %pad_maximum_fusion.2.refs_0_), channel_id=1, source_target_pairs={{0,4},{1,3},{2,6},{3,1},{4,0},{5,7},{6,2},{7,5},{8,12},{9,11},{10,... | collective-permute-start | bytes 786440 | tf_op jit(solution)/shard_map/ppermute | solution.py:226
  62.0 10.8 %collective-permute-start.12 = (bf16[8,64,256]{2,1,0:T(8,128)(2,1)S(1)}, bf16[8,64,256]{2,1,0:T(8,128)(2,1)S(1)}, u32[]{:S(2)}, u32[]{:S(2)}) collective-permute-start(bf16[8,64,256]{2,1,0:T(8,128)(2,1)S(1)} %pad_maximum_fusion.1.refs_0_), channel_id=1, source_target_pairs={{0,4},{1,3},{2,6},{3,1},{4,0},{5,7},{6,2},{7,5},{8,12},{9,11},{10,... | collective-permute-start | bytes 786440 | tf_op jit(solution)/shard_map/ppermute | solution.py:226
  62.9 10.1 %collective-permute-start.25 = (bf16[8,64,256]{2,1,0:T(8,128)(2,1)S(1)}, bf16[8,64,256]{2,1,0:T(8,128)(2,1)S(1)}, u32[]{:S(2)}, u32[]{:S(2)}) collective-permute-start(bf16[8,64,256]{2,1,0:T(8,128)(2,1)S(1)} %pad_maximum_fusion.2.refs_0_), channel_id=1, source_target_pairs={{0,2},{1,5},{2,0},{3,7},{4,6},{5,1},{6,4},{7,3},{8,10},{9,13},{10,... | collective-permute-start | bytes 786440 | tf_op jit(solution)/shard_map/ppermute | solution.py:226
  67.1 6.4 %collective-permute-start.26 = (bf16[8,64,256]{2,1,0:T(8,128)(2,1)S(1)}, bf16[8,64,256]{2,1,0:T(8,128)(2,1)S(1)}, u32[]{:S(2)}, u32[]{:S(2)}) collective-permute-start(bf16[8,64,256]{2,1,0:T(8,128)(2,1)S(1)} %collective-permute-done.24.refs_1_), channel_id=1, source_target_pairs={{0,2},{1,5},{2,0},{3,7},{4,6},{5,1},{6,4},{7,3},{8,10},{9,13},{10,... | collective-permute-start | bytes 786440 | tf_op jit(solution)/shard_map/ppermute | solution.py:226
  67.1 9.4 %collective-permute-start.13 = (bf16[8,64,256]{2,1,0:T(8,128)(2,1)S(1)}, bf16[8,64,256]{2,1,0:T(8,128)(2,1)S(1)}, u32[]{:S(2)}, u32[]{:S(2)}) collective-permute-start(bf16[8,64,256]{2,1,0:T(8,128)(2,1)S(1)} %pad_maximum_fusion.1.refs_0_), channel_id=1, source_target_pairs={{0,2},{1,5},{2,0},{3,7},{4,6},{5,1},{6,4},{7,3},{8,10},{9,13},{10,... | collective-permute-start | bytes 786440 | tf_op jit(solution)/shard_map/ppermute | solution.py:226
  72.8 6.4 %collective-permute-start.14 = (bf16[8,64,256]{2,1,0:T(8,128)(2,1)S(1)}, bf16[8,64,256]{2,1,0:T(8,128)(2,1)S(1)}, u32[]{:S(2)}, u32[]{:S(2)}) collective-permute-start(bf16[8,64,256]{2,1,0:T(8,128)(2,1)S(1)} %collective-permute-done.12.refs_1_), channel_id=1, source_target_pairs={{0,2},{1,5},{2,0},{3,7},{4,6},{5,1},{6,4},{7,3},{8,10},{9,13},{10,... | collective-permute-start | bytes 786440 | tf_op jit(solution)/shard_map/ppermute | solution.py:226
  (6 other events, 24.3 us)

commit v3 on v2

v3 whole, which is shorter than its diff:
```python
import functools
import math

import jax
import jax.numpy as jnp
from jax import lax
from jax.experimental import pallas as pl
from jax.experimental.pallas import tpu as pltpu
from jax.sharding import PartitionSpec as P

f32 = jnp.float32
bf16 = jnp.bfloat16
two_pi = 2.0 * math.pi


def in_vmem(shape, dtype):
    return pltpu.VMEM(shape, dtype)


def held(*arrays):
    return [pltpu.with_memory_space_constraint(array, pltpu.VMEM) for array in arrays]


def in_hbm(array):
    return pltpu.with_memory_space_constraint(array, pltpu.HBM)


def after(array, *others):
    return lax.optimization_barrier((array, *others))[0]


whole = pl.BlockSpec(memory_space=pltpu.VMEM)
small = pl.CostEstimate(flops=1000, bytes_accessed=1000, transcendentals=0)


def row_modes(place, core, modes_row, rows, own_modes, series_length):
    lanes = modes_row.shape[1]
    row = lax.broadcasted_iota(jnp.int32, (rows, lanes), 0)
    lane = lax.broadcasted_iota(jnp.int32, (rows, lanes), 1)
    block_rows = 2 * own_modes
    far = rows // block_rows // 4
    block = row // block_rows
    inside = row - block * block_rows
    quarter = block // far
    relative = (quarter // 2) * (1 + core) + (quarter % 2) * (2 - core) + 4 * (block % far)
    imaginary = inside // own_modes
    wanted = (place ^ relative) * own_modes + inside - imaginary * own_modes
    picked = jnp.where(lane == wanted, modes_row.astype(f32), 0.0)
    mode = jnp.sum(picked, axis=1, keepdims=True).astype(jnp.int32)
    return mode, imaginary[:, :1] * (series_length // 4)


def wave(phases, series_length):
    turns = phases.astype(f32) * (1.0 / series_length)
    quarters = jnp.floor(turns * 4.0 + 0.5)
    angle = (turns - quarters * 0.25) * two_pi
    square = angle * angle
    cosine = 1.0 + square * (-0.5 + square * (1 / 24 + square * (-1 / 720 + square * (1 / 40320))))
    sine = angle * (1.0 + square * (-1 / 6 + square * (1 / 120 + square * (-1 / 5040))))
    which = quarters.astype(jnp.int32)
    odd = which & 1 == 1
    cos_size = jnp.where(odd, sine, cosine)
    sin_size = jnp.where(odd, cosine, sine)
    cos_flip = (which == 1) | (which == 2)
    sin_flip = (which == 2) | (which == 3)
    return jnp.where(cos_flip, -cos_size, cos_size), jnp.where(sin_flip, -sin_size, sin_size)


def fill_table(modes_ref, table_ref, own_modes, series_length):
    rows, time_count = table_ref.shape
    place = lax.axis_index("tm")
    mode, shift = row_modes(place, lax.axis_index("head"), modes_ref[...], rows, own_modes, series_length)
    lane = lax.broadcasted_iota(jnp.int32, (rows, 128), 1)
    last = series_length - 1
    cos_a, sin_a = wave((mode * (place * time_count + lane * 128) + shift) & last, series_length)
    cos_b, sin_b = wave((mode * lane) & last, series_length)
    for piece in range(time_count // 128):
        value = cos_a[:, piece:piece + 1] * cos_b - sin_a[:, piece:piece + 1] * sin_b
        table_ref[:, piece * 128:piece * 128 + 128] = value.astype(bf16)


def forward_kernel(first, count, offset, half, own_modes, series_length, extra_ref, series_ref, *refs):
    if first:
        send_ref, keep_ref, table_ref, held, sems = refs
    else:
        send_ref, keep_ref, held, sems = refs
        table_ref = extra_ref
    base = lax.axis_index("head") * half + offset
    copies = [pltpu.make_async_copy(series_ref.at[base + b], held.at[b], sems.at[b]) for b in range(count)]
    for copy in copies:
        copy.start()
    if first:
        fill_table(extra_ref, table_ref, own_modes, series_length)
    middle = table_ref.shape[0] // 2
    for b in range(count):
        copies[b].wait()
        part = jnp.dot(table_ref[...], held[b], preferred_element_type=f32)
        send_ref[b] = part[middle:].astype(bf16)
        keep_ref[b] = part[:middle]


def forward(first, series, extra, count, offset, half, own_modes, series_length, rows):
    _, time_count, width = series.shape
    outs = [in_vmem((count, rows // 2, width), bf16), in_vmem((count, rows // 2, width), f32)]
    if first:
        outs.append(in_vmem((rows, time_count), bf16))
        extra = in_hbm(extra)
    else:
        extra, = held(extra)
    return pl.pallas_call(
        functools.partial(forward_kernel, first, count, offset, half, own_modes, series_length),
        out_shape=outs,
        in_specs=[whole, pl.BlockSpec(memory_space=pltpu.HBM)],
        out_specs=[whole] * len(outs),
        scratch_shapes=[pltpu.VMEM((count, time_count, width), bf16), pltpu.SemaphoreType.DMA((count,))],
        compiler_params=pltpu.CompilerParams(vmem_limit_bytes=16 * 2**20),
        cost_estimate=small,
        name="forward_first" if first else "forward_second",
    )(extra, in_hbm(series))


def onward_kernel(keep_ref, arrived_ref, out_ref):
    middle = keep_ref.shape[1] // 2
    out_ref[...] = (keep_ref[:, middle:] + arrived_ref[:, middle:].astype(f32)).astype(bf16)


def onward(keep, arrived):
    count, rows, width = keep.shape
    return pl.pallas_call(
        onward_kernel,
        out_shape=in_vmem((count, rows // 2, width), bf16),
        in_specs=[whole] * 2,
        out_specs=whole,
        compiler_params=pltpu.CompilerParams(vmem_limit_bytes=16 * 2**20),
        cost_estimate=small,
        name="sum_onward",
    )(*held(keep, arrived))


def total_kernel(block_rows, keep_ref, arrived_ref, second_ref, own_ref, *far_refs):
    middle = second_ref.shape[1]
    total = keep_ref[:, :middle] + arrived_ref[:, :middle].astype(f32) + second_ref[...].astype(f32)
    own_ref[...] = total[:, :block_rows]
    for index, ref in enumerate(far_refs):
        ref[...] = total[:, (index + 1) * block_rows:(index + 2) * block_rows].astype(bf16)


def total_rows(keep, arrived, second, block_rows):
    count, rows, width = second.shape
    if block_rows % 16:
        total = keep[:, :rows] + arrived[:, :rows].astype(f32) + second.astype(f32)
        parts = [total[:, start:start + block_rows] for start in range(0, rows, block_rows)]
        return parts[0], [part.astype(bf16) for part in parts[1:]]
    share = (count, block_rows, width)
    parts = pl.pallas_call(
        functools.partial(total_kernel, block_rows),
        out_shape=[in_vmem(share, f32)] + [in_vmem(share, bf16)] * (rows // block_rows - 1),
        in_specs=[whole] * 3,
        out_specs=[whole] * (rows // block_rows),
        compiler_params=pltpu.CompilerParams(vmem_limit_bytes=16 * 2**20),
        cost_estimate=small,
        name="sum_total",
    )(*held(keep, arrived, second))
    return parts[0], parts[1:]


def prepare_kernel(weight_ref, table_ref, *out_refs):
    modes, heads, size, width = weight_ref.shape
    negative = lax.broadcasted_iota(jnp.int32, (size, width), 1) < size
    for m in range(modes):
        for h in range(heads):
            weight = weight_ref[m, h]
            turned = pltpu.roll(weight, size, 1)
            start = 2 * size * m
            out_refs[h][start:start + size] = weight.astype(bf16)
            out_refs[h][start + size:start + 2 * size] = jnp.where(negative, -turned, turned).astype(bf16)
    out_refs[heads][...] = table_ref[...].T


def prepare(weight, table):
    modes, heads, size, width = weight.shape
    outs = pl.pallas_call(
        prepare_kernel,
        out_shape=[in_vmem((modes * 2 * size, width), bf16)] * heads + [in_vmem(table.shape[::-1], bf16)],
        in_specs=[whole] * 2,
        out_specs=[whole] * (heads + 1),
        compiler_params=pltpu.CompilerParams(vmem_limit_bytes=16 * 2**20),
        cost_estimate=small,
        name="prepare_mix",
    )(in_hbm(weight), *held(table))
    return outs[:heads], outs[heads]


def split_rows(value):
    high = value.astype(bf16)
    low = (value - high.astype(f32)).astype(bf16)
    return jnp.concatenate([high, low], axis=0)


def fold_rows(value):
    half = value.shape[0] // 2
    return value[:half] + value[half:]


def mix_kernel(scale, own_modes, arrivals, own_ref, *refs):
    arrived = refs[:arrivals]
    query_refs, out_weight_refs, mix_refs = refs[arrivals:arrivals + 2], refs[arrivals + 2:arrivals + 4], refs[arrivals + 4:-2]
    here_ref, there_ref = refs[-2:]
    total = own_ref[...]
    for ref in arrived:
        total = total + ref[...].astype(f32)
    total = total * scale
    count, _, width = total.shape
    rows = count * own_modes
    half = width // 2
    core = lax.axis_index("head")
    pieces = split_rows(jnp.concatenate(
        [total[:, :own_modes].reshape(rows, width), total[:, own_modes:].reshape(rows, width)], axis=0
    ))
    lower = lax.broadcasted_iota(jnp.int32, (rows, 128), 1) < 64
    row_mode = lax.broadcasted_iota(jnp.int32, (2 * rows, 128), 0) % own_modes
    mixed = []
    for group, query_ref in enumerate(query_refs):
        queries = fold_rows(jnp.dot(pieces, query_ref[...], preferred_element_type=f32))
        mixed_real, mixed_imag = [], []
        for pair in range(half // 128):
            columns = slice(pair * 128, pair * 128 + 128)
            real, imag = queries[:rows, columns], queries[rows:, columns]
            both = [
                jnp.where(lower, real, pltpu.roll(imag, 64, 1)),
                jnp.where(lower, pltpu.roll(real, 64, 1), imag),
            ]
            heads = []
            for which in range(2):
                spread = split_rows(both[which])
                zero = jnp.zeros_like(spread)
                spread = jnp.concatenate([jnp.where(row_mode == k, spread, zero) for k in range(own_modes)], axis=1)
                mix_ref = mix_refs[group * (half // 64) + 2 * pair + which]
                heads.append(fold_rows(jnp.dot(spread, mix_ref[...], preferred_element_type=f32)))
            mixed_real.append(jnp.where(lower, heads[0], pltpu.roll(heads[1], 64, 1)))
            mixed_imag.append(jnp.where(lower, pltpu.roll(heads[0], 64, 1), heads[1]))
        both = jnp.concatenate([jnp.concatenate(mixed_real, axis=1), jnp.concatenate(mixed_imag, axis=1)], axis=0)
        mixed.append(split_rows(both))
    first = jnp.where(core == 0, mixed[0], mixed[1])
    second = jnp.where(core == 0, mixed[1], mixed[0])
    both = jnp.concatenate([first, second], axis=1)
    for weight_ref, out_ref in zip(out_weight_refs, (here_ref, there_ref)):
        result = fold_rows(jnp.dot(both, weight_ref[...], preferred_element_type=f32)).astype(bf16)
        out_ref[...] = jnp.concatenate(
            [result[:rows].reshape(count, own_modes, half), result[rows:].reshape(count, own_modes, half)], axis=1
        )


def mix(own, arrived, queries, outs, mixes, scale, own_modes):
    count, block_rows, width = own.shape
    here = width // 2
    if own_modes % 8 == 0:
        shape = in_vmem((count, block_rows, here), bf16)
        return pl.pallas_call(
            functools.partial(mix_kernel, scale, own_modes, len(arrived)),
            out_shape=[shape, shape],
            in_specs=[whole] * (5 + len(arrived) + len(mixes)),
            out_specs=[whole, whole],
            compiler_params=pltpu.CompilerParams(vmem_limit_bytes=16 * 2**20),
            cost_estimate=small,
            name="mix_modes",
        )(*held(own, *arrived, *queries, *outs, *mixes))
    core = lax.axis_index("head")
    highest = lax.Precision.HIGHEST
    total = (own + sum(piece.astype(f32) for piece in arrived)) * scale
    mixed = []
    heads = len(mixes) // 2
    for group, query in enumerate(queries):
        weights = jnp.stack(mixes[group * heads:(group + 1) * heads])
        projected = jnp.einsum("brf,fg->brg", total, query.astype(f32), precision=highest)
        projected = projected.reshape(count, 2, own_modes, heads, 64)
        weights = weights.reshape(heads, own_modes, 2, 64, 2, 64).astype(f32)
        part = jnp.einsum("brmhi,hmriso->bsmho", projected, weights, precision=highest)
        mixed.append(part.reshape(count, block_rows, here))
    mixed = jnp.concatenate(mixed, axis=2)
    results = []
    for out_weight in outs:
        rolled = jnp.where(core == 0, out_weight, jnp.roll(out_weight, here, axis=0)).astype(f32)
        results.append(jnp.einsum("brf,fg->brg", mixed, rolled, precision=highest).astype(bf16))
    return results


def inverse_kernel(half, offset, table_ref, *refs):
    pieces, (out_ref, held, sems) = refs[:4], refs[-3:]
    count = held.shape[0]
    own = count // 2
    core = lax.axis_index("head")
    copies = []
    for b in range(count):
        spectra = jnp.concatenate([piece[b] for piece in pieces], axis=0)
        held[b] = jnp.dot(table_ref[...], spectra, preferred_element_type=f32).astype(bf16)
        index = (core ^ (b // own)) * half + offset + b % own
        copies.append(pltpu.make_async_copy(held.at[b], out_ref.at[index], sems.at[b]))
        copies[-1].start()
    for copy in copies:
        copy.wait()


def inverse(table, pieces, previous, series_count, half, offset):
    time_count, rows = table.shape
    count, _, width = pieces[0].shape
    in_specs = [whole] * 5
    args = held(table, *pieces)
    aliases = {}
    if previous is not None:
        in_specs.append(pl.BlockSpec(memory_space=pltpu.HBM))
        aliases = {len(args): 0}
        args.append(in_hbm(previous))
    return pl.pallas_call(
        functools.partial(inverse_kernel, half, offset),
        out_shape=pltpu.HBM((series_count, time_count, width), bf16),
        in_specs=in_specs,
        out_specs=pl.BlockSpec(memory_space=pltpu.HBM),
        scratch_shapes=[pltpu.VMEM((count, time_count, width), bf16), pltpu.SemaphoreType.DMA((count,))],
        input_output_aliases=aliases,
        compiler_params=pltpu.CompilerParams(vmem_limit_bytes=16 * 2**20),
        cost_estimate=small,
        name="inverse_first" if previous is None else "inverse_second",
    )(*args)


def to_devices(value, masks, size):
    pairs = [(2 * i + c, 2 * (i ^ masks[c]) + c) for i in range(size) for c in range(2)]
    return lax.ppermute(value, ("tm", "head"), pairs)


going_first, going_second = (1, 2), (2, 1)


def to_core(value):
    return lax.ppermute(value, "head", [(0, 1), (1, 0)])


def send_far(parts, size):
    return [to_devices(parts[z - 1], (4 * z, 4 * z), size) for z in range(len(parts), 0, -1)]


def join_kernel(*refs):
    out_ref = refs[-1]
    rows = refs[0].shape[1]
    for index, ref in enumerate(refs[:-1]):
        out_ref[:, index * rows:(index + 1) * rows] = ref[...]


def gather_far(block, size):
    far = [to_devices(block, (4 * z, 4 * z), size) for z in range(size // 4 - 1, 0, -1)]
    pieces = [block] + far[::-1]
    count, rows, width = block.shape
    if rows % 16:
        return jnp.concatenate(pieces, axis=1)
    return pl.pallas_call(
        join_kernel,
        out_shape=in_vmem((count, rows * len(pieces), width), bf16),
        in_specs=[whole] * len(pieces),
        out_specs=whole,
        compiler_params=pltpu.CompilerParams(vmem_limit_bytes=16 * 2**20),
        cost_estimate=small,
        name="join_rows",
    )(*held(*pieces))


def body(series, modes, query_weight, mix_weight, out_weight):
    series_count, shard_rows, width = series.shape
    own_modes, heads_here, head_size, _ = mix_weight.shape
    mode_total = modes.shape[0]
    size = lax.axis_size("tm")
    series_length = size * shard_rows
    rows = 2 * mode_total
    half = series_count // 2
    count_a = half // 2
    count_b = half - count_a

    send_a, keep_a, table = forward(
        True, series, modes[None, :], count_a, 0, half, own_modes, series_length, rows
    )
    send_b, keep_b = forward(False, series, table, count_b, count_a, half, own_modes, series_length, rows)
    block_rows = 2 * own_modes
    scale = 1.0 / math.sqrt(series_length * mode_total)
    arrived_a = to_devices(send_a, going_first, size)
    arrived_b = to_devices(send_b, going_first, size)

    mix_here, table_back = prepare(mix_weight, table)
    query_weight, out_weight = after(query_weight, table), after(out_weight, table)
    weights = [[query_weight, to_core(query_weight)], [out_weight, to_core(out_weight)]]
    weights.append([*mix_here, *(to_core(w) for w in mix_here)])

    onward_a = onward(after(keep_a, keep_b, mix_here[0]), arrived_a)
    second_a = to_devices(onward_a, going_second, size)
    onward_b = onward(after(keep_b, onward_a), arrived_b)
    second_b = to_devices(onward_b, going_second, size)
    own_a, far_a = total_rows(after(keep_a, onward_b), arrived_a, second_a, block_rows)
    far_a = send_far(far_a, size)
    own_b, far_b = total_rows(after(keep_b, own_a), arrived_b, second_b, block_rows)
    far_b = send_far(far_b, size)

    here_a, there_a = mix(after(own_a, own_b), far_a, *weights, scale, own_modes)
    block_a = jnp.concatenate([here_a, to_core(there_a)], axis=0)
    here_b, there_b = mix(after(own_b, block_a), far_b, *weights, scale, own_modes)
    block_b = jnp.concatenate([here_b, to_core(there_b)], axis=0)
    rows_a = after(gather_far(block_a, size), block_b)
    second_a = to_devices(rows_a, going_second, size)
    first_a = to_devices(rows_a, going_first, size)
    both_a = to_devices(second_a, going_first, size)
    rows_b = gather_far(block_b, size)
    second_b = to_devices(rows_b, going_second, size)
    first_b = to_devices(rows_b, going_first, size)
    pieces_a = [after(rows_a, second_b), second_a, first_a, both_a]
    output = inverse(table_back, pieces_a, None, series_count, half, 0)
    both_b = to_devices(after(second_b, first_a), going_first, size)
    return inverse(table_back, [rows_b, second_b, first_b, both_b], output, series_count, half, count_a)


def solution(mesh):
    in_specs = (
        P(None, "tm", None),
        P(),
        P(None, "head"),
        P("tm", "head", None, None),
        P(None, "head"),
    )
    out_specs = P(None, "tm", "head")
    return jax.shard_map(body, mesh=mesh, in_specs=in_specs, out_specs=out_specs, check_vma=False)
```

time: 82.7 us -> 73.3 us (0.89)
  other arithmetic: 6.89 us -> 0 us
  local copies, waits for them, and re-layouts: 4.93 us -> 0.02 us
  starting transfers between devices: 31.2 us -> 35 us
  waiting for transfers between devices: 22.9 us -> 21.6 us
    ppermute x22, waiting for transfers between devices: 22.9 us -> 19.2 us  [to_devices(): return lax.ppermute(value, ('tm', 'head'), pairs)]
    ppermute x22, starting transfers between devices: 30.5 us -> 33.8 us  [to_devices(): return lax.ppermute(value, ('tm', 'head'), pairs)]
    another operation x5 -> x0, other arithmetic: 2.62 us -> none
    ppermute x5 -> x8, waiting for transfers between devices: 0.01 us -> 2.38 us  [to_core(): return lax.ppermute(value, 'head', [(0, 1), (1, 0)])]
    convert_element_type x2 -> x0, other arithmetic: 2.05 us -> none  [reduce_scatter(): onward = (keep[:, q:] + arrived[:, q:].astype(f32)).astype(bf16)]
    concatenate x4 -> x2, local copies, waits for them, and re-layouts: 1.94 us -> 0.01 us  [the longest x1 0.01 us: body(): block_a = jnp.concatenate([here_a, to_core(there_a)], axis=0)]
    concatenate x3 -> x0, other arithmetic: 1.76 us -> none  [the longest x1 1.72 us: body(): mix_full = jnp.concatenate([mix_here, to_core(mix_here)], axis=0)]
    unnamed x10 -> x6, local copies, waits for them, and re-layouts: 1.66 us -> 0.02 us
  transfers between devices with their start and end apart: 27 -> 30, of which waited for: 9 -> 10; matrix products, arithmetic and copies ran while one was open for 13% -> 0% of each run, Pallas kernels for 11% -> 14%
where the time goes in v3:
time: 73.3 us; the launch traced here: 73.1 us
  starting transfers between devices  35 us (48%)
  waiting for transfers between devices  21.6 us (29%)
  Pallas kernels  16.4 us (22%)
    ppermute x22, starting transfers between devices, to_devices(): return lax.ppermute(value, ('tm', 'head'), pairs)  33.8 us
    ppermute x22, waiting for transfers between devices, to_devices(): return lax.ppermute(value, ('tm', 'head'), pairs)  19.2 us
    pallas_call x2, Pallas kernels, forward(): pl.pallas_call(functools.partial(forward_kernel, first, count, offset, ha...  6.74 us
    pallas_call x2, Pallas kernels, inverse(): pl.pallas_call(functools.partial(inverse_kernel, half, offset), out_shape...  5.01 us
    pallas_call x2, Pallas kernels, mix(): pl.pallas_call(functools.partial(mix_kernel, scale, own_modes, len(arrive...  2.65 us
    ppermute x8, waiting for transfers between devices, to_core(): return lax.ppermute(value, 'head', [(0, 1), (1, 0)])  2.38 us
    pallas_call x1, Pallas kernels, prepare(): pl.pallas_call(prepare_kernel, out_shape=[in_vmem((modes * 2 * size, widt...  1.69 us
  transfers between devices with their start and end apart: 30, of which 10 were waited for; matrix products, arithmetic and copies ran while one was open for 0% of the time, Pallas kernels for 14%

profile of v3, /device:TPU:0, one launch (start us, length us, event | category | flops | bytes accessed | tf_op | source)
XLA Modules:
  0.0 73.1 jit_solution(13624614251219626531)
XLA Ops:
  0.0 3.7 %forward_first.1 = (bf16[4,128,512]{2,1,0:T(8,128)(2,1)S(1)}, f32[4,128,512]{2,1,0:T(8,128)S(1)}, bf16[256,1024]{1,0:T(8,128)(2,1)S(1)}) custom-call(s32[1,128]{1,0:T(1,128)} %bitcast.1, bf16[16,1024,512]{2,1,0:T(8,128)(2,1)} %series_ref.3), custom_call_target="tpu_custom_call" | custom-call | flops 1000 | bytes 1000 | tf_op jit(solution)/shard_map/forward_first/pallas_call | solution.py:110
  3.7 3.0 %collective-permute-start = (bf16[4,128,512]{2,1,0:T(8,128)(2,1)S(1)}, bf16[4,128,512]{2,1,0:T(8,128)(2,1)S(1)}, u32[]{:S(2)}, u32[]{:S(2)}) collective-permute-start(bf16[4,128,512]{2,1,0:T(8,128)(2,1)S(1)} %get-tuple-element.44), channel_id=1, source_target_pairs={{0,2},{1,5},{2,0},{3,7},{4,6},{5,1},{6,4},{7,3},{8,10},{9,13},{10,... | collective-permute-start | bytes 1572872 | tf_op jit(solution)/shard_map/ppermute | solution.py:329
  6.7 3.1 %forward_second.1 = (bf16[4,128,512]{2,1,0:T(8,128)(2,1)S(1)}, f32[4,128,512]{2,1,0:T(8,128)S(1)}) custom-call(bf16[256,1024]{1,0:T(8,128)(2,1)S(1)} %get-tuple-element.38.table_ref.extra_ref, bf16[16,1024,512]{2,1,0:T(8,128)(2,1)} %series_ref.3), custom_call_target="tpu_custom_call" | custom-call | flops 1000 | bytes 1000 | tf_op jit(solution)/shard_map/forward_second/pallas_call | solution.py:110
  10.4 1.7 %prepare_mix.1 = (bf16[1024,128]{1,0:T(8,128)(2,1)S(1)}, bf16[1024,128]{1,0:T(8,128)(2,1)S(1)}, bf16[1024,128]{1,0:T(8,128)(2,1)S(1)}, bf16[1024,128]{1,0:T(8,128)(2,1)S(1)}, bf16[1024,256]{1,0:T(8,128)(2,1)S(1)}) custom-call(f32[8,4,64,128]{3,2,1,0:T(8,128)} %weight_ref.1, bf16[256,1024]{1,0:T(8,128)(2,1)S(1)} %get-tuple-element.38.table_ref.extra_ref), custom_call_target="tpu_custom_call" | custom-call | flops 1000 | bytes 1000 | tf_op jit(solution)/shard_map/prepare_mix/pallas_call | solution.py:182
  12.1 1.7 %collective-permute-done.arrived_ref = bf16[4,128,512]{2,1,0:T(8,128)(2,1)S(1)} collective-permute-done((bf16[4,128,512]{2,1,0:T(8,128)(2,1)S(1)}, bf16[4,128,512]{2,1,0:T(8,128)(2,1)S(1)}, u32[]{:S(2)}, u32[]{:S(2)}) %collective-permute-start) | collective-permute-done | bytes 524320 | tf_op jit(solution)/shard_map/ppermute | solution.py:329
  13.9 2.1 %collective-permute-start.2 = (bf16[4,64,512]{2,1,0:T(8,128)(2,1)S(1)}, bf16[4,64,512]{2,1,0:T(8,128)(2,1)S(1)}, u32[]{:S(2)}, u32[]{:S(2)}) collective-permute-start(bf16[4,64,512]{2,1,0:T(8,128)(2,1)S(1)} %sum_onward.2), channel_id=1, source_target_pairs={{0,4},{1,3},{2,6},{3,1},{4,0},{5,7},{6,2},{7,5},{8,12},{9,11},{10,... | collective-permute-start | bytes 786440 | tf_op jit(solution)/shard_map/ppermute | solution.py:329
  16.0 6.3 %collective-permute-done.1.arrived_ref = bf16[4,128,512]{2,1,0:T(8,128)(2,1)S(1)} collective-permute-done((bf16[4,128,512]{2,1,0:T(8,128)(2,1)S(1)}, bf16[4,128,512]{2,1,0:T(8,128)(2,1)S(1)}, u32[]{:S(2)}, u32[]{:S(2)}) %collective-permute-start.1) | collective-permute-done | bytes 524320 | tf_op jit(solution)/shard_map/ppermute | solution.py:329
  22.3 2.1 %collective-permute-start.3 = (bf16[4,64,512]{2,1,0:T(8,128)(2,1)S(1)}, bf16[4,64,512]{2,1,0:T(8,128)(2,1)S(1)}, u32[]{:S(2)}, u32[]{:S(2)}) collective-permute-start(bf16[4,64,512]{2,1,0:T(8,128)(2,1)S(1)} %sum_onward.3), channel_id=1, source_target_pairs={{0,4},{1,3},{2,6},{3,1},{4,0},{5,7},{6,2},{7,5},{8,12},{9,11},{10,... | collective-permute-start | bytes 786440 | tf_op jit(solution)/shard_map/ppermute | solution.py:329
  25.1 3.7 %collective-permute-start.4 = (bf16[4,16,512]{2,1,0:T(8,128)(2,1)S(1)}, bf16[4,16,512]{2,1,0:T(8,128)(2,1)S(1)}, u32[]{:S(2)}, u32[]{:S(2)}) collective-permute-start(bf16[4,16,512]{2,1,0:T(8,128)(2,1)S(1)} %get-tuple-element.52), channel_id=1, source_target_pairs={{0,24},{1,25},{2,26},{3,27},{4,28},{5,29},{6,30},{7,31},{8,16},{9,... | collective-permute-start | bytes 196616 | tf_op jit(solution)/shard_map/ppermute | solution.py:329
  28.8 2.1 %collective-permute-start.6 = (bf16[4,16,512]{2,1,0:T(8,128)(2,1)S(1)}, bf16[4,16,512]{2,1,0:T(8,128)(2,1)S(1)}, u32[]{:S(2)}, u32[]{:S(2)}) collective-permute-start(bf16[4,16,512]{2,1,0:T(8,128)(2,1)S(1)} %get-tuple-element.54), channel_id=1, source_target_pairs={{0,8},{1,9},{2,10},{3,11},{4,12},{5,13},{6,14},{7,15},{8,0},{9,1},... | collective-permute-start | bytes 196616 | tf_op jit(solution)/shard_map/ppermute | solution.py:329
  31.0 2.5 %collective-permute-start.14 = (bf16[4,16,512]{2,1,0:T(8,128)(2,1)S(1)}, bf16[4,16,512]{2,1,0:T(8,128)(2,1)S(1)}, u32[]{:S(2)}, u32[]{:S(2)}) collective-permute-start(bf16[4,16,512]{2,1,0:T(8,128)(2,1)S(1)} %get-tuple-element.63), channel_id=1, source_target_pairs={{0,24},{1,25},{2,26},{3,27},{4,28},{5,29},{6,30},{7,31},{8,16},{9,... | collective-permute-start | bytes 196616 | tf_op jit(solution)/shard_map/ppermute | solution.py:329
  33.7 1.7 %collective-permute-start.16 = (bf16[4,16,512]{2,1,0:T(8,128)(2,1)S(1)}, bf16[4,16,512]{2,1,0:T(8,128)(2,1)S(1)}, u32[]{:S(2)}, u32[]{:S(2)}) collective-permute-start(bf16[4,16,512]{2,1,0:T(8,128)(2,1)S(1)} %get-tuple-element.65), channel_id=1, source_target_pairs={{0,8},{1,9},{2,10},{3,11},{4,12},{5,13},{6,14},{7,15},{8,0},{9,1},... | collective-permute-start | bytes 196616 | tf_op jit(solution)/shard_map/ppermute | solution.py:329
  38.1 2.5 %collective-permute-start.25 = (bf16[8,16,256]{2,1,0:T(8,128)(2,1)S(1)}, bf16[8,16,256]{2,1,0:T(8,128)(2,1)S(1)}, u32[]{:S(2)}, u32[]{:S(2)}) collective-permute-start(bf16[8,16,256]{2,1,0:T(8,128)(2,1)S(1)} %constant_dynamic-update-slice_fusion.refs_0_), channel_id=1, source_target_pairs={{0,24},{1,25},{2,26},{3,27},{4,28},{5,29},{6,30},{7,31},{8,16},{9,... | collective-permute-start | bytes 196616 | tf_op jit(solution)/shard_map/ppermute | solution.py:329
  40.5 1.9 %collective-permute-start.23 = (bf16[8,16,256]{2,1,0:T(8,128)(2,1)S(1)}, bf16[8,16,256]{2,1,0:T(8,128)(2,1)S(1)}, u32[]{:S(2)}, u32[]{:S(2)}) collective-permute-start(bf16[8,16,256]{2,1,0:T(8,128)(2,1)S(1)} %constant_dynamic-update-slice_fusion.refs_0_), channel_id=1, source_target_pairs={{0,8},{1,9},{2,10},{3,11},{4,12},{5,13},{6,14},{7,15},{8,0},{9,1},... | collective-permute-start | bytes 196616 | tf_op jit(solution)/shard_map/ppermute | solution.py:329
  45.1 2.5 %collective-permute-start.20 = (bf16[8,16,256]{2,1,0:T(8,128)(2,1)S(1)}, bf16[8,16,256]{2,1,0:T(8,128)(2,1)S(1)}, u32[]{:S(2)}, u32[]{:S(2)}) collective-permute-start(bf16[8,16,256]{2,1,0:T(8,128)(2,1)S(1)} %constant_dynamic-update-slice_fusion.2.refs_0_), channel_id=1, source_target_pairs={{0,24},{1,25},{2,26},{3,27},{4,28},{5,29},{6,30},{7,31},{8,16},{9,... | collective-permute-start | bytes 196616 | tf_op jit(solution)/shard_map/ppermute | solution.py:329
  47.6 1.9 %collective-permute-start.18 = (bf16[8,16,256]{2,1,0:T(8,128)(2,1)S(1)}, bf16[8,16,256]{2,1,0:T(8,128)(2,1)S(1)}, u32[]{:S(2)}, u32[]{:S(2)}) collective-permute-start(bf16[8,16,256]{2,1,0:T(8,128)(2,1)S(1)} %constant_dynamic-update-slice_fusion.2.refs_0_), channel_id=1, source_target_pairs={{0,8},{1,9},{2,10},{3,11},{4,12},{5,13},{6,14},{7,15},{8,0},{9,1},... | collective-permute-start | bytes 196616 | tf_op jit(solution)/shard_map/ppermute | solution.py:329
  49.5 1.6 %collective-permute-start.28 = (bf16[8,64,256]{2,1,0:T(8,128)(2,1)S(1)}, bf16[8,64,256]{2,1,0:T(8,128)(2,1)S(1)}, u32[]{:S(2)}, u32[]{:S(2)}) collective-permute-start(bf16[8,64,256]{2,1,0:T(8,128)(2,1)S(1)} %join_rows.3.refs_0_), channel_id=1, source_target_pairs={{0,4},{1,3},{2,6},{3,1},{4,0},{5,7},{6,2},{7,5},{8,12},{9,11},{10,... | collective-permute-start | bytes 786440 | tf_op jit(solution)/shard_map/ppermute | solution.py:329
  51.1 1.5 %collective-permute-start.26 = (bf16[8,64,256]{2,1,0:T(8,128)(2,1)S(1)}, bf16[8,64,256]{2,1,0:T(8,128)(2,1)S(1)}, u32[]{:S(2)}, u32[]{:S(2)}) collective-permute-start(bf16[8,64,256]{2,1,0:T(8,128)(2,1)S(1)} %join_rows.3.refs_0_), channel_id=1, source_target_pairs={{0,2},{1,5},{2,0},{3,7},{4,6},{5,1},{6,4},{7,3},{8,10},{9,13},{10,... | collective-permute-start | bytes 786440 | tf_op jit(solution)/shard_map/ppermute | solution.py:329
  53.9 1.6 %collective-permute-start.21 = (bf16[8,64,256]{2,1,0:T(8,128)(2,1)S(1)}, bf16[8,64,256]{2,1,0:T(8,128)(2,1)S(1)}, u32[]{:S(2)}, u32[]{:S(2)}) collective-permute-start(bf16[8,64,256]{2,1,0:T(8,128)(2,1)S(1)} %join_rows.2.refs_0_), channel_id=1, source_target_pairs={{0,4},{1,3},{2,6},{3,1},{4,0},{5,7},{6,2},{7,5},{8,12},{9,11},{10,... | collective-permute-start | bytes 786440 | tf_op jit(solution)/shard_map/ppermute | solution.py:329
  56.9 1.7 %collective-permute-done.28.refs_1_ = bf16[8,64,256]{2,1,0:T(8,128)(2,1)S(1)} collective-permute-done((bf16[8,64,256]{2,1,0:T(8,128)(2,1)S(1)}, bf16[8,64,256]{2,1,0:T(8,128)(2,1)S(1)}, u32[]{:S(2)}, u32[]{:S(2)}) %collective-permute-start.28) | collective-permute-done | bytes 262176 | tf_op jit(solution)/shard_map/ppermute | solution.py:329
  59.3 4.9 %collective-permute-done.21.refs_1_ = bf16[8,64,256]{2,1,0:T(8,128)(2,1)S(1)} collective-permute-done((bf16[8,64,256]{2,1,0:T(8,128)(2,1)S(1)}, bf16[8,64,256]{2,1,0:T(8,128)(2,1)S(1)}, u32[]{:S(2)}, u32[]{:S(2)}) %collective-permute-start.21) | collective-permute-done | bytes 262176 | tf_op jit(solution)/shard_map/ppermute | solution.py:329
  65.9 2.5 %inverse_first.1.refs_4_ = bf16[16,1024,256]{2,1,0:T(8,128)(2,1)} custom-call(bf16[1024,256]{1,0:T(8,128)(2,1)S(1)} %get-tuple-element.39.table_ref, bf16[8,64,256]{2,1,0:T(8,128)(2,1)S(1)} %join_rows.3.refs_0_, bf16[8,64,256]{2,1,0:T(8,128)(2,1)S(1)} %collective-permute-done.28.refs_1_, bf16[8,64,256]{2,1,0:T(8,128)(2,1)S(1)} %collective-permute-done.26.refs_2_, ...), custom_call_target="tpu_custom_call" | custom-call | flops 1000 | bytes 1000 | tf_op jit(solution)/shard_map/inverse_first/pallas_call | solution.py:314
  68.4 2.2 %collective-permute-done.27.refs_3_ = bf16[8,64,256]{2,1,0:T(8,128)(2,1)S(1)} collective-permute-done((bf16[8,64,256]{2,1,0:T(8,128)(2,1)S(1)}, bf16[8,64,256]{2,1,0:T(8,128)(2,1)S(1)}, u32[]{:S(2)}, u32[]{:S(2)}) %collective-permute-start.27) | collective-permute-done | bytes 262176 | tf_op jit(solution)/shard_map/ppermute | solution.py:329
  70.6 2.5 %inverse_second.1 = bf16[16,1024,256]{2,1,0:T(8,128)(2,1)} custom-call(bf16[1024,256]{1,0:T(8,128)(2,1)S(1)} %get-tuple-element.39.table_ref, bf16[8,64,256]{2,1,0:T(8,128)(2,1)S(1)} %join_rows.2.refs_0_, bf16[8,64,256]{2,1,0:T(8,128)(2,1)S(1)} %collective-permute-done.21.refs_1_, ...), custom_call_target="tpu_custom_call", output_to_operand_aliasing={{}: (5, {})} | custom-call | flops 1000 | bytes 1000 | tf_op jit(solution)/shard_map/inverse_second/pallas_call | solution.py:314
  (57 shorter events, 12.0 us)
Async XLA Ops:
  3.7 10.2 %collective-permute-start = (bf16[4,128,512]{2,1,0:T(8,128)(2,1)S(1)}, bf16[4,128,512]{2,1,0:T(8,128)(2,1)S(1)}, u32[]{:S(2)}, u32[]{:S(2)}) collective-permute-start(bf16[4,128,512]{2,1,0:T(8,128)(2,1)S(1)} %get-tuple-element.44), channel_id=1, source_target_pairs={{0,2},{1,5},{2,0},{3,7},{4,6},{5,1},{6,4},{7,3},{8,10},{9,13},{10,... | collective-permute-start | bytes 1572872 | tf_op jit(solution)/shard_map/ppermute | solution.py:329
  9.8 12.5 %collective-permute-start.1 = (bf16[4,128,512]{2,1,0:T(8,128)(2,1)S(1)}, bf16[4,128,512]{2,1,0:T(8,128)(2,1)S(1)}, u32[]{:S(2)}, u32[]{:S(2)}) collective-permute-start(bf16[4,128,512]{2,1,0:T(8,128)(2,1)S(1)} %get-tuple-element.46), channel_id=1, source_target_pairs={{0,2},{1,5},{2,0},{3,7},{4,6},{5,1},{6,4},{7,3},{8,10},{9,13},{10,... | collective-permute-start | bytes 1572872 | tf_op jit(solution)/shard_map/ppermute | solution.py:329
  9.9 12.5 %collective-permute-start.7 = (bf16[512,256]{1,0:T(8,128)(2,1)S(1)}, bf16[512,256]{1,0:T(8,128)(2,1)S(1)}, u32[]{:S(2)}, u32[]{:S(2)}) collective-permute-start(bf16[512,256]{1,0:T(8,128)(2,1)S(1)} %copy-done), channel_id=1, source_target_pairs={{0,1},{1,0},{2,3},{3,2},{4,5},{5,4},{6,7},{7,6},{8,9},{9,8},{10,11... | collective-permute-start | bytes 786440 | tf_op jit(solution)/shard_map/ppermute | solution.py:336
  9.9 14.5 %collective-permute-start.8 = (bf16[512,256]{1,0:T(8,128)(2,1)S(1)}, bf16[512,256]{1,0:T(8,128)(2,1)S(1)}, u32[]{:S(2)}, u32[]{:S(2)}) collective-permute-start(bf16[512,256]{1,0:T(8,128)(2,1)S(1)} %copy-done.1), channel_id=1, source_target_pairs={{0,1},{1,0},{2,3},{3,2},{4,5},{5,4},{6,7},{7,6},{8,9},{9,8},{10,11... | collective-permute-start | bytes 786440 | tf_op jit(solution)/shard_map/ppermute | solution.py:336
  13.9 10.8 %collective-permute-start.2 = (bf16[4,64,512]{2,1,0:T(8,128)(2,1)S(1)}, bf16[4,64,512]{2,1,0:T(8,128)(2,1)S(1)}, u32[]{:S(2)}, u32[]{:S(2)}) collective-permute-start(bf16[4,64,512]{2,1,0:T(8,128)(2,1)S(1)} %sum_onward.2), channel_id=1, source_target_pairs={{0,4},{1,3},{2,6},{3,1},{4,0},{5,7},{6,2},{7,5},{8,12},{9,11},{10,... | collective-permute-start | bytes 786440 | tf_op jit(solution)/shard_map/ppermute | solution.py:329
  16.0 9.0 %collective-permute-start.10 = (bf16[1024,128]{1,0:T(8,128)(2,1)S(1)}, bf16[1024,128]{1,0:T(8,128)(2,1)S(1)}, u32[]{:S(2)}, u32[]{:S(2)}) collective-permute-start(bf16[1024,128]{1,0:T(8,128)(2,1)S(1)} %get-tuple-element.57.refs_8_), channel_id=1, source_target_pairs={{0,1},{1,0},{2,3},{3,2},{4,5},{5,4},{6,7},{7,6},{8,9},{9,8},{10,11... | collective-permute-start | bytes 786440 | tf_op jit(solution)/shard_map/ppermute | solution.py:336
  22.3 6.5 %collective-permute-start.3 = (bf16[4,64,512]{2,1,0:T(8,128)(2,1)S(1)}, bf16[4,64,512]{2,1,0:T(8,128)(2,1)S(1)}, u32[]{:S(2)}, u32[]{:S(2)}) collective-permute-start(bf16[4,64,512]{2,1,0:T(8,128)(2,1)S(1)} %sum_onward.3), channel_id=1, source_target_pairs={{0,4},{1,3},{2,6},{3,1},{4,0},{5,7},{6,2},{7,5},{8,12},{9,11},{10,... | collective-permute-start | bytes 786440 | tf_op jit(solution)/shard_map/ppermute | solution.py:329
  24.5 6.5 %collective-permute-start.12 = (bf16[1024,128]{1,0:T(8,128)(2,1)S(1)}, bf16[1024,128]{1,0:T(8,128)(2,1)S(1)}, u32[]{:S(2)}, u32[]{:S(2)}) collective-permute-start(bf16[1024,128]{1,0:T(8,128)(2,1)S(1)} %get-tuple-element.59.refs_10_), channel_id=1, source_target_pairs={{0,1},{1,0},{2,3},{3,2},{4,5},{5,4},{6,7},{7,6},{8,9},{9,8},{10,11... | collective-permute-start | bytes 786440 | tf_op jit(solution)/shard_map/ppermute | solution.py:336
  24.7 8.9 %collective-permute-start.9 = (bf16[1024,128]{1,0:T(8,128)(2,1)S(1)}, bf16[1024,128]{1,0:T(8,128)(2,1)S(1)}, u32[]{:S(2)}, u32[]{:S(2)}) collective-permute-start(bf16[1024,128]{1,0:T(8,128)(2,1)S(1)} %get-tuple-element.42.refs_7_), channel_id=1, source_target_pairs={{0,1},{1,0},{2,3},{3,2},{4,5},{5,4},{6,7},{7,6},{8,9},{9,8},{10,11... | collective-permute-start | bytes 786440 | tf_op jit(solution)/shard_map/ppermute | solution.py:336
  25.1 8.7 %collective-permute-start.4 = (bf16[4,16,512]{2,1,0:T(8,128)(2,1)S(1)}, bf16[4,16,512]{2,1,0:T(8,128)(2,1)S(1)}, u32[]{:S(2)}, u32[]{:S(2)}) collective-permute-start(bf16[4,16,512]{2,1,0:T(8,128)(2,1)S(1)} %get-tuple-element.52), channel_id=1, source_target_pairs={{0,24},{1,25},{2,26},{3,27},{4,28},{5,29},{6,30},{7,31},{8,16},{9,... | collective-permute-start | bytes 196616 | tf_op jit(solution)/shard_map/ppermute | solution.py:329
  28.7 6.7 %collective-permute-start.5 = (bf16[4,16,512]{2,1,0:T(8,128)(2,1)S(1)}, bf16[4,16,512]{2,1,0:T(8,128)(2,1)S(1)}, u32[]{:S(2)}, u32[]{:S(2)}) collective-permute-start(bf16[4,16,512]{2,1,0:T(8,128)(2,1)S(1)} %get-tuple-element.53), channel_id=1, source_target_pairs={{0,16},{1,17},{2,18},{3,19},{4,20},{5,21},{6,22},{7,23},{8,24},{9,... | collective-permute-start | bytes 196616 | tf_op jit(solution)/shard_map/ppermute | solution.py:329
  28.8 6.6 %collective-permute-start.6 = (bf16[4,16,512]{2,1,0:T(8,128)(2,1)S(1)}, bf16[4,16,512]{2,1,0:T(8,128)(2,1)S(1)}, u32[]{:S(2)}, u32[]{:S(2)}) collective-permute-start(bf16[4,16,512]{2,1,0:T(8,128)(2,1)S(1)} %get-tuple-element.54), channel_id=1, source_target_pairs={{0,8},{1,9},{2,10},{3,11},{4,12},{5,13},{6,14},{7,15},{8,0},{9,1},... | collective-permute-start | bytes 196616 | tf_op jit(solution)/shard_map/ppermute | solution.py:329
  31.0 9.6 %collective-permute-start.14 = (bf16[4,16,512]{2,1,0:T(8,128)(2,1)S(1)}, bf16[4,16,512]{2,1,0:T(8,128)(2,1)S(1)}, u32[]{:S(2)}, u32[]{:S(2)}) collective-permute-start(bf16[4,16,512]{2,1,0:T(8,128)(2,1)S(1)} %get-tuple-element.63), channel_id=1, source_target_pairs={{0,24},{1,25},{2,26},{3,27},{4,28},{5,29},{6,30},{7,31},{8,16},{9,... | collective-permute-start | bytes 196616 | tf_op jit(solution)/shard_map/ppermute | solution.py:329
  33.5 8.9 %collective-permute-start.15 = (bf16[4,16,512]{2,1,0:T(8,128)(2,1)S(1)}, bf16[4,16,512]{2,1,0:T(8,128)(2,1)S(1)}, u32[]{:S(2)}, u32[]{:S(2)}) collective-permute-start(bf16[4,16,512]{2,1,0:T(8,128)(2,1)S(1)} %get-tuple-element.64), channel_id=1, source_target_pairs={{0,16},{1,17},{2,18},{3,19},{4,20},{5,21},{6,22},{7,23},{8,24},{9,... | collective-permute-start | bytes 196616 | tf_op jit(solution)/shard_map/ppermute | solution.py:329
  33.7 8.7 %collective-permute-start.16 = (bf16[4,16,512]{2,1,0:T(8,128)(2,1)S(1)}, bf16[4,16,512]{2,1,0:T(8,128)(2,1)S(1)}, u32[]{:S(2)}, u32[]{:S(2)}) collective-permute-start(bf16[4,16,512]{2,1,0:T(8,128)(2,1)S(1)} %get-tuple-element.65), channel_id=1, source_target_pairs={{0,8},{1,9},{2,10},{3,11},{4,12},{5,13},{6,14},{7,15},{8,0},{9,1},... | collective-permute-start | bytes 196616 | tf_op jit(solution)/shard_map/ppermute | solution.py:329
  38.1 9.5 %collective-permute-start.25 = (bf16[8,16,256]{2,1,0:T(8,128)(2,1)S(1)}, bf16[8,16,256]{2,1,0:T(8,128)(2,1)S(1)}, u32[]{:S(2)}, u32[]{:S(2)}) collective-permute-start(bf16[8,16,256]{2,1,0:T(8,128)(2,1)S(1)} %constant_dynamic-update-slice_fusion.refs_0_), channel_id=1, source_target_pairs={{0,24},{1,25},{2,26},{3,27},{4,28},{5,29},{6,30},{7,31},{8,16},{9,... | collective-permute-start | bytes 196616 | tf_op jit(solution)/shard_map/ppermute | solution.py:329
  40.5 8.9 %collective-permute-start.24 = (bf16[8,16,256]{2,1,0:T(8,128)(2,1)S(1)}, bf16[8,16,256]{2,1,0:T(8,128)(2,1)S(1)}, u32[]{:S(2)}, u32[]{:S(2)}) collective-permute-start(bf16[8,16,256]{2,1,0:T(8,128)(2,1)S(1)} %constant_dynamic-update-slice_fusion.refs_0_), channel_id=1, source_target_pairs={{0,16},{1,17},{2,18},{3,19},{4,20},{5,21},{6,22},{7,23},{8,24},{9,... | collective-permute-start | bytes 196616 | tf_op jit(solution)/shard_map/ppermute | solution.py:329
  40.5 8.9 %collective-permute-start.23 = (bf16[8,16,256]{2,1,0:T(8,128)(2,1)S(1)}, bf16[8,16,256]{2,1,0:T(8,128)(2,1)S(1)}, u32[]{:S(2)}, u32[]{:S(2)}) collective-permute-start(bf16[8,16,256]{2,1,0:T(8,128)(2,1)S(1)} %constant_dynamic-update-slice_fusion.refs_0_), channel_id=1, source_target_pairs={{0,8},{1,9},{2,10},{3,11},{4,12},{5,13},{6,14},{7,15},{8,0},{9,1},... | collective-permute-start | bytes 196616 | tf_op jit(solution)/shard_map/ppermute | solution.py:329
  45.1 7.5 %collective-permute-start.20 = (bf16[8,16,256]{2,1,0:T(8,128)(2,1)S(1)}, bf16[8,16,256]{2,1,0:T(8,128)(2,1)S(1)}, u32[]{:S(2)}, u32[]{:S(2)}) collective-permute-start(bf16[8,16,256]{2,1,0:T(8,128)(2,1)S(1)} %constant_dynamic-update-slice_fusion.2.refs_0_), channel_id=1, source_target_pairs={{0,24},{1,25},{2,26},{3,27},{4,28},{5,29},{6,30},{7,31},{8,16},{9,... | collective-permute-start | bytes 196616 | tf_op jit(solution)/shard_map/ppermute | solution.py:329
  49.5 9.2 %collective-permute-start.28 = (bf16[8,64,256]{2,1,0:T(8,128)(2,1)S(1)}, bf16[8,64,256]{2,1,0:T(8,128)(2,1)S(1)}, u32[]{:S(2)}, u32[]{:S(2)}) collective-permute-start(bf16[8,64,256]{2,1,0:T(8,128)(2,1)S(1)} %join_rows.3.refs_0_), channel_id=1, source_target_pairs={{0,4},{1,3},{2,6},{3,1},{4,0},{5,7},{6,2},{7,5},{8,12},{9,11},{10,... | collective-permute-start | bytes 786440 | tf_op jit(solution)/shard_map/ppermute | solution.py:329
  51.1 8.2 %collective-permute-start.26 = (bf16[8,64,256]{2,1,0:T(8,128)(2,1)S(1)}, bf16[8,64,256]{2,1,0:T(8,128)(2,1)S(1)}, u32[]{:S(2)}, u32[]{:S(2)}) collective-permute-start(bf16[8,64,256]{2,1,0:T(8,128)(2,1)S(1)} %join_rows.3.refs_0_), channel_id=1, source_target_pairs={{0,2},{1,5},{2,0},{3,7},{4,6},{5,1},{6,4},{7,3},{8,10},{9,13},{10,... | collective-permute-start | bytes 786440 | tf_op jit(solution)/shard_map/ppermute | solution.py:329
  53.9 10.4 %collective-permute-start.21 = (bf16[8,64,256]{2,1,0:T(8,128)(2,1)S(1)}, bf16[8,64,256]{2,1,0:T(8,128)(2,1)S(1)}, u32[]{:S(2)}, u32[]{:S(2)}) collective-permute-start(bf16[8,64,256]{2,1,0:T(8,128)(2,1)S(1)} %join_rows.2.refs_0_), channel_id=1, source_target_pairs={{0,4},{1,3},{2,6},{3,1},{4,0},{5,7},{6,2},{7,5},{8,12},{9,11},{10,... | collective-permute-start | bytes 786440 | tf_op jit(solution)/shard_map/ppermute | solution.py:329
  55.5 12.9 %collective-permute-start.22 = (bf16[8,64,256]{2,1,0:T(8,128)(2,1)S(1)}, bf16[8,64,256]{2,1,0:T(8,128)(2,1)S(1)}, u32[]{:S(2)}, u32[]{:S(2)}) collective-permute-start(bf16[8,64,256]{2,1,0:T(8,128)(2,1)S(1)} %join_rows.2.refs_0_), channel_id=1, source_target_pairs={{0,2},{1,5},{2,0},{3,7},{4,6},{5,1},{6,4},{7,3},{8,10},{9,13},{10,... | collective-permute-start | bytes 786440 | tf_op jit(solution)/shard_map/ppermute | solution.py:329
  58.6 7.2 %collective-permute-start.29 = (bf16[8,64,256]{2,1,0:T(8,128)(2,1)S(1)}, bf16[8,64,256]{2,1,0:T(8,128)(2,1)S(1)}, u32[]{:S(2)}, u32[]{:S(2)}) collective-permute-start(bf16[8,64,256]{2,1,0:T(8,128)(2,1)S(1)} %collective-permute-done.28.refs_1_), channel_id=1, source_target_pairs={{0,2},{1,5},{2,0},{3,7},{4,6},{5,1},{6,4},{7,3},{8,10},{9,13},{10,... | collective-permute-start | bytes 786440 | tf_op jit(solution)/shard_map/ppermute | solution.py:329
  (8 other events, 34.4 us)

commit v4 on v3

--- a/solution.py
+++ b/solution.py
@@ -11,6 +11,9 @@
 f32 = jnp.float32
 bf16 = jnp.bfloat16
 two_pi = 2.0 * math.pi
+
+
+ahead = pl.CostEstimate(flops=3 * 10**9, bytes_accessed=1000, transcendentals=0)
 
 
 def in_vmem(shape, dtype):
@@ -83,7 +86,7 @@
     if first:
         send_ref, keep_ref, table_ref, held, sems = refs
     else:
-        send_ref, keep_ref, held, sems = refs
+        corner_ref, side_ref, keep_ref, held, sems = refs
         table_ref = extra_ref
     base = lax.axis_index("head") * half + offset
     copies = [pltpu.make_async_copy(series_ref.at[base + b], held.at[b], sems.at[b]) for b in range(count)]
@@ -95,13 +98,18 @@
     for b in range(count):
         copies[b].wait()
         part = jnp.dot(table_ref[...], held[b], preferred_element_type=f32)
-        send_ref[b] = part[middle:].astype(bf16)
+        if first:
+            send_ref[b] = part[middle:].astype(bf16)
+        else:
+            side_ref[b] = part[middle:middle + middle // 2].astype(bf16)
+            corner_ref[b] = part[middle + middle // 2:].astype(bf16)
         keep_ref[b] = part[:middle]
 
 
 def forward(first, series, extra, count, offset, half, own_modes, series_length, rows):
     _, time_count, width = series.shape
-    outs = [in_vmem((count, rows // 2, width), bf16), in_vmem((count, rows // 2, width), f32)]
+    sends = [in_vmem((count, rows // 2, width), bf16)] if first else [in_vmem((count, rows // 4, width), bf16)] * 2
+    outs = sends + [in_vmem((count, rows // 2, width), f32)]
     if first:
         outs.append(in_vmem((rows, time_count), bf16))
         extra = in_hbm(extra)
@@ -121,10 +129,10 @@
 
 def onward_kernel(keep_ref, arrived_ref, out_ref):
     middle = keep_ref.shape[1] // 2
-    out_ref[...] = (keep_ref[:, middle:] + arrived_ref[:, middle:].astype(f32)).astype(bf16)
-
-
-def onward(keep, arrived):
+    out_ref[...] = (keep_ref[:, middle:] + arrived_ref[:, -middle:].astype(f32)).astype(bf16)
+
+
+def onward(keep, arrived, cost=small):
     count, rows, width = keep.shape
     return pl.pallas_call(
         onward_kernel,
@@ -132,7 +140,7 @@
         in_specs=[whole] * 2,
         out_specs=whole,
         compiler_params=pltpu.CompilerParams(vmem_limit_bytes=16 * 2**20),
-        cost_estimate=small,
+        cost_estimate=cost,
         name="sum_onward",
     )(*held(keep, arrived))
 
@@ -164,31 +172,55 @@
     return parts[0], parts[1:]
 
 
-def prepare_kernel(weight_ref, table_ref, *out_refs):
+mix_arrays = 2
+
+
+def prepare_kernel(weight_ref, query_ref, out_weight_ref, table_ref, *refs):
     modes, heads, size, width = weight_ref.shape
     negative = lax.broadcasted_iota(jnp.int32, (size, width), 1) < size
-    for m in range(modes):
-        for h in range(heads):
+    for h in range(heads):
+        out_ref = refs[h * mix_arrays // heads]
+        start = h % (heads // mix_arrays) * modes * 2 * size
+        for m in range(modes):
             weight = weight_ref[m, h]
             turned = pltpu.roll(weight, size, 1)
-            start = 2 * size * m
-            out_refs[h][start:start + size] = weight.astype(bf16)
-            out_refs[h][start + size:start + 2 * size] = jnp.where(negative, -turned, turned).astype(bf16)
-    out_refs[heads][...] = table_ref[...].T
-
-
-def prepare(weight, table):
+            out_ref[start:start + size] = weight.astype(bf16)
+            out_ref[start + size:start + 2 * size] = jnp.where(negative, -turned, turned).astype(bf16)
+            start += 2 * size
+    out_ref, back_ref = refs[mix_arrays:]
+    start = 0
+    for ref in (query_ref, out_weight_ref):
+        depth, columns = ref.shape
+        for first in range(0, columns, width):
+            out_ref[start:start + depth] = ref[:, first:first + width]
+            start += depth
+    back_ref[...] = table_ref[...].T
+
+
+def prepare(weight, query, out_weight, table):
     modes, heads, size, width = weight.shape
+    mixes = in_vmem((modes * heads // mix_arrays * 2 * size, width), bf16)
     outs = pl.pallas_call(
         prepare_kernel,
-        out_shape=[in_vmem((modes * 2 * size, width), bf16)] * heads + [in_vmem(table.shape[::-1], bf16)],
-        in_specs=[whole] * 2,
-        out_specs=[whole] * (heads + 1),
+        out_shape=[mixes] * mix_arrays + [in_vmem((2 * query.size // width, width), bf16), in_vmem(table.shape[::-1], bf16)],
+        in_specs=[whole] * 4,
+        out_specs=[whole] * (mix_arrays + 2),
         compiler_params=pltpu.CompilerParams(vmem_limit_bytes=16 * 2**20),
         cost_estimate=small,
-        name="prepare_mix",
-    )(in_hbm(weight), *held(table))
-    return outs[:heads], outs[heads]
+        name="prepare_weights",
+    )(in_hbm(weight), in_hbm(query), in_hbm(out_weight), *held(table))
+    return outs[:-1], outs[-1]
+
+
+def packed_parts(packed, heads, depth):
+    weights = packed[-1][...]
+    mixes = []
+    for array in packed[:-1]:
+        step = array.shape[0] * mix_arrays // heads
+        mixes += [array[start:start + step] for start in range(0, array.shape[0], step)]
+    columns = [weights[start:start + depth] for start in range(0, weights.shape[0], depth)]
+    middle = len(columns) // 2
+    return mixes, jnp.concatenate(columns[:middle], axis=1), jnp.concatenate(columns[middle:], axis=1)
 
 
 def split_rows(value):
@@ -204,8 +236,8 @@
 
 def mix_kernel(scale, own_modes, arrivals, own_ref, *refs):
     arrived = refs[:arrivals]
-    query_refs, out_weight_refs, mix_refs = refs[arrivals:arrivals + 2], refs[arrivals + 2:arrivals + 4], refs[arrivals + 4:-2]
-    here_ref, there_ref = refs[-2:]
+    packed_refs, (here_ref, there_ref) = refs[arrivals:-2], refs[-2:]
+    each = len(packed_refs) // 2
     total = own_ref[...]
     for ref in arrived:
         total = total + ref[...].astype(f32)
@@ -219,9 +251,11 @@
     ))
     lower = lax.broadcasted_iota(jnp.int32, (rows, 128), 1) < 64
     row_mode = lax.broadcasted_iota(jnp.int32, (2 * rows, 128), 0) % own_modes
-    mixed = []
-    for group, query_ref in enumerate(query_refs):
-        queries = fold_rows(jnp.dot(pieces, query_ref[...], preferred_element_type=f32))
+    mixed, out_weights = [], []
+    for packed in (packed_refs[:each], packed_refs[each:]):
+        mixes, query, out_weight = packed_parts(packed, half // 64, width)
+        out_weights.append(out_weight)
+        queries = fold_rows(jnp.dot(pieces, query, preferred_element_type=f32))
         mixed_real, mixed_imag = [], []
         for pair in range(half // 128):
             columns = slice(pair * 128, pair * 128 + 128)
@@ -235,8 +269,7 @@
                 spread = split_rows(both[which])
                 zero = jnp.zeros_like(spread)
                 spread = jnp.concatenate([jnp.where(row_mode == k, spread, zero) for k in range(own_modes)], axis=1)
-                mix_ref = mix_refs[group * (half // 64) + 2 * pair + which]
-                heads.append(fold_rows(jnp.dot(spread, mix_ref[...], preferred_element_type=f32)))
+                heads.append(fold_rows(jnp.dot(spread, mixes[2 * pair + which], preferred_element_type=f32)))
             mixed_real.append(jnp.where(lower, heads[0], pltpu.roll(heads[1], 64, 1)))
             mixed_imag.append(jnp.where(lower, pltpu.roll(heads[0], 64, 1), heads[1]))
         both = jnp.concatenate([jnp.concatenate(mixed_real, axis=1), jnp.concatenate(mixed_imag, axis=1)], axis=0)
@@ -244,14 +277,14 @@
     first = jnp.where(core == 0, mixed[0], mixed[1])
     second = jnp.where(core == 0, mixed[1], mixed[0])
     both = jnp.concatenate([first, second], axis=1)
-    for weight_ref, out_ref in zip(out_weight_refs, (here_ref, there_ref)):
-        result = fold_rows(jnp.dot(both, weight_ref[...], preferred_element_type=f32)).astype(bf16)
+    for out_weight, out_ref in zip(out_weights, (here_ref, there_ref)):
+        result = fold_rows(jnp.dot(both, out_weight, preferred_element_type=f32)).astype(bf16)
         out_ref[...] = jnp.concatenate(
             [result[:rows].reshape(count, own_modes, half), result[rows:].reshape(count, own_modes, half)], axis=1
         )
 
 
-def mix(own, arrived, queries, outs, mixes, scale, own_modes):
+def mix(own, arrived, packed, scale, own_modes):
     count, block_rows, width = own.shape
     here = width // 2
     if own_modes % 8 == 0:
@@ -259,29 +292,29 @@
         return pl.pallas_call(
             functools.partial(mix_kernel, scale, own_modes, len(arrived)),
             out_shape=[shape, shape],
-            in_specs=[whole] * (5 + len(arrived) + len(mixes)),
+            in_specs=[whole] * (1 + len(arrived) + 2 * len(packed[0])),
             out_specs=[whole, whole],
             compiler_params=pltpu.CompilerParams(vmem_limit_bytes=16 * 2**20),
             cost_estimate=small,
             name="mix_modes",
-        )(*held(own, *arrived, *queries, *outs, *mixes))
+        )(*held(own, *arrived, *packed[0], *packed[1]))
     core = lax.axis_index("head")
     highest = lax.Precision.HIGHEST
     total = (own + sum(piece.astype(f32) for piece in arrived)) * scale
-    mixed = []
-    heads = len(mixes) // 2
-    for group, query in enumerate(queries):
-        weights = jnp.stack(mixes[group * heads:(group + 1) * heads])
+    heads = here // 64
+    mixed, results = [], []
+    for side in packed:
+        mixes, query, _ = packed_parts(side, heads, width)
         projected = jnp.einsum("brf,fg->brg", total, query.astype(f32), precision=highest)
         projected = projected.reshape(count, 2, own_modes, heads, 64)
-        weights = weights.reshape(heads, own_modes, 2, 64, 2, 64).astype(f32)
+        weights = jnp.stack(mixes).reshape(heads, own_modes, 2, 64, 2, 64).astype(f32)
         part = jnp.einsum("brmhi,hmriso->bsmho", projected, weights, precision=highest)
         mixed.append(part.reshape(count, block_rows, here))
     mixed = jnp.concatenate(mixed, axis=2)
-    results = []
-    for out_weight in outs:
-        rolled = jnp.where(core == 0, out_weight, jnp.roll(out_weight, here, axis=0)).astype(f32)
-        results.append(jnp.einsum("brf,fg->brg", mixed, rolled, precision=highest).astype(bf16))
+    mixed = jnp.where(core == 0, mixed, jnp.roll(mixed, here, axis=2))
+    for side in packed:
+        out_weight = packed_parts(side, heads, width)[2].astype(f32)
+        results.append(jnp.einsum("brf,fg->brg", mixed, out_weight, precision=highest).astype(bf16))
     return results
 
 
@@ -378,29 +411,28 @@
     send_a, keep_a, table = forward(
         True, series, modes[None, :], count_a, 0, half, own_modes, series_length, rows
     )
-    send_b, keep_b = forward(False, series, table, count_b, count_a, half, own_modes, series_length, rows)
+    corner_b, side_b, keep_b = forward(False, series, table, count_b, count_a, half, own_modes, series_length, rows)
     block_rows = 2 * own_modes
     scale = 1.0 / math.sqrt(series_length * mode_total)
     arrived_a = to_devices(send_a, going_first, size)
-    arrived_b = to_devices(send_b, going_first, size)
-
-    mix_here, table_back = prepare(mix_weight, table)
-    query_weight, out_weight = after(query_weight, table), after(out_weight, table)
-    weights = [[query_weight, to_core(query_weight)], [out_weight, to_core(out_weight)]]
-    weights.append([*mix_here, *(to_core(w) for w in mix_here)])
-
-    onward_a = onward(after(keep_a, keep_b, mix_here[0]), arrived_a)
+    corner_b = to_devices(corner_b, going_first, size)
+
+    packed, table_back = prepare(after(mix_weight, keep_b), query_weight, out_weight, table)
+    packed = [packed, [to_core(array) for array in packed]]
+
+    onward_a = onward(after(keep_a, keep_b, *packed[0]), arrived_a)
     second_a = to_devices(onward_a, going_second, size)
-    onward_b = onward(after(keep_b, onward_a), arrived_b)
+    onward_b = onward(after(keep_b, onward_a), corner_b, ahead)
     second_b = to_devices(onward_b, going_second, size)
-    own_a, far_a = total_rows(after(keep_a, onward_b), arrived_a, second_a, block_rows)
+    side_b = to_devices(after(side_b, onward_b), going_first, size)
+    own_a, far_a = total_rows(after(keep_a, onward_b, *packed[1]), arrived_a, second_a, block_rows)
     far_a = send_far(far_a, size)
-    own_b, far_b = total_rows(after(keep_b, own_a), arrived_b, second_b, block_rows)
+    own_b, far_b = total_rows(after(keep_b, own_a), side_b, second_b, block_rows)
     far_b = send_far(far_b, size)
 
-    here_a, there_a = mix(after(own_a, own_b), far_a, *weights, scale, own_modes)
+    here_a, there_a = mix(after(own_a, own_b), far_a, packed, scale, own_modes)
     block_a = jnp.concatenate([here_a, to_core(there_a)], axis=0)
-    here_b, there_b = mix(after(own_b, block_a), far_b, *weights, scale, own_modes)
+    here_b, there_b = mix(after(own_b, block_a), far_b, packed, scale, own_modes)
     block_b = jnp.concatenate([here_b, to_core(there_b)], axis=0)
     rows_a = after(gather_far(block_a, size), block_b)
     second_a = to_devices(rows_a, going_second, size)

time: 73.3 us -> 71.1 us (0.970)
  waiting for transfers between devices: 21.6 us -> 17.8 us
  starting transfers between devices: 35 us -> 36.5 us
    ppermute x22 -> x23, waiting for transfers between devices: 19.2 us -> 15.4 us  [to_devices(): return lax.ppermute(value, ('tm', 'head'), pairs)]
    ppermute x22 -> x23, starting transfers between devices: 33.8 us -> 35.7 us  [to_devices(): return lax.ppermute(value, ('tm', 'head'), pairs)]
    ppermute x8 -> x5, waiting for transfers between devices: 2.38 us -> 2.37 us  [to_core(): return lax.ppermute(value, 'head', [(0, 1), (1, 0)])]
  transfers between devices with their start and end apart: 30 -> 28, of which waited for: 10 -> 11; matrix products, arithmetic and copies ran while one was open for 0% -> 0% of each run, Pallas kernels for 14% -> 15%
where the time goes in v4:
time: 71.1 us; the launch traced here: 70.9 us
  starting transfers between devices  36.5 us (51%)
  waiting for transfers between devices  17.8 us (25%)
  Pallas kernels  16.5 us (23%)
    ppermute x23, starting transfers between devices, to_devices(): return lax.ppermute(value, ('tm', 'head'), pairs)  35.7 us
    ppermute x23, waiting for transfers between devices, to_devices(): return lax.ppermute(value, ('tm', 'head'), pairs)  15.4 us
    pallas_call x2, Pallas kernels, forward(): pl.pallas_call(functools.partial(forward_kernel, first, count, offset, ha...  6.69 us
    pallas_call x2, Pallas kernels, inverse(): pl.pallas_call(functools.partial(inverse_kernel, half, offset), out_shape...  5.01 us
    pallas_call x2, Pallas kernels, mix(): pl.pallas_call(functools.partial(mix_kernel, scale, own_modes, len(arrive...  2.65 us
    ppermute x5, waiting for transfers between devices, to_core(): return lax.ppermute(value, 'head', [(0, 1), (1, 0)])  2.37 us
    pallas_call x1, Pallas kernels, prepare(): pl.pallas_call(prepare_kernel, out_shape=[mixes] * mix_arrays + [in_vmem(...  1.9 us
  transfers between devices with their start and end apart: 28, of which 11 were waited for; matrix products, arithmetic and copies ran while one was open for 0% of the time, Pallas kernels for 15%

profile of v4, /device:TPU:0, one launch (start us, length us, event | category | flops | bytes accessed | tf_op | source)
XLA Modules:
  0.0 70.9 jit_solution(13933559014967647025)
XLA Ops:
  0.0 3.7 %forward_first.1 = (bf16[4,128,512]{2,1,0:T(8,128)(2,1)S(1)}, f32[4,128,512]{2,1,0:T(8,128)S(1)}, bf16[256,1024]{1,0:T(8,128)(2,1)S(1)}) custom-call(s32[1,128]{1,0:T(1,128)} %bitcast.1, bf16[16,1024,512]{2,1,0:T(8,128)(2,1)} %series_ref.3), custom_call_target="tpu_custom_call" | custom-call | flops 1000 | bytes 1000 | tf_op jit(solution)/shard_map/forward_first/pallas_call | solution.py:118
  3.7 3.0 %collective-permute-start = (bf16[4,128,512]{2,1,0:T(8,128)(2,1)S(1)}, bf16[4,128,512]{2,1,0:T(8,128)(2,1)S(1)}, u32[]{:S(2)}, u32[]{:S(2)}) collective-permute-start(bf16[4,128,512]{2,1,0:T(8,128)(2,1)S(1)} %get-tuple-element.47), channel_id=1, source_target_pairs={{0,2},{1,5},{2,0},{3,7},{4,6},{5,1},{6,4},{7,3},{8,10},{9,13},{10,... | collective-permute-start | bytes 1572872 | tf_op jit(solution)/shard_map/ppermute | solution.py:362
  6.7 3.0 %forward_second.1 = (bf16[4,64,512]{2,1,0:T(8,128)(2,1)S(1)}, bf16[4,64,512]{2,1,0:T(8,128)(2,1)S(1)}, f32[4,128,512]{2,1,0:T(8,128)S(1)}) custom-call(bf16[256,1024]{1,0:T(8,128)(2,1)S(1)} %get-tuple-element.38.extra_ref.table_ref, bf16[16,1024,512]{2,1,0:T(8,128)(2,1)} %series_ref.3), custom_call_target="tpu_custom_call" | custom-call | flops 1000 | bytes 1000 | tf_op jit(solution)/shard_map/forward_second/pallas_call | solution.py:118
  9.8 1.9 %prepare_weights.1 = (bf16[2048,128]{1,0:T(8,128)(2,1)S(1)}, bf16[2048,128]{1,0:T(8,128)(2,1)S(1)}, bf16[2048,128]{1,0:T(8,128)(2,1)S(1)}, bf16[1024,256]{1,0:T(8,128)(2,1)S(1)}) custom-call(f32[8,4,64,128]{3,2,1,0:T(8,128)} %weight_ref, bf16[512,256]{1,0:T(8,128)(2,1)} %query_ref.1, bf16[512,256]{1,0:T(8,128)(2,1)} %out_weight_ref.1, ...), custom_call_target="tpu_custom_call" | custom-call | flops 1000 | bytes 1000 | tf_op jit(solution)/shard_map/prepare_weights/pallas_call | solution.py:203
  12.4 1.5 %collective-permute-done.arrived_ref = bf16[4,128,512]{2,1,0:T(8,128)(2,1)S(1)} collective-permute-done((bf16[4,128,512]{2,1,0:T(8,128)(2,1)S(1)}, bf16[4,128,512]{2,1,0:T(8,128)(2,1)S(1)}, u32[]{:S(2)}, u32[]{:S(2)}) %collective-permute-start) | collective-permute-done | bytes 524320 | tf_op jit(solution)/shard_map/ppermute | solution.py:362
  13.9 2.1 %collective-permute-start.5 = (bf16[4,64,512]{2,1,0:T(8,128)(2,1)S(1)}, bf16[4,64,512]{2,1,0:T(8,128)(2,1)S(1)}, u32[]{:S(2)}, u32[]{:S(2)}) collective-permute-start(bf16[4,64,512]{2,1,0:T(8,128)(2,1)S(1)} %sum_onward.2), channel_id=1, source_target_pairs={{0,4},{1,3},{2,6},{3,1},{4,0},{5,7},{6,2},{7,5},{8,12},{9,11},{10,... | collective-permute-start | bytes 786440 | tf_op jit(solution)/shard_map/ppermute | solution.py:362
  16.0 1.4 %collective-permute-done.1.arrived_ref = bf16[4,64,512]{2,1,0:T(8,128)(2,1)S(1)} collective-permute-done((bf16[4,64,512]{2,1,0:T(8,128)(2,1)S(1)}, bf16[4,64,512]{2,1,0:T(8,128)(2,1)S(1)}, u32[]{:S(2)}, u32[]{:S(2)}) %collective-permute-start.1) | collective-permute-done | bytes 262176 | tf_op jit(solution)/shard_map/ppermute | solution.py:362
  17.4 2.4 %collective-permute-start.6 = (bf16[4,64,512]{2,1,0:T(8,128)(2,1)S(1)}, bf16[4,64,512]{2,1,0:T(8,128)(2,1)S(1)}, u32[]{:S(2)}, u32[]{:S(2)}) collective-permute-start(bf16[4,64,512]{2,1,0:T(8,128)(2,1)S(1)} %get-tuple-element.54), channel_id=1, source_target_pairs={{0,2},{1,5},{2,0},{3,7},{4,6},{5,1},{6,4},{7,3},{8,10},{9,13},{10,... | collective-permute-start | bytes 786440 | tf_op jit(solution)/shard_map/ppermute | solution.py:362
  19.9 1.5 %collective-permute-start.7 = (bf16[4,64,512]{2,1,0:T(8,128)(2,1)S(1)}, bf16[4,64,512]{2,1,0:T(8,128)(2,1)S(1)}, u32[]{:S(2)}, u32[]{:S(2)}) collective-permute-start(bf16[4,64,512]{2,1,0:T(8,128)(2,1)S(1)} %sum_onward.3), channel_id=1, source_target_pairs={{0,4},{1,3},{2,6},{3,1},{4,0},{5,7},{6,2},{7,5},{8,12},{9,11},{10,... | collective-permute-start | bytes 786440 | tf_op jit(solution)/shard_map/ppermute | solution.py:362
  22.1 4.5 %collective-permute-start.8 = (bf16[4,16,512]{2,1,0:T(8,128)(2,1)S(1)}, bf16[4,16,512]{2,1,0:T(8,128)(2,1)S(1)}, u32[]{:S(2)}, u32[]{:S(2)}) collective-permute-start(bf16[4,16,512]{2,1,0:T(8,128)(2,1)S(1)} %get-tuple-element.57), channel_id=1, source_target_pairs={{0,24},{1,25},{2,26},{3,27},{4,28},{5,29},{6,30},{7,31},{8,16},{9,... | collective-permute-start | bytes 196616 | tf_op jit(solution)/shard_map/ppermute | solution.py:362
  27.4 3.8 %collective-permute-start.12 = (bf16[4,16,512]{2,1,0:T(8,128)(2,1)S(1)}, bf16[4,16,512]{2,1,0:T(8,128)(2,1)S(1)}, u32[]{:S(2)}, u32[]{:S(2)}) collective-permute-start(bf16[4,16,512]{2,1,0:T(8,128)(2,1)S(1)} %get-tuple-element.63), channel_id=1, source_target_pairs={{0,24},{1,25},{2,26},{3,27},{4,28},{5,29},{6,30},{7,31},{8,16},{9,... | collective-permute-start | bytes 196616 | tf_op jit(solution)/shard_map/ppermute | solution.py:362
  35.8 2.4 %collective-permute-start.23 = (bf16[8,16,256]{2,1,0:T(8,128)(2,1)S(1)}, bf16[8,16,256]{2,1,0:T(8,128)(2,1)S(1)}, u32[]{:S(2)}, u32[]{:S(2)}) collective-permute-start(bf16[8,16,256]{2,1,0:T(8,128)(2,1)S(1)} %constant_dynamic-update-slice_fusion.refs_0_), channel_id=1, source_target_pairs={{0,24},{1,25},{2,26},{3,27},{4,28},{5,29},{6,30},{7,31},{8,16},{9,... | collective-permute-start | bytes 196616 | tf_op jit(solution)/shard_map/ppermute | solution.py:362
  38.4 1.8 %collective-permute-start.21 = (bf16[8,16,256]{2,1,0:T(8,128)(2,1)S(1)}, bf16[8,16,256]{2,1,0:T(8,128)(2,1)S(1)}, u32[]{:S(2)}, u32[]{:S(2)}) collective-permute-start(bf16[8,16,256]{2,1,0:T(8,128)(2,1)S(1)} %constant_dynamic-update-slice_fusion.refs_0_), channel_id=1, source_target_pairs={{0,8},{1,9},{2,10},{3,11},{4,12},{5,13},{6,14},{7,15},{8,0},{9,1},... | collective-permute-start | bytes 196616 | tf_op jit(solution)/shard_map/ppermute | solution.py:362
  42.8 2.4 %collective-permute-start.18 = (bf16[8,16,256]{2,1,0:T(8,128)(2,1)S(1)}, bf16[8,16,256]{2,1,0:T(8,128)(2,1)S(1)}, u32[]{:S(2)}, u32[]{:S(2)}) collective-permute-start(bf16[8,16,256]{2,1,0:T(8,128)(2,1)S(1)} %constant_dynamic-update-slice_fusion.2.refs_0_), channel_id=1, source_target_pairs={{0,24},{1,25},{2,26},{3,27},{4,28},{5,29},{6,30},{7,31},{8,16},{9,... | collective-permute-start | bytes 196616 | tf_op jit(solution)/shard_map/ppermute | solution.py:362
  45.2 2.0 %collective-permute-start.16 = (bf16[8,16,256]{2,1,0:T(8,128)(2,1)S(1)}, bf16[8,16,256]{2,1,0:T(8,128)(2,1)S(1)}, u32[]{:S(2)}, u32[]{:S(2)}) collective-permute-start(bf16[8,16,256]{2,1,0:T(8,128)(2,1)S(1)} %constant_dynamic-update-slice_fusion.2.refs_0_), channel_id=1, source_target_pairs={{0,8},{1,9},{2,10},{3,11},{4,12},{5,13},{6,14},{7,15},{8,0},{9,1},... | collective-permute-start | bytes 196616 | tf_op jit(solution)/shard_map/ppermute | solution.py:362
  47.2 1.7 %collective-permute-start.26 = (bf16[8,64,256]{2,1,0:T(8,128)(2,1)S(1)}, bf16[8,64,256]{2,1,0:T(8,128)(2,1)S(1)}, u32[]{:S(2)}, u32[]{:S(2)}) collective-permute-start(bf16[8,64,256]{2,1,0:T(8,128)(2,1)S(1)} %join_rows.3.refs_0_), channel_id=1, source_target_pairs={{0,4},{1,3},{2,6},{3,1},{4,0},{5,7},{6,2},{7,5},{8,12},{9,11},{10,... | collective-permute-start | bytes 786440 | tf_op jit(solution)/shard_map/ppermute | solution.py:362
  49.0 1.5 %collective-permute-start.24 = (bf16[8,64,256]{2,1,0:T(8,128)(2,1)S(1)}, bf16[8,64,256]{2,1,0:T(8,128)(2,1)S(1)}, u32[]{:S(2)}, u32[]{:S(2)}) collective-permute-start(bf16[8,64,256]{2,1,0:T(8,128)(2,1)S(1)} %join_rows.3.refs_0_), channel_id=1, source_target_pairs={{0,2},{1,5},{2,0},{3,7},{4,6},{5,1},{6,4},{7,3},{8,10},{9,13},{10,... | collective-permute-start | bytes 786440 | tf_op jit(solution)/shard_map/ppermute | solution.py:362
  51.6 1.7 %collective-permute-start.19 = (bf16[8,64,256]{2,1,0:T(8,128)(2,1)S(1)}, bf16[8,64,256]{2,1,0:T(8,128)(2,1)S(1)}, u32[]{:S(2)}, u32[]{:S(2)}) collective-permute-start(bf16[8,64,256]{2,1,0:T(8,128)(2,1)S(1)} %join_rows.2.refs_0_), channel_id=1, source_target_pairs={{0,4},{1,3},{2,6},{3,1},{4,0},{5,7},{6,2},{7,5},{8,12},{9,11},{10,... | collective-permute-start | bytes 786440 | tf_op jit(solution)/shard_map/ppermute | solution.py:362
  53.3 1.5 %collective-permute-start.20 = (bf16[8,64,256]{2,1,0:T(8,128)(2,1)S(1)}, bf16[8,64,256]{2,1,0:T(8,128)(2,1)S(1)}, u32[]{:S(2)}, u32[]{:S(2)}) collective-permute-start(bf16[8,64,256]{2,1,0:T(8,128)(2,1)S(1)} %join_rows.2.refs_0_), channel_id=1, source_target_pairs={{0,2},{1,5},{2,0},{3,7},{4,6},{5,1},{6,4},{7,3},{8,10},{9,13},{10,... | collective-permute-start | bytes 786440 | tf_op jit(solution)/shard_map/ppermute | solution.py:362
  54.8 1.6 %collective-permute-done.26.refs_1_ = bf16[8,64,256]{2,1,0:T(8,128)(2,1)S(1)} collective-permute-done((bf16[8,64,256]{2,1,0:T(8,128)(2,1)S(1)}, bf16[8,64,256]{2,1,0:T(8,128)(2,1)S(1)}, u32[]{:S(2)}, u32[]{:S(2)}) %collective-permute-start.26) | collective-permute-done | bytes 262176 | tf_op jit(solution)/shard_map/ppermute | solution.py:362
  57.0 5.0 %collective-permute-done.19.refs_1_ = bf16[8,64,256]{2,1,0:T(8,128)(2,1)S(1)} collective-permute-done((bf16[8,64,256]{2,1,0:T(8,128)(2,1)S(1)}, bf16[8,64,256]{2,1,0:T(8,128)(2,1)S(1)}, u32[]{:S(2)}, u32[]{:S(2)}) %collective-permute-start.19) | collective-permute-done | bytes 262176 | tf_op jit(solution)/shard_map/ppermute | solution.py:362
  63.8 2.5 %inverse_first.1.refs_4_ = bf16[16,1024,256]{2,1,0:T(8,128)(2,1)} custom-call(bf16[1024,256]{1,0:T(8,128)(2,1)S(1)} %get-tuple-element.41.table_ref, bf16[8,64,256]{2,1,0:T(8,128)(2,1)S(1)} %join_rows.3.refs_0_, bf16[8,64,256]{2,1,0:T(8,128)(2,1)S(1)} %collective-permute-done.26.refs_1_, bf16[8,64,256]{2,1,0:T(8,128)(2,1)S(1)} %collective-permute-done.24.refs_2_, ...), custom_call_target="tpu_custom_call" | custom-call | flops 1000 | bytes 1000 | tf_op jit(solution)/shard_map/inverse_first/pallas_call | solution.py:347
  66.3 2.2 %collective-permute-done.25.refs_3_ = bf16[8,64,256]{2,1,0:T(8,128)(2,1)S(1)} collective-permute-done((bf16[8,64,256]{2,1,0:T(8,128)(2,1)S(1)}, bf16[8,64,256]{2,1,0:T(8,128)(2,1)S(1)}, u32[]{:S(2)}, u32[]{:S(2)}) %collective-permute-start.25) | collective-permute-done | bytes 262176 | tf_op jit(solution)/shard_map/ppermute | solution.py:362
  68.4 2.5 %inverse_second.1 = bf16[16,1024,256]{2,1,0:T(8,128)(2,1)} custom-call(bf16[1024,256]{1,0:T(8,128)(2,1)S(1)} %get-tuple-element.41.table_ref, bf16[8,64,256]{2,1,0:T(8,128)(2,1)S(1)} %join_rows.2.refs_0_, bf16[8,64,256]{2,1,0:T(8,128)(2,1)S(1)} %collective-permute-done.19.refs_1_, ...), custom_call_target="tpu_custom_call", output_to_operand_aliasing={{}: (5, {})} | custom-call | flops 1000 | bytes 1000 | tf_op jit(solution)/shard_map/inverse_second/pallas_call | solution.py:347
  (49 shorter events, 13.1 us)
Async XLA Ops:
  3.7 10.2 %collective-permute-start = (bf16[4,128,512]{2,1,0:T(8,128)(2,1)S(1)}, bf16[4,128,512]{2,1,0:T(8,128)(2,1)S(1)}, u32[]{:S(2)}, u32[]{:S(2)}) collective-permute-start(bf16[4,128,512]{2,1,0:T(8,128)(2,1)S(1)} %get-tuple-element.47), channel_id=1, source_target_pairs={{0,2},{1,5},{2,0},{3,7},{4,6},{5,1},{6,4},{7,3},{8,10},{9,13},{10,... | collective-permute-start | bytes 1572872 | tf_op jit(solution)/shard_map/ppermute | solution.py:362
  9.7 7.7 %collective-permute-start.1 = (bf16[4,64,512]{2,1,0:T(8,128)(2,1)S(1)}, bf16[4,64,512]{2,1,0:T(8,128)(2,1)S(1)}, u32[]{:S(2)}, u32[]{:S(2)}) collective-permute-start(bf16[4,64,512]{2,1,0:T(8,128)(2,1)S(1)} %get-tuple-element.49), channel_id=1, source_target_pairs={{0,2},{1,5},{2,0},{3,7},{4,6},{5,1},{6,4},{7,3},{8,10},{9,13},{10,... | collective-permute-start | bytes 786440 | tf_op jit(solution)/shard_map/ppermute | solution.py:362
  11.7 8.1 %collective-permute-start.2 = (bf16[2048,128]{1,0:T(8,128)(2,1)S(1)}, bf16[2048,128]{1,0:T(8,128)(2,1)S(1)}, u32[]{:S(2)}, u32[]{:S(2)}) collective-permute-start(bf16[2048,128]{1,0:T(8,128)(2,1)S(1)} %get-tuple-element.43.refs_3_), channel_id=1, source_target_pairs={{0,1},{1,0},{2,3},{3,2},{4,5},{5,4},{6,7},{7,6},{8,9},{9,8},{10,11... | collective-permute-start | bytes 1572872 | tf_op jit(solution)/shard_map/ppermute | solution.py:369
  11.8 9.6 %collective-permute-start.3 = (bf16[2048,128]{1,0:T(8,128)(2,1)S(1)}, bf16[2048,128]{1,0:T(8,128)(2,1)S(1)}, u32[]{:S(2)}, u32[]{:S(2)}) collective-permute-start(bf16[2048,128]{1,0:T(8,128)(2,1)S(1)} %get-tuple-element.44.refs_4_), channel_id=1, source_target_pairs={{0,1},{1,0},{2,3},{3,2},{4,5},{5,4},{6,7},{7,6},{8,9},{9,8},{10,11... | collective-permute-start | bytes 1572872 | tf_op jit(solution)/shard_map/ppermute | solution.py:369
  12.3 9.1 %collective-permute-start.4 = (bf16[2048,128]{1,0:T(8,128)(2,1)S(1)}, bf16[2048,128]{1,0:T(8,128)(2,1)S(1)}, u32[]{:S(2)}, u32[]{:S(2)}) collective-permute-start(bf16[2048,128]{1,0:T(8,128)(2,1)S(1)} %get-tuple-element.45.refs_5_), channel_id=1, source_target_pairs={{0,1},{1,0},{2,3},{3,2},{4,5},{5,4},{6,7},{7,6},{8,9},{9,8},{10,11... | collective-permute-start | bytes 1572872 | tf_op jit(solution)/shard_map/ppermute | solution.py:369
  13.9 8.2 %collective-permute-start.5 = (bf16[4,64,512]{2,1,0:T(8,128)(2,1)S(1)}, bf16[4,64,512]{2,1,0:T(8,128)(2,1)S(1)}, u32[]{:S(2)}, u32[]{:S(2)}) collective-permute-start(bf16[4,64,512]{2,1,0:T(8,128)(2,1)S(1)} %sum_onward.2), channel_id=1, source_target_pairs={{0,4},{1,3},{2,6},{3,1},{4,0},{5,7},{6,2},{7,5},{8,12},{9,11},{10,... | collective-permute-start | bytes 786440 | tf_op jit(solution)/shard_map/ppermute | solution.py:362
  17.4 9.8 %collective-permute-start.6 = (bf16[4,64,512]{2,1,0:T(8,128)(2,1)S(1)}, bf16[4,64,512]{2,1,0:T(8,128)(2,1)S(1)}, u32[]{:S(2)}, u32[]{:S(2)}) collective-permute-start(bf16[4,64,512]{2,1,0:T(8,128)(2,1)S(1)} %get-tuple-element.54), channel_id=1, source_target_pairs={{0,2},{1,5},{2,0},{3,7},{4,6},{5,1},{6,4},{7,3},{8,10},{9,13},{10,... | collective-permute-start | bytes 786440 | tf_op jit(solution)/shard_map/ppermute | solution.py:362
  19.9 7.4 %collective-permute-start.7 = (bf16[4,64,512]{2,1,0:T(8,128)(2,1)S(1)}, bf16[4,64,512]{2,1,0:T(8,128)(2,1)S(1)}, u32[]{:S(2)}, u32[]{:S(2)}) collective-permute-start(bf16[4,64,512]{2,1,0:T(8,128)(2,1)S(1)} %sum_onward.3), channel_id=1, source_target_pairs={{0,4},{1,3},{2,6},{3,1},{4,0},{5,7},{6,2},{7,5},{8,12},{9,11},{10,... | collective-permute-start | bytes 786440 | tf_op jit(solution)/shard_map/ppermute | solution.py:362
  22.1 9.0 %collective-permute-start.8 = (bf16[4,16,512]{2,1,0:T(8,128)(2,1)S(1)}, bf16[4,16,512]{2,1,0:T(8,128)(2,1)S(1)}, u32[]{:S(2)}, u32[]{:S(2)}) collective-permute-start(bf16[4,16,512]{2,1,0:T(8,128)(2,1)S(1)} %get-tuple-element.57), channel_id=1, source_target_pairs={{0,24},{1,25},{2,26},{3,27},{4,28},{5,29},{6,30},{7,31},{8,16},{9,... | collective-permute-start | bytes 196616 | tf_op jit(solution)/shard_map/ppermute | solution.py:362
  26.6 6.5 %collective-permute-start.9 = (bf16[4,16,512]{2,1,0:T(8,128)(2,1)S(1)}, bf16[4,16,512]{2,1,0:T(8,128)(2,1)S(1)}, u32[]{:S(2)}, u32[]{:S(2)}) collective-permute-start(bf16[4,16,512]{2,1,0:T(8,128)(2,1)S(1)} %get-tuple-element.58), channel_id=1, source_target_pairs={{0,16},{1,17},{2,18},{3,19},{4,20},{5,21},{6,22},{7,23},{8,24},{9,... | collective-permute-start | bytes 196616 | tf_op jit(solution)/shard_map/ppermute | solution.py:362
  26.6 6.5 %collective-permute-start.10 = (bf16[4,16,512]{2,1,0:T(8,128)(2,1)S(1)}, bf16[4,16,512]{2,1,0:T(8,128)(2,1)S(1)}, u32[]{:S(2)}, u32[]{:S(2)}) collective-permute-start(bf16[4,16,512]{2,1,0:T(8,128)(2,1)S(1)} %get-tuple-element.59), channel_id=1, source_target_pairs={{0,8},{1,9},{2,10},{3,11},{4,12},{5,13},{6,14},{7,15},{8,0},{9,1},... | collective-permute-start | bytes 196616 | tf_op jit(solution)/shard_map/ppermute | solution.py:362
  27.4 11.0 %collective-permute-start.12 = (bf16[4,16,512]{2,1,0:T(8,128)(2,1)S(1)}, bf16[4,16,512]{2,1,0:T(8,128)(2,1)S(1)}, u32[]{:S(2)}, u32[]{:S(2)}) collective-permute-start(bf16[4,16,512]{2,1,0:T(8,128)(2,1)S(1)} %get-tuple-element.63), channel_id=1, source_target_pairs={{0,24},{1,25},{2,26},{3,27},{4,28},{5,29},{6,30},{7,31},{8,16},{9,... | collective-permute-start | bytes 196616 | tf_op jit(solution)/shard_map/ppermute | solution.py:362
  31.2 9.0 %collective-permute-start.13 = (bf16[4,16,512]{2,1,0:T(8,128)(2,1)S(1)}, bf16[4,16,512]{2,1,0:T(8,128)(2,1)S(1)}, u32[]{:S(2)}, u32[]{:S(2)}) collective-permute-start(bf16[4,16,512]{2,1,0:T(8,128)(2,1)S(1)} %get-tuple-element.64), channel_id=1, source_target_pairs={{0,16},{1,17},{2,18},{3,19},{4,20},{5,21},{6,22},{7,23},{8,24},{9,... | collective-permute-start | bytes 196616 | tf_op jit(solution)/shard_map/ppermute | solution.py:362
  31.2 9.0 %collective-permute-start.14 = (bf16[4,16,512]{2,1,0:T(8,128)(2,1)S(1)}, bf16[4,16,512]{2,1,0:T(8,128)(2,1)S(1)}, u32[]{:S(2)}, u32[]{:S(2)}) collective-permute-start(bf16[4,16,512]{2,1,0:T(8,128)(2,1)S(1)} %get-tuple-element.65), channel_id=1, source_target_pairs={{0,8},{1,9},{2,10},{3,11},{4,12},{5,13},{6,14},{7,15},{8,0},{9,1},... | collective-permute-start | bytes 196616 | tf_op jit(solution)/shard_map/ppermute | solution.py:362
  35.8 9.4 %collective-permute-start.23 = (bf16[8,16,256]{2,1,0:T(8,128)(2,1)S(1)}, bf16[8,16,256]{2,1,0:T(8,128)(2,1)S(1)}, u32[]{:S(2)}, u32[]{:S(2)}) collective-permute-start(bf16[8,16,256]{2,1,0:T(8,128)(2,1)S(1)} %constant_dynamic-update-slice_fusion.refs_0_), channel_id=1, source_target_pairs={{0,24},{1,25},{2,26},{3,27},{4,28},{5,29},{6,30},{7,31},{8,16},{9,... | collective-permute-start | bytes 196616 | tf_op jit(solution)/shard_map/ppermute | solution.py:362
  38.2 9.0 %collective-permute-start.22 = (bf16[8,16,256]{2,1,0:T(8,128)(2,1)S(1)}, bf16[8,16,256]{2,1,0:T(8,128)(2,1)S(1)}, u32[]{:S(2)}, u32[]{:S(2)}) collective-permute-start(bf16[8,16,256]{2,1,0:T(8,128)(2,1)S(1)} %constant_dynamic-update-slice_fusion.refs_0_), channel_id=1, source_target_pairs={{0,16},{1,17},{2,18},{3,19},{4,20},{5,21},{6,22},{7,23},{8,24},{9,... | collective-permute-start | bytes 196616 | tf_op jit(solution)/shard_map/ppermute | solution.py:362
  38.4 8.8 %collective-permute-start.21 = (bf16[8,16,256]{2,1,0:T(8,128)(2,1)S(1)}, bf16[8,16,256]{2,1,0:T(8,128)(2,1)S(1)}, u32[]{:S(2)}, u32[]{:S(2)}) collective-permute-start(bf16[8,16,256]{2,1,0:T(8,128)(2,1)S(1)} %constant_dynamic-update-slice_fusion.refs_0_), channel_id=1, source_target_pairs={{0,8},{1,9},{2,10},{3,11},{4,12},{5,13},{6,14},{7,15},{8,0},{9,1},... | collective-permute-start | bytes 196616 | tf_op jit(solution)/shard_map/ppermute | solution.py:362
  42.8 7.7 %collective-permute-start.18 = (bf16[8,16,256]{2,1,0:T(8,128)(2,1)S(1)}, bf16[8,16,256]{2,1,0:T(8,128)(2,1)S(1)}, u32[]{:S(2)}, u32[]{:S(2)}) collective-permute-start(bf16[8,16,256]{2,1,0:T(8,128)(2,1)S(1)} %constant_dynamic-update-slice_fusion.2.refs_0_), channel_id=1, source_target_pairs={{0,24},{1,25},{2,26},{3,27},{4,28},{5,29},{6,30},{7,31},{8,16},{9,... | collective-permute-start | bytes 196616 | tf_op jit(solution)/shard_map/ppermute | solution.py:362
  47.2 9.2 %collective-permute-start.26 = (bf16[8,64,256]{2,1,0:T(8,128)(2,1)S(1)}, bf16[8,64,256]{2,1,0:T(8,128)(2,1)S(1)}, u32[]{:S(2)}, u32[]{:S(2)}) collective-permute-start(bf16[8,64,256]{2,1,0:T(8,128)(2,1)S(1)} %join_rows.3.refs_0_), channel_id=1, source_target_pairs={{0,4},{1,3},{2,6},{3,1},{4,0},{5,7},{6,2},{7,5},{8,12},{9,11},{10,... | collective-permute-start | bytes 786440 | tf_op jit(solution)/shard_map/ppermute | solution.py:362
  49.0 8.1 %collective-permute-start.24 = (bf16[8,64,256]{2,1,0:T(8,128)(2,1)S(1)}, bf16[8,64,256]{2,1,0:T(8,128)(2,1)S(1)}, u32[]{:S(2)}, u32[]{:S(2)}) collective-permute-start(bf16[8,64,256]{2,1,0:T(8,128)(2,1)S(1)} %join_rows.3.refs_0_), channel_id=1, source_target_pairs={{0,2},{1,5},{2,0},{3,7},{4,6},{5,1},{6,4},{7,3},{8,10},{9,13},{10,... | collective-permute-start | bytes 786440 | tf_op jit(solution)/shard_map/ppermute | solution.py:362
  51.6 10.5 %collective-permute-start.19 = (bf16[8,64,256]{2,1,0:T(8,128)(2,1)S(1)}, bf16[8,64,256]{2,1,0:T(8,128)(2,1)S(1)}, u32[]{:S(2)}, u32[]{:S(2)}) collective-permute-start(bf16[8,64,256]{2,1,0:T(8,128)(2,1)S(1)} %join_rows.2.refs_0_), channel_id=1, source_target_pairs={{0,4},{1,3},{2,6},{3,1},{4,0},{5,7},{6,2},{7,5},{8,12},{9,11},{10,... | collective-permute-start | bytes 786440 | tf_op jit(solution)/shard_map/ppermute | solution.py:362
  53.3 12.9 %collective-permute-start.20 = (bf16[8,64,256]{2,1,0:T(8,128)(2,1)S(1)}, bf16[8,64,256]{2,1,0:T(8,128)(2,1)S(1)}, u32[]{:S(2)}, u32[]{:S(2)}) collective-permute-start(bf16[8,64,256]{2,1,0:T(8,128)(2,1)S(1)} %join_rows.2.refs_0_), channel_id=1, source_target_pairs={{0,2},{1,5},{2,0},{3,7},{4,6},{5,1},{6,4},{7,3},{8,10},{9,13},{10,... | collective-permute-start | bytes 786440 | tf_op jit(solution)/shard_map/ppermute | solution.py:362
  56.4 7.3 %collective-permute-start.27 = (bf16[8,64,256]{2,1,0:T(8,128)(2,1)S(1)}, bf16[8,64,256]{2,1,0:T(8,128)(2,1)S(1)}, u32[]{:S(2)}, u32[]{:S(2)}) collective-permute-start(bf16[8,64,256]{2,1,0:T(8,128)(2,1)S(1)} %collective-permute-done.26.refs_1_), channel_id=1, source_target_pairs={{0,2},{1,5},{2,0},{3,7},{4,6},{5,1},{6,4},{7,3},{8,10},{9,13},{10,... | collective-permute-start | bytes 786440 | tf_op jit(solution)/shard_map/ppermute | solution.py:362
  62.1 6.4 %collective-permute-start.25 = (bf16[8,64,256]{2,1,0:T(8,128)(2,1)S(1)}, bf16[8,64,256]{2,1,0:T(8,128)(2,1)S(1)}, u32[]{:S(2)}, u32[]{:S(2)}) collective-permute-start(bf16[8,64,256]{2,1,0:T(8,128)(2,1)S(1)} %collective-permute-done.19.refs_1_), channel_id=1, source_target_pairs={{0,2},{1,5},{2,0},{3,7},{4,6},{5,1},{6,4},{7,3},{8,10},{9,13},{10,... | collective-permute-start | bytes 786440 | tf_op jit(solution)/shard_map/ppermute | solution.py:362
  (4 other events, 15.3 us)

commit v5 on v4

--- a/solution.py
+++ b/solution.py
@@ -40,14 +40,13 @@
     lanes = modes_row.shape[1]
     row = lax.broadcasted_iota(jnp.int32, (rows, lanes), 0)
     lane = lax.broadcasted_iota(jnp.int32, (rows, lanes), 1)
-    block_rows = 2 * own_modes
-    far = rows // block_rows // 4
-    block = row // block_rows
-    inside = row - block * block_rows
-    quarter = block // far
-    relative = (quarter // 2) * (1 + core) + (quarter % 2) * (2 - core) + 4 * (block % far)
-    imaginary = inside // own_modes
-    wanted = (place ^ relative) * own_modes + inside - imaginary * own_modes
+    far = rows // own_modes // 8
+    mode_bits, far_bits = own_modes.bit_length() - 1, far.bit_length() - 1
+    block = row >> (mode_bits + 1)
+    quarter = block >> far_bits
+    relative = ((quarter >> 1) << core) + ((quarter & 1) << (1 - core)) + 4 * (block & (far - 1))
+    imaginary = (row >> mode_bits) & 1
+    wanted = ((place ^ relative) << mode_bits) + (row & (own_modes - 1))
     picked = jnp.where(lane == wanted, modes_row.astype(f32), 0.0)
     mode = jnp.sum(picked, axis=1, keepdims=True).astype(jnp.int32)
     return mode, imaginary[:, :1] * (series_length // 4)
@@ -84,7 +83,7 @@
 
 def forward_kernel(first, count, offset, half, own_modes, series_length, extra_ref, series_ref, *refs):
     if first:
-        send_ref, keep_ref, table_ref, held, sems = refs
+        corner_ref, side_ref, keep_ref, table_ref, held, sems = refs
     else:
         corner_ref, side_ref, keep_ref, held, sems = refs
         table_ref = extra_ref
@@ -98,17 +97,14 @@
     for b in range(count):
         copies[b].wait()
         part = jnp.dot(table_ref[...], held[b], preferred_element_type=f32)
-        if first:
-            send_ref[b] = part[middle:].astype(bf16)
-        else:
-            side_ref[b] = part[middle:middle + middle // 2].astype(bf16)
-            corner_ref[b] = part[middle + middle // 2:].astype(bf16)
+        side_ref[b] = part[middle:middle + middle // 2].astype(bf16)
+        corner_ref[b] = part[middle + middle // 2:].astype(bf16)
         keep_ref[b] = part[:middle]
 
 
 def forward(first, series, extra, count, offset, half, own_modes, series_length, rows):
     _, time_count, width = series.shape
-    sends = [in_vmem((count, rows // 2, width), bf16)] if first else [in_vmem((count, rows // 4, width), bf16)] * 2
+    sends = [in_vmem((count, rows // 4, width), bf16)] * 2
     outs = sends + [in_vmem((count, rows // 2, width), f32)]
     if first:
         outs.append(in_vmem((rows, time_count), bf16))
@@ -145,30 +141,45 @@
     )(*held(keep, arrived))
 
 
-def total_kernel(block_rows, keep_ref, arrived_ref, second_ref, own_ref, *far_refs):
-    middle = second_ref.shape[1]
-    total = keep_ref[:, :middle] + arrived_ref[:, :middle].astype(f32) + second_ref[...].astype(f32)
+def base_kernel(keep_ref, side_ref, out_ref):
+    out_ref[...] = keep_ref[:, :side_ref.shape[1]] + side_ref[...].astype(f32)
+
+
+def base(keep, side):
+    return pl.pallas_call(
+        base_kernel,
+        out_shape=in_vmem(side.shape, f32),
+        in_specs=[whole] * 2,
+        out_specs=whole,
+        compiler_params=pltpu.CompilerParams(vmem_limit_bytes=16 * 2**20),
+        cost_estimate=small,
+        name="sum_base",
+    )(*held(keep, side))
+
+
+def total_kernel(block_rows, base_ref, second_ref, own_ref, *far_refs):
+    total = base_ref[...] + second_ref[...].astype(f32)
     own_ref[...] = total[:, :block_rows]
     for index, ref in enumerate(far_refs):
         ref[...] = total[:, (index + 1) * block_rows:(index + 2) * block_rows].astype(bf16)
 
 
-def total_rows(keep, arrived, second, block_rows):
+def total_rows(base, second, block_rows):
     count, rows, width = second.shape
     if block_rows % 16:
-        total = keep[:, :rows] + arrived[:, :rows].astype(f32) + second.astype(f32)
+        total = base + second.astype(f32)
         parts = [total[:, start:start + block_rows] for start in range(0, rows, block_rows)]
         return parts[0], [part.astype(bf16) for part in parts[1:]]
     share = (count, block_rows, width)
     parts = pl.pallas_call(
         functools.partial(total_kernel, block_rows),
         out_shape=[in_vmem(share, f32)] + [in_vmem(share, bf16)] * (rows // block_rows - 1),
-        in_specs=[whole] * 3,
+        in_specs=[whole] * 2,
         out_specs=[whole] * (rows // block_rows),
         compiler_params=pltpu.CompilerParams(vmem_limit_bytes=16 * 2**20),
         cost_estimate=small,
         name="sum_total",
-    )(*held(keep, arrived, second))
+    )(*held(base, second))
     return parts[0], parts[1:]
 
 
@@ -208,7 +219,7 @@
         compiler_params=pltpu.CompilerParams(vmem_limit_bytes=16 * 2**20),
         cost_estimate=small,
         name="prepare_weights",
-    )(in_hbm(weight), in_hbm(query), in_hbm(out_weight), *held(table))
+    )(*held(weight, query, out_weight, table))
     return outs[:-1], outs[-1]
 
 
@@ -250,7 +261,7 @@
         [total[:, :own_modes].reshape(rows, width), total[:, own_modes:].reshape(rows, width)], axis=0
     ))
     lower = lax.broadcasted_iota(jnp.int32, (rows, 128), 1) < 64
-    row_mode = lax.broadcasted_iota(jnp.int32, (2 * rows, 128), 0) % own_modes
+    row_mode = lax.broadcasted_iota(jnp.int32, (2 * rows, 128), 0) & (own_modes - 1)
     mixed, out_weights = [], []
     for packed in (packed_refs[:each], packed_refs[each:]):
         mixes, query, out_weight = packed_parts(packed, half // 64, width)
@@ -318,25 +329,24 @@
     return results
 
 
-def inverse_kernel(half, offset, table_ref, *refs):
+def inverse_kernel(half, offset, start, own, table_ref, *refs):
     pieces, (out_ref, held, sems) = refs[:4], refs[-3:]
-    count = held.shape[0]
-    own = count // 2
     core = lax.axis_index("head")
     copies = []
-    for b in range(count):
-        spectra = jnp.concatenate([piece[b] for piece in pieces], axis=0)
-        held[b] = jnp.dot(table_ref[...], spectra, preferred_element_type=f32).astype(bf16)
-        index = (core ^ (b // own)) * half + offset + b % own
-        copies.append(pltpu.make_async_copy(held.at[b], out_ref.at[index], sems.at[b]))
+    for index in range(held.shape[0]):
+        b = start + index
+        spectra = jnp.concatenate([piece[b] for piece in pieces[:3]] + [pieces[3][index]], axis=0)
+        held[index] = jnp.dot(table_ref[...], spectra, preferred_element_type=f32).astype(bf16)
+        place = (core ^ (b // own)) * half + offset + b % own
+        copies.append(pltpu.make_async_copy(held.at[index], out_ref.at[place], sems.at[index]))
         copies[-1].start()
     for copy in copies:
         copy.wait()
 
 
-def inverse(table, pieces, previous, series_count, half, offset):
+def inverse(table, pieces, previous, series_count, half, offset, start=0):
     time_count, rows = table.shape
-    count, _, width = pieces[0].shape
+    count, _, width = pieces[3].shape
     in_specs = [whole] * 5
     args = held(table, *pieces)
     aliases = {}
@@ -345,7 +355,7 @@
         aliases = {len(args): 0}
         args.append(in_hbm(previous))
     return pl.pallas_call(
-        functools.partial(inverse_kernel, half, offset),
+        functools.partial(inverse_kernel, half, offset, start, pieces[0].shape[0] // 2),
         out_shape=pltpu.HBM((series_count, time_count, width), bf16),
         in_specs=in_specs,
         out_specs=pl.BlockSpec(memory_space=pltpu.HBM),
@@ -353,7 +363,7 @@
         input_output_aliases=aliases,
         compiler_params=pltpu.CompilerParams(vmem_limit_bytes=16 * 2**20),
         cost_estimate=small,
-        name="inverse_first" if previous is None else "inverse_second",
+        name="inverse_first" if previous is None else "inverse_next",
     )(*args)
 
 
@@ -408,26 +418,29 @@
     count_a = half // 2
     count_b = half - count_a
 
-    send_a, keep_a, table = forward(
+    corner_a, side_a, keep_a, table = forward(
         True, series, modes[None, :], count_a, 0, half, own_modes, series_length, rows
     )
     corner_b, side_b, keep_b = forward(False, series, table, count_b, count_a, half, own_modes, series_length, rows)
     block_rows = 2 * own_modes
     scale = 1.0 / math.sqrt(series_length * mode_total)
-    arrived_a = to_devices(send_a, going_first, size)
+    corner_a = to_devices(corner_a, going_first, size)
+    side_a = to_devices(side_a, going_first, size)
     corner_b = to_devices(corner_b, going_first, size)
 
-    packed, table_back = prepare(after(mix_weight, keep_b), query_weight, out_weight, table)
+    packed, table_back = prepare(mix_weight, query_weight, out_weight, after(table, keep_b))
     packed = [packed, [to_core(array) for array in packed]]
 
-    onward_a = onward(after(keep_a, keep_b, *packed[0]), arrived_a)
+    onward_a = onward(after(keep_a, keep_b, *packed[0]), corner_a)
     second_a = to_devices(onward_a, going_second, size)
-    onward_b = onward(after(keep_b, onward_a), corner_b, ahead)
+    base_a = base(after(keep_a, onward_a), side_a)
+    onward_b = onward(after(keep_b, base_a), corner_b, ahead)
     second_b = to_devices(onward_b, going_second, size)
     side_b = to_devices(after(side_b, onward_b), going_first, size)
-    own_a, far_a = total_rows(after(keep_a, onward_b, *packed[1]), arrived_a, second_a, block_rows)
+    own_a, far_a = total_rows(after(base_a, onward_b, *packed[1]), second_a, block_rows)
     far_a = send_far(far_a, size)
-    own_b, far_b = total_rows(after(keep_b, own_a), side_b, second_b, block_rows)
+    base_b = base(after(keep_b, own_a), side_b)
+    own_b, far_b = total_rows(base_b, second_b, block_rows)
     far_b = send_far(far_b, size)
 
     here_a, there_a = mix(after(own_a, own_b), far_a, packed, scale, own_modes)
@@ -443,8 +456,12 @@
     first_b = to_devices(rows_b, going_first, size)
     pieces_a = [after(rows_a, second_b), second_a, first_a, both_a]
     output = inverse(table_back, pieces_a, None, series_count, half, 0)
-    both_b = to_devices(after(second_b, first_a), going_first, size)
-    return inverse(table_back, [rows_b, second_b, first_b, both_b], output, series_count, half, count_a)
+    second_now = after(second_b, first_a)
+    both_b = [to_devices(second_now[:count_b], going_first, size), to_devices(second_now[count_b:], going_first, size)]
+    for part, start in zip(both_b, (0, count_b)):
+        pieces_b = [rows_b, second_b, first_b, part]
+        output = inverse(table_back, pieces_b, output, series_count, half, count_a, start)
+    return output
 
 
 def solution(mesh):

time: 71.1 us -> 70.7 us (level)
  waiting for transfers between devices: 17.8 us -> 13.8 us
  starting transfers between devices: 36.5 us -> 40.1 us
    ppermute x23 -> x25, waiting for transfers between devices: 15.4 us -> 11.4 us  [to_devices(): return lax.ppermute(value, ('tm', 'head'), pairs)]
    ppermute x23 -> x25, starting transfers between devices: 35.7 us -> 39.3 us  [to_devices(): return lax.ppermute(value, ('tm', 'head'), pairs)]
    pallas_call x1, Pallas kernels: 1.9 us -> 0.52 us  [prepare(): pl.pallas_call(prepare_kernel, out_shape=[mixes] * mix_arrays + [in_vmem(...]
    pallas_call x2 -> x5, Pallas kernels: 5.01 us -> 6.17 us  [the longest x3 6.08 us: inverse(): pl.pallas_call(functools.partial(inverse_kernel, half, offset, start, pie...]
  transfers between devices with their start and end apart: 28 -> 30, of which waited for: 11 -> 10; matrix products, arithmetic and copies ran while one was open for 0% -> 0% of each run, Pallas kernels for 15% -> 15%
where the time goes in v5:
time: 70.7 us; the launch traced here: 70.5 us
  starting transfers between devices  40.1 us (57%)
  Pallas kernels  16.4 us (23%)
  waiting for transfers between devices  13.8 us (20%)
    ppermute x25, starting transfers between devices, to_devices(): return lax.ppermute(value, ('tm', 'head'), pairs)  39.3 us
    ppermute x25, waiting for transfers between devices, to_devices(): return lax.ppermute(value, ('tm', 'head'), pairs)  11.4 us
    pallas_call x2, Pallas kernels, forward(): pl.pallas_call(functools.partial(forward_kernel, first, count, offset, ha...  6.8 us
    pallas_call x3, Pallas kernels, inverse(): pl.pallas_call(functools.partial(inverse_kernel, half, offset, start, pie...  6.08 us
    pallas_call x2, Pallas kernels, mix(): pl.pallas_call(functools.partial(mix_kernel, scale, own_modes, len(arrive...  2.66 us
    ppermute x5, waiting for transfers between devices, to_core(): return lax.ppermute(value, 'head', [(0, 1), (1, 0)])  2.37 us
  transfers between devices with their start and end apart: 30, of which 10 were waited for; matrix products, arithmetic and copies ran while one was open for 0% of the time, Pallas kernels for 15%

profile of v5, /device:TPU:0, one launch (start us, length us, event | category | flops | bytes accessed | tf_op | source)
XLA Modules:
  0.0 70.5 jit_solution(16790166203398952939)
XLA Ops:
  0.0 3.7 %forward_first.1 = (bf16[4,64,512]{2,1,0:T(8,128)(2,1)S(1)}, bf16[4,64,512]{2,1,0:T(8,128)(2,1)S(1)}, f32[4,128,512]{2,1,0:T(8,128)S(1)}, bf16[256,1024]{1,0:T(8,128)(2,1)S(1)}) custom-call(s32[1,128]{1,0:T(1,128)} %bitcast.1, bf16[16,1024,512]{2,1,0:T(8,128)(2,1)} %series_ref.3), custom_call_target="tpu_custom_call" | custom-call | flops 1000 | bytes 1000 | tf_op jit(solution)/shard_map/forward_first/pallas_call | solution.py:114
  3.7 3.0 %collective-permute-start = (bf16[4,64,512]{2,1,0:T(8,128)(2,1)S(1)}, bf16[4,64,512]{2,1,0:T(8,128)(2,1)S(1)}, u32[]{:S(2)}, u32[]{:S(2)}) collective-permute-start(bf16[4,64,512]{2,1,0:T(8,128)(2,1)S(1)} %get-tuple-element.49), channel_id=1, source_target_pairs={{0,2},{1,5},{2,0},{3,7},{4,6},{5,1},{6,4},{7,3},{8,10},{9,13},{10,... | collective-permute-start | bytes 786440 | tf_op jit(solution)/shard_map/ppermute | solution.py:372
  6.8 3.1 %forward_second.1 = (bf16[4,64,512]{2,1,0:T(8,128)(2,1)S(1)}, bf16[4,64,512]{2,1,0:T(8,128)(2,1)S(1)}, f32[4,128,512]{2,1,0:T(8,128)S(1)}) custom-call(bf16[256,1024]{1,0:T(8,128)(2,1)S(1)} %get-tuple-element.42.extra_ref.table_ref, bf16[16,1024,512]{2,1,0:T(8,128)(2,1)} %series_ref.3), custom_call_target="tpu_custom_call" | custom-call | flops 1000 | bytes 1000 | tf_op jit(solution)/shard_map/forward_second/pallas_call | solution.py:114
  9.9 2.0 %collective-permute-start.2 = (bf16[4,64,512]{2,1,0:T(8,128)(2,1)S(1)}, bf16[4,64,512]{2,1,0:T(8,128)(2,1)S(1)}, u32[]{:S(2)}, u32[]{:S(2)}) collective-permute-start(bf16[4,64,512]{2,1,0:T(8,128)(2,1)S(1)} %get-tuple-element.53), channel_id=1, source_target_pairs={{0,2},{1,5},{2,0},{3,7},{4,6},{5,1},{6,4},{7,3},{8,10},{9,13},{10,... | collective-permute-start | bytes 786440 | tf_op jit(solution)/shard_map/ppermute | solution.py:372
  13.8 2.0 %collective-permute-start.6 = (bf16[4,64,512]{2,1,0:T(8,128)(2,1)S(1)}, bf16[4,64,512]{2,1,0:T(8,128)(2,1)S(1)}, u32[]{:S(2)}, u32[]{:S(2)}) collective-permute-start(bf16[4,64,512]{2,1,0:T(8,128)(2,1)S(1)} %sum_onward.2), channel_id=1, source_target_pairs={{0,4},{1,3},{2,6},{3,1},{4,0},{5,7},{6,2},{7,5},{8,12},{9,11},{10,... | collective-permute-start | bytes 786440 | tf_op jit(solution)/shard_map/ppermute | solution.py:372
  15.9 1.4 %collective-permute-done.2.arrived_ref = bf16[4,64,512]{2,1,0:T(8,128)(2,1)S(1)} collective-permute-done((bf16[4,64,512]{2,1,0:T(8,128)(2,1)S(1)}, bf16[4,64,512]{2,1,0:T(8,128)(2,1)S(1)}, u32[]{:S(2)}, u32[]{:S(2)}) %collective-permute-start.2) | collective-permute-done | bytes 262176 | tf_op jit(solution)/shard_map/ppermute | solution.py:372
  17.4 2.5 %collective-permute-start.7 = (bf16[4,64,512]{2,1,0:T(8,128)(2,1)S(1)}, bf16[4,64,512]{2,1,0:T(8,128)(2,1)S(1)}, u32[]{:S(2)}, u32[]{:S(2)}) collective-permute-start(bf16[4,64,512]{2,1,0:T(8,128)(2,1)S(1)} %get-tuple-element.58), channel_id=1, source_target_pairs={{0,2},{1,5},{2,0},{3,7},{4,6},{5,1},{6,4},{7,3},{8,10},{9,13},{10,... | collective-permute-start | bytes 786440 | tf_op jit(solution)/shard_map/ppermute | solution.py:372
  20.0 1.5 %collective-permute-start.8 = (bf16[4,64,512]{2,1,0:T(8,128)(2,1)S(1)}, bf16[4,64,512]{2,1,0:T(8,128)(2,1)S(1)}, u32[]{:S(2)}, u32[]{:S(2)}) collective-permute-start(bf16[4,64,512]{2,1,0:T(8,128)(2,1)S(1)} %sum_onward.3), channel_id=1, source_target_pairs={{0,4},{1,3},{2,6},{3,1},{4,0},{5,7},{6,2},{7,5},{8,12},{9,11},{10,... | collective-permute-start | bytes 786440 | tf_op jit(solution)/shard_map/ppermute | solution.py:372
  21.9 4.5 %collective-permute-start.9 = (bf16[4,16,512]{2,1,0:T(8,128)(2,1)S(1)}, bf16[4,16,512]{2,1,0:T(8,128)(2,1)S(1)}, u32[]{:S(2)}, u32[]{:S(2)}) collective-permute-start(bf16[4,16,512]{2,1,0:T(8,128)(2,1)S(1)} %get-tuple-element.61), channel_id=1, source_target_pairs={{0,24},{1,25},{2,26},{3,27},{4,28},{5,29},{6,30},{7,31},{8,16},{9,... | collective-permute-start | bytes 196616 | tf_op jit(solution)/shard_map/ppermute | solution.py:372
  27.1 3.8 %collective-permute-start.13 = (bf16[4,16,512]{2,1,0:T(8,128)(2,1)S(1)}, bf16[4,16,512]{2,1,0:T(8,128)(2,1)S(1)}, u32[]{:S(2)}, u32[]{:S(2)}) collective-permute-start(bf16[4,16,512]{2,1,0:T(8,128)(2,1)S(1)} %get-tuple-element.67), channel_id=1, source_target_pairs={{0,24},{1,25},{2,26},{3,27},{4,28},{5,29},{6,30},{7,31},{8,16},{9,... | collective-permute-start | bytes 196616 | tf_op jit(solution)/shard_map/ppermute | solution.py:372
  35.6 2.4 %collective-permute-start.24 = (bf16[8,16,256]{2,1,0:T(8,128)(2,1)S(1)}, bf16[8,16,256]{2,1,0:T(8,128)(2,1)S(1)}, u32[]{:S(2)}, u32[]{:S(2)}) collective-permute-start(bf16[8,16,256]{2,1,0:T(8,128)(2,1)S(1)} %constant_dynamic-update-slice_fusion.refs_0_), channel_id=1, source_target_pairs={{0,24},{1,25},{2,26},{3,27},{4,28},{5,29},{6,30},{7,31},{8,16},{9,... | collective-permute-start | bytes 196616 | tf_op jit(solution)/shard_map/ppermute | solution.py:372
  37.9 2.0 %collective-permute-start.22 = (bf16[8,16,256]{2,1,0:T(8,128)(2,1)S(1)}, bf16[8,16,256]{2,1,0:T(8,128)(2,1)S(1)}, u32[]{:S(2)}, u32[]{:S(2)}) collective-permute-start(bf16[8,16,256]{2,1,0:T(8,128)(2,1)S(1)} %constant_dynamic-update-slice_fusion.refs_0_), channel_id=1, source_target_pairs={{0,8},{1,9},{2,10},{3,11},{4,12},{5,13},{6,14},{7,15},{8,0},{9,1},... | collective-permute-start | bytes 196616 | tf_op jit(solution)/shard_map/ppermute | solution.py:372
  42.6 2.4 %collective-permute-start.19 = (bf16[8,16,256]{2,1,0:T(8,128)(2,1)S(1)}, bf16[8,16,256]{2,1,0:T(8,128)(2,1)S(1)}, u32[]{:S(2)}, u32[]{:S(2)}) collective-permute-start(bf16[8,16,256]{2,1,0:T(8,128)(2,1)S(1)} %constant_dynamic-update-slice_fusion.2.refs_0_), channel_id=1, source_target_pairs={{0,24},{1,25},{2,26},{3,27},{4,28},{5,29},{6,30},{7,31},{8,16},{9,... | collective-permute-start | bytes 196616 | tf_op jit(solution)/shard_map/ppermute | solution.py:372
  45.0 2.0 %collective-permute-start.17 = (bf16[8,16,256]{2,1,0:T(8,128)(2,1)S(1)}, bf16[8,16,256]{2,1,0:T(8,128)(2,1)S(1)}, u32[]{:S(2)}, u32[]{:S(2)}) collective-permute-start(bf16[8,16,256]{2,1,0:T(8,128)(2,1)S(1)} %constant_dynamic-update-slice_fusion.2.refs_0_), channel_id=1, source_target_pairs={{0,8},{1,9},{2,10},{3,11},{4,12},{5,13},{6,14},{7,15},{8,0},{9,1},... | collective-permute-start | bytes 196616 | tf_op jit(solution)/shard_map/ppermute | solution.py:372
  47.0 1.8 %collective-permute-start.28 = (bf16[8,64,256]{2,1,0:T(8,128)(2,1)S(1)}, bf16[8,64,256]{2,1,0:T(8,128)(2,1)S(1)}, u32[]{:S(2)}, u32[]{:S(2)}) collective-permute-start(bf16[8,64,256]{2,1,0:T(8,128)(2,1)S(1)} %join_rows.3.refs_0_), channel_id=1, source_target_pairs={{0,4},{1,3},{2,6},{3,1},{4,0},{5,7},{6,2},{7,5},{8,12},{9,11},{10,... | collective-permute-start | bytes 786440 | tf_op jit(solution)/shard_map/ppermute | solution.py:372
  48.8 1.5 %collective-permute-start.25 = (bf16[8,64,256]{2,1,0:T(8,128)(2,1)S(1)}, bf16[8,64,256]{2,1,0:T(8,128)(2,1)S(1)}, u32[]{:S(2)}, u32[]{:S(2)}) collective-permute-start(bf16[8,64,256]{2,1,0:T(8,128)(2,1)S(1)} %join_rows.3.refs_0_), channel_id=1, source_target_pairs={{0,2},{1,5},{2,0},{3,7},{4,6},{5,1},{6,4},{7,3},{8,10},{9,13},{10,... | collective-permute-start | bytes 786440 | tf_op jit(solution)/shard_map/ppermute | solution.py:372
  51.4 1.8 %collective-permute-start.20 = (bf16[8,64,256]{2,1,0:T(8,128)(2,1)S(1)}, bf16[8,64,256]{2,1,0:T(8,128)(2,1)S(1)}, u32[]{:S(2)}, u32[]{:S(2)}) collective-permute-start(bf16[8,64,256]{2,1,0:T(8,128)(2,1)S(1)} %join_rows.2.refs_0_), channel_id=1, source_target_pairs={{0,4},{1,3},{2,6},{3,1},{4,0},{5,7},{6,2},{7,5},{8,12},{9,11},{10,... | collective-permute-start | bytes 786440 | tf_op jit(solution)/shard_map/ppermute | solution.py:372
  53.1 1.5 %collective-permute-start.21 = (bf16[8,64,256]{2,1,0:T(8,128)(2,1)S(1)}, bf16[8,64,256]{2,1,0:T(8,128)(2,1)S(1)}, u32[]{:S(2)}, u32[]{:S(2)}) collective-permute-start(bf16[8,64,256]{2,1,0:T(8,128)(2,1)S(1)} %join_rows.2.refs_0_), channel_id=1, source_target_pairs={{0,2},{1,5},{2,0},{3,7},{4,6},{5,1},{6,4},{7,3},{8,10},{9,13},{10,... | collective-permute-start | bytes 786440 | tf_op jit(solution)/shard_map/ppermute | solution.py:372
  54.6 1.6 %collective-permute-done.28.refs_1_ = bf16[8,64,256]{2,1,0:T(8,128)(2,1)S(1)} collective-permute-done((bf16[8,64,256]{2,1,0:T(8,128)(2,1)S(1)}, bf16[8,64,256]{2,1,0:T(8,128)(2,1)S(1)}, u32[]{:S(2)}, u32[]{:S(2)}) %collective-permute-start.28) | collective-permute-done | bytes 262176 | tf_op jit(solution)/shard_map/ppermute | solution.py:372
  56.8 5.0 %collective-permute-done.20.refs_1_ = bf16[8,64,256]{2,1,0:T(8,128)(2,1)S(1)} collective-permute-done((bf16[8,64,256]{2,1,0:T(8,128)(2,1)S(1)}, bf16[8,64,256]{2,1,0:T(8,128)(2,1)S(1)}, u32[]{:S(2)}, u32[]{:S(2)}) %collective-permute-start.20) | collective-permute-done | bytes 262176 | tf_op jit(solution)/shard_map/ppermute | solution.py:372
  62.5 1.4 %collective-permute-start.26 = (bf16[4,64,256]{2,1,0:T(8,128)(2,1)S(1)}, bf16[4,64,256]{2,1,0:T(8,128)(2,1)S(1)}, u32[]{:S(2)}, u32[]{:S(2)}) collective-permute-start(bf16[4,64,256]{2,1,0:T(8,128)(2,1)S(1)} %get-tuple-element.76), channel_id=1, source_target_pairs={{0,2},{1,5},{2,0},{3,7},{4,6},{5,1},{6,4},{7,3},{8,10},{9,13},{10,... | collective-permute-start | bytes 393224 | tf_op jit(solution)/shard_map/ppermute | solution.py:372
  64.0 2.5 %inverse_first.1.refs_4_ = bf16[16,1024,256]{2,1,0:T(8,128)(2,1)} custom-call(bf16[1024,256]{1,0:T(8,128)(2,1)S(1)} %get-tuple-element.43.table_ref, bf16[8,64,256]{2,1,0:T(8,128)(2,1)S(1)} %join_rows.3.refs_0_, bf16[8,64,256]{2,1,0:T(8,128)(2,1)S(1)} %collective-permute-done.28.refs_1_, bf16[8,64,256]{2,1,0:T(8,128)(2,1)S(1)} %collective-permute-done.25.refs_2_, ...), custom_call_target="tpu_custom_call" | custom-call | flops 1000 | bytes 1000 | tf_op jit(solution)/shard_map/inverse_first/pallas_call | solution.py:357
  66.9 1.8 %inverse_next.2.refs_4_ = bf16[16,1024,256]{2,1,0:T(8,128)(2,1)} custom-call(bf16[1024,256]{1,0:T(8,128)(2,1)S(1)} %get-tuple-element.43.table_ref, bf16[8,64,256]{2,1,0:T(8,128)(2,1)S(1)} %join_rows.2.refs_0_, bf16[8,64,256]{2,1,0:T(8,128)(2,1)S(1)} %collective-permute-done.20.refs_1_, ...), custom_call_target="tpu_custom_call", output_to_operand_aliasing={{}: (5, {})} | custom-call | flops 1000 | bytes 1000 | tf_op jit(solution)/shard_map/inverse_next/pallas_call | solution.py:357
  68.7 1.8 %inverse_next.3 = bf16[16,1024,256]{2,1,0:T(8,128)(2,1)} custom-call(bf16[1024,256]{1,0:T(8,128)(2,1)S(1)} %get-tuple-element.43.table_ref, bf16[8,64,256]{2,1,0:T(8,128)(2,1)S(1)} %join_rows.2.refs_0_, bf16[8,64,256]{2,1,0:T(8,128)(2,1)S(1)} %collective-permute-done.20.refs_1_, ...), custom_call_target="tpu_custom_call", output_to_operand_aliasing={{}: (5, {})} | custom-call | flops 1000 | bytes 1000 | tf_op jit(solution)/shard_map/inverse_next/pallas_call | solution.py:357
  (63 shorter events, 13.2 us)
Async XLA Ops:
  3.7 9.4 %collective-permute-start = (bf16[4,64,512]{2,1,0:T(8,128)(2,1)S(1)}, bf16[4,64,512]{2,1,0:T(8,128)(2,1)S(1)}, u32[]{:S(2)}, u32[]{:S(2)}) collective-permute-start(bf16[4,64,512]{2,1,0:T(8,128)(2,1)S(1)} %get-tuple-element.49), channel_id=1, source_target_pairs={{0,2},{1,5},{2,0},{3,7},{4,6},{5,1},{6,4},{7,3},{8,10},{9,13},{10,... | collective-permute-start | bytes 786440 | tf_op jit(solution)/shard_map/ppermute | solution.py:372
  6.7 7.2 %collective-permute-start.1 = (bf16[4,64,512]{2,1,0:T(8,128)(2,1)S(1)}, bf16[4,64,512]{2,1,0:T(8,128)(2,1)S(1)}, u32[]{:S(2)}, u32[]{:S(2)}) collective-permute-start(bf16[4,64,512]{2,1,0:T(8,128)(2,1)S(1)} %get-tuple-element.51), channel_id=1, source_target_pairs={{0,2},{1,5},{2,0},{3,7},{4,6},{5,1},{6,4},{7,3},{8,10},{9,13},{10,... | collective-permute-start | bytes 786440 | tf_op jit(solution)/shard_map/ppermute | solution.py:372
  9.9 7.5 %collective-permute-start.2 = (bf16[4,64,512]{2,1,0:T(8,128)(2,1)S(1)}, bf16[4,64,512]{2,1,0:T(8,128)(2,1)S(1)}, u32[]{:S(2)}, u32[]{:S(2)}) collective-permute-start(bf16[4,64,512]{2,1,0:T(8,128)(2,1)S(1)} %get-tuple-element.53), channel_id=1, source_target_pairs={{0,2},{1,5},{2,0},{3,7},{4,6},{5,1},{6,4},{7,3},{8,10},{9,13},{10,... | collective-permute-start | bytes 786440 | tf_op jit(solution)/shard_map/ppermute | solution.py:372
  12.5 7.5 %collective-permute-start.3 = (bf16[2048,128]{1,0:T(8,128)(2,1)S(1)}, bf16[2048,128]{1,0:T(8,128)(2,1)S(1)}, u32[]{:S(2)}, u32[]{:S(2)}) collective-permute-start(bf16[2048,128]{1,0:T(8,128)(2,1)S(1)} %get-tuple-element.45.refs_3_), channel_id=1, source_target_pairs={{0,1},{1,0},{2,3},{3,2},{4,5},{5,4},{6,7},{7,6},{8,9},{9,8},{10,11... | collective-permute-start | bytes 1572872 | tf_op jit(solution)/shard_map/ppermute | solution.py:379
  12.5 9.0 %collective-permute-start.4 = (bf16[2048,128]{1,0:T(8,128)(2,1)S(1)}, bf16[2048,128]{1,0:T(8,128)(2,1)S(1)}, u32[]{:S(2)}, u32[]{:S(2)}) collective-permute-start(bf16[2048,128]{1,0:T(8,128)(2,1)S(1)} %get-tuple-element.46.refs_4_), channel_id=1, source_target_pairs={{0,1},{1,0},{2,3},{3,2},{4,5},{5,4},{6,7},{7,6},{8,9},{9,8},{10,11... | collective-permute-start | bytes 1572872 | tf_op jit(solution)/shard_map/ppermute | solution.py:379
  13.0 8.5 %collective-permute-start.5 = (bf16[2048,128]{1,0:T(8,128)(2,1)S(1)}, bf16[2048,128]{1,0:T(8,128)(2,1)S(1)}, u32[]{:S(2)}, u32[]{:S(2)}) collective-permute-start(bf16[2048,128]{1,0:T(8,128)(2,1)S(1)} %get-tuple-element.47.refs_5_), channel_id=1, source_target_pairs={{0,1},{1,0},{2,3},{3,2},{4,5},{5,4},{6,7},{7,6},{8,9},{9,8},{10,11... | collective-permute-start | bytes 1572872 | tf_op jit(solution)/shard_map/ppermute | solution.py:379
  13.8 8.0 %collective-permute-start.6 = (bf16[4,64,512]{2,1,0:T(8,128)(2,1)S(1)}, bf16[4,64,512]{2,1,0:T(8,128)(2,1)S(1)}, u32[]{:S(2)}, u32[]{:S(2)}) collective-permute-start(bf16[4,64,512]{2,1,0:T(8,128)(2,1)S(1)} %sum_onward.2), channel_id=1, source_target_pairs={{0,4},{1,3},{2,6},{3,1},{4,0},{5,7},{6,2},{7,5},{8,12},{9,11},{10,... | collective-permute-start | bytes 786440 | tf_op jit(solution)/shard_map/ppermute | solution.py:372
  17.4 9.6 %collective-permute-start.7 = (bf16[4,64,512]{2,1,0:T(8,128)(2,1)S(1)}, bf16[4,64,512]{2,1,0:T(8,128)(2,1)S(1)}, u32[]{:S(2)}, u32[]{:S(2)}) collective-permute-start(bf16[4,64,512]{2,1,0:T(8,128)(2,1)S(1)} %get-tuple-element.58), channel_id=1, source_target_pairs={{0,2},{1,5},{2,0},{3,7},{4,6},{5,1},{6,4},{7,3},{8,10},{9,13},{10,... | collective-permute-start | bytes 786440 | tf_op jit(solution)/shard_map/ppermute | solution.py:372
  20.0 7.1 %collective-permute-start.8 = (bf16[4,64,512]{2,1,0:T(8,128)(2,1)S(1)}, bf16[4,64,512]{2,1,0:T(8,128)(2,1)S(1)}, u32[]{:S(2)}, u32[]{:S(2)}) collective-permute-start(bf16[4,64,512]{2,1,0:T(8,128)(2,1)S(1)} %sum_onward.3), channel_id=1, source_target_pairs={{0,4},{1,3},{2,6},{3,1},{4,0},{5,7},{6,2},{7,5},{8,12},{9,11},{10,... | collective-permute-start | bytes 786440 | tf_op jit(solution)/shard_map/ppermute | solution.py:372
  21.9 9.1 %collective-permute-start.9 = (bf16[4,16,512]{2,1,0:T(8,128)(2,1)S(1)}, bf16[4,16,512]{2,1,0:T(8,128)(2,1)S(1)}, u32[]{:S(2)}, u32[]{:S(2)}) collective-permute-start(bf16[4,16,512]{2,1,0:T(8,128)(2,1)S(1)} %get-tuple-element.61), channel_id=1, source_target_pairs={{0,24},{1,25},{2,26},{3,27},{4,28},{5,29},{6,30},{7,31},{8,16},{9,... | collective-permute-start | bytes 196616 | tf_op jit(solution)/shard_map/ppermute | solution.py:372
  26.4 6.6 %collective-permute-start.10 = (bf16[4,16,512]{2,1,0:T(8,128)(2,1)S(1)}, bf16[4,16,512]{2,1,0:T(8,128)(2,1)S(1)}, u32[]{:S(2)}, u32[]{:S(2)}) collective-permute-start(bf16[4,16,512]{2,1,0:T(8,128)(2,1)S(1)} %get-tuple-element.62), channel_id=1, source_target_pairs={{0,16},{1,17},{2,18},{3,19},{4,20},{5,21},{6,22},{7,23},{8,24},{9,... | collective-permute-start | bytes 196616 | tf_op jit(solution)/shard_map/ppermute | solution.py:372
  26.4 6.6 %collective-permute-start.11 = (bf16[4,16,512]{2,1,0:T(8,128)(2,1)S(1)}, bf16[4,16,512]{2,1,0:T(8,128)(2,1)S(1)}, u32[]{:S(2)}, u32[]{:S(2)}) collective-permute-start(bf16[4,16,512]{2,1,0:T(8,128)(2,1)S(1)} %get-tuple-element.63), channel_id=1, source_target_pairs={{0,8},{1,9},{2,10},{3,11},{4,12},{5,13},{6,14},{7,15},{8,0},{9,1},... | collective-permute-start | bytes 196616 | tf_op jit(solution)/shard_map/ppermute | solution.py:372
  27.1 10.8 %collective-permute-start.13 = (bf16[4,16,512]{2,1,0:T(8,128)(2,1)S(1)}, bf16[4,16,512]{2,1,0:T(8,128)(2,1)S(1)}, u32[]{:S(2)}, u32[]{:S(2)}) collective-permute-start(bf16[4,16,512]{2,1,0:T(8,128)(2,1)S(1)} %get-tuple-element.67), channel_id=1, source_target_pairs={{0,24},{1,25},{2,26},{3,27},{4,28},{5,29},{6,30},{7,31},{8,16},{9,... | collective-permute-start | bytes 196616 | tf_op jit(solution)/shard_map/ppermute | solution.py:372
  30.9 9.0 %collective-permute-start.14 = (bf16[4,16,512]{2,1,0:T(8,128)(2,1)S(1)}, bf16[4,16,512]{2,1,0:T(8,128)(2,1)S(1)}, u32[]{:S(2)}, u32[]{:S(2)}) collective-permute-start(bf16[4,16,512]{2,1,0:T(8,128)(2,1)S(1)} %get-tuple-element.68), channel_id=1, source_target_pairs={{0,16},{1,17},{2,18},{3,19},{4,20},{5,21},{6,22},{7,23},{8,24},{9,... | collective-permute-start | bytes 196616 | tf_op jit(solution)/shard_map/ppermute | solution.py:372
  30.9 9.0 %collective-permute-start.15 = (bf16[4,16,512]{2,1,0:T(8,128)(2,1)S(1)}, bf16[4,16,512]{2,1,0:T(8,128)(2,1)S(1)}, u32[]{:S(2)}, u32[]{:S(2)}) collective-permute-start(bf16[4,16,512]{2,1,0:T(8,128)(2,1)S(1)} %get-tuple-element.69), channel_id=1, source_target_pairs={{0,8},{1,9},{2,10},{3,11},{4,12},{5,13},{6,14},{7,15},{8,0},{9,1},... | collective-permute-start | bytes 196616 | tf_op jit(solution)/shard_map/ppermute | solution.py:372
  35.6 9.4 %collective-permute-start.24 = (bf16[8,16,256]{2,1,0:T(8,128)(2,1)S(1)}, bf16[8,16,256]{2,1,0:T(8,128)(2,1)S(1)}, u32[]{:S(2)}, u32[]{:S(2)}) collective-permute-start(bf16[8,16,256]{2,1,0:T(8,128)(2,1)S(1)} %constant_dynamic-update-slice_fusion.refs_0_), channel_id=1, source_target_pairs={{0,24},{1,25},{2,26},{3,27},{4,28},{5,29},{6,30},{7,31},{8,16},{9,... | collective-permute-start | bytes 196616 | tf_op jit(solution)/shard_map/ppermute | solution.py:372
  37.9 9.0 %collective-permute-start.23 = (bf16[8,16,256]{2,1,0:T(8,128)(2,1)S(1)}, bf16[8,16,256]{2,1,0:T(8,128)(2,1)S(1)}, u32[]{:S(2)}, u32[]{:S(2)}) collective-permute-start(bf16[8,16,256]{2,1,0:T(8,128)(2,1)S(1)} %constant_dynamic-update-slice_fusion.refs_0_), channel_id=1, source_target_pairs={{0,16},{1,17},{2,18},{3,19},{4,20},{5,21},{6,22},{7,23},{8,24},{9,... | collective-permute-start | bytes 196616 | tf_op jit(solution)/shard_map/ppermute | solution.py:372
  37.9 9.0 %collective-permute-start.22 = (bf16[8,16,256]{2,1,0:T(8,128)(2,1)S(1)}, bf16[8,16,256]{2,1,0:T(8,128)(2,1)S(1)}, u32[]{:S(2)}, u32[]{:S(2)}) collective-permute-start(bf16[8,16,256]{2,1,0:T(8,128)(2,1)S(1)} %constant_dynamic-update-slice_fusion.refs_0_), channel_id=1, source_target_pairs={{0,8},{1,9},{2,10},{3,11},{4,12},{5,13},{6,14},{7,15},{8,0},{9,1},... | collective-permute-start | bytes 196616 | tf_op jit(solution)/shard_map/ppermute | solution.py:372
  42.6 7.7 %collective-permute-start.19 = (bf16[8,16,256]{2,1,0:T(8,128)(2,1)S(1)}, bf16[8,16,256]{2,1,0:T(8,128)(2,1)S(1)}, u32[]{:S(2)}, u32[]{:S(2)}) collective-permute-start(bf16[8,16,256]{2,1,0:T(8,128)(2,1)S(1)} %constant_dynamic-update-slice_fusion.2.refs_0_), channel_id=1, source_target_pairs={{0,24},{1,25},{2,26},{3,27},{4,28},{5,29},{6,30},{7,31},{8,16},{9,... | collective-permute-start | bytes 196616 | tf_op jit(solution)/shard_map/ppermute | solution.py:372
  47.0 9.2 %collective-permute-start.28 = (bf16[8,64,256]{2,1,0:T(8,128)(2,1)S(1)}, bf16[8,64,256]{2,1,0:T(8,128)(2,1)S(1)}, u32[]{:S(2)}, u32[]{:S(2)}) collective-permute-start(bf16[8,64,256]{2,1,0:T(8,128)(2,1)S(1)} %join_rows.3.refs_0_), channel_id=1, source_target_pairs={{0,4},{1,3},{2,6},{3,1},{4,0},{5,7},{6,2},{7,5},{8,12},{9,11},{10,... | collective-permute-start | bytes 786440 | tf_op jit(solution)/shard_map/ppermute | solution.py:372
  48.8 8.1 %collective-permute-start.25 = (bf16[8,64,256]{2,1,0:T(8,128)(2,1)S(1)}, bf16[8,64,256]{2,1,0:T(8,128)(2,1)S(1)}, u32[]{:S(2)}, u32[]{:S(2)}) collective-permute-start(bf16[8,64,256]{2,1,0:T(8,128)(2,1)S(1)} %join_rows.3.refs_0_), channel_id=1, source_target_pairs={{0,2},{1,5},{2,0},{3,7},{4,6},{5,1},{6,4},{7,3},{8,10},{9,13},{10,... | collective-permute-start | bytes 786440 | tf_op jit(solution)/shard_map/ppermute | solution.py:372
  51.4 10.5 %collective-permute-start.20 = (bf16[8,64,256]{2,1,0:T(8,128)(2,1)S(1)}, bf16[8,64,256]{2,1,0:T(8,128)(2,1)S(1)}, u32[]{:S(2)}, u32[]{:S(2)}) collective-permute-start(bf16[8,64,256]{2,1,0:T(8,128)(2,1)S(1)} %join_rows.2.refs_0_), channel_id=1, source_target_pairs={{0,4},{1,3},{2,6},{3,1},{4,0},{5,7},{6,2},{7,5},{8,12},{9,11},{10,... | collective-permute-start | bytes 786440 | tf_op jit(solution)/shard_map/ppermute | solution.py:372
  53.1 13.4 %collective-permute-start.21 = (bf16[8,64,256]{2,1,0:T(8,128)(2,1)S(1)}, bf16[8,64,256]{2,1,0:T(8,128)(2,1)S(1)}, u32[]{:S(2)}, u32[]{:S(2)}) collective-permute-start(bf16[8,64,256]{2,1,0:T(8,128)(2,1)S(1)} %join_rows.2.refs_0_), channel_id=1, source_target_pairs={{0,2},{1,5},{2,0},{3,7},{4,6},{5,1},{6,4},{7,3},{8,10},{9,13},{10,... | collective-permute-start | bytes 786440 | tf_op jit(solution)/shard_map/ppermute | solution.py:372
  56.2 7.7 %collective-permute-start.29 = (bf16[8,64,256]{2,1,0:T(8,128)(2,1)S(1)}, bf16[8,64,256]{2,1,0:T(8,128)(2,1)S(1)}, u32[]{:S(2)}, u32[]{:S(2)}) collective-permute-start(bf16[8,64,256]{2,1,0:T(8,128)(2,1)S(1)} %collective-permute-done.28.refs_1_), channel_id=1, source_target_pairs={{0,2},{1,5},{2,0},{3,7},{4,6},{5,1},{6,4},{7,3},{8,10},{9,13},{10,... | collective-permute-start | bytes 786440 | tf_op jit(solution)/shard_map/ppermute | solution.py:372
  (9 other events, 42.0 us)

commit v6 on v5

--- a/solution.py
+++ b/solution.py
@@ -261,7 +261,7 @@
         [total[:, :own_modes].reshape(rows, width), total[:, own_modes:].reshape(rows, width)], axis=0
     ))
     lower = lax.broadcasted_iota(jnp.int32, (rows, 128), 1) < 64
-    row_mode = lax.broadcasted_iota(jnp.int32, (2 * rows, 128), 0) & (own_modes - 1)
+    row_mode = lax.broadcasted_iota(jnp.int32, (rows, 128), 0) & (own_modes - 1)
     mixed, out_weights = [], []
     for packed in (packed_refs[:each], packed_refs[each:]):
         mixes, query, out_weight = packed_parts(packed, half // 64, width)
@@ -277,19 +277,19 @@
             ]
             heads = []
             for which in range(2):
-                spread = split_rows(both[which])
+                spread = both[which].astype(bf16)
                 zero = jnp.zeros_like(spread)
                 spread = jnp.concatenate([jnp.where(row_mode == k, spread, zero) for k in range(own_modes)], axis=1)
-                heads.append(fold_rows(jnp.dot(spread, mixes[2 * pair + which], preferred_element_type=f32)))
+                heads.append(jnp.dot(spread, mixes[2 * pair + which], preferred_element_type=f32))
             mixed_real.append(jnp.where(lower, heads[0], pltpu.roll(heads[1], 64, 1)))
             mixed_imag.append(jnp.where(lower, pltpu.roll(heads[0], 64, 1), heads[1]))
         both = jnp.concatenate([jnp.concatenate(mixed_real, axis=1), jnp.concatenate(mixed_imag, axis=1)], axis=0)
-        mixed.append(split_rows(both))
+        mixed.append(both.astype(bf16))
     first = jnp.where(core == 0, mixed[0], mixed[1])
     second = jnp.where(core == 0, mixed[1], mixed[0])
     both = jnp.concatenate([first, second], axis=1)
     for out_weight, out_ref in zip(out_weights, (here_ref, there_ref)):
-        result = fold_rows(jnp.dot(both, out_weight, preferred_element_type=f32)).astype(bf16)
+        result = jnp.dot(both, out_weight, preferred_element_type=f32).astype(bf16)
         out_ref[...] = jnp.concatenate(
             [result[:rows].reshape(count, own_modes, half), result[rows:].reshape(count, own_modes, half)], axis=1
         )

time: 70.7 us -> 70.5 us (level)
  no operation moved by 1% of the time
where the time goes in v6:
time: 70.5 us; the launch traced here: 70.3 us
  starting transfers between devices  40.1 us (57%)
  Pallas kernels  16.2 us (23%)
  waiting for transfers between devices  13.7 us (19%)
    ppermute x25, starting transfers between devices, to_devices(): return lax.ppermute(value, ('tm', 'head'), pairs)  39.4 us
    ppermute x25, waiting for transfers between devices, to_devices(): return lax.ppermute(value, ('tm', 'head'), pairs)  11.4 us
    pallas_call x2, Pallas kernels, forward(): pl.pallas_call(functools.partial(forward_kernel, first, count, offset, ha...  6.8 us
    pallas_call x3, Pallas kernels, inverse(): pl.pallas_call(functools.partial(inverse_kernel, half, offset, start, pie...  6.08 us
    pallas_call x2, Pallas kernels, mix(): pl.pallas_call(functools.partial(mix_kernel, scale, own_modes, len(arrive...  2.5 us
    ppermute x5, waiting for transfers between devices, to_core(): return lax.ppermute(value, 'head', [(0, 1), (1, 0)])  2.37 us
  transfers between devices with their start and end apart: 30, of which 10 were waited for; matrix products, arithmetic and copies ran while one was open for 0% of the time, Pallas kernels for 15%

profile of v6, /device:TPU:0, one launch (start us, length us, event | category | flops | bytes accessed | tf_op | source)
XLA Modules:
  0.0 70.3 jit_solution(17806986903335221209)
XLA Ops:
  0.0 3.7 %forward_first.1 = (bf16[4,64,512]{2,1,0:T(8,128)(2,1)S(1)}, bf16[4,64,512]{2,1,0:T(8,128)(2,1)S(1)}, f32[4,128,512]{2,1,0:T(8,128)S(1)}, bf16[256,1024]{1,0:T(8,128)(2,1)S(1)}) custom-call(s32[1,128]{1,0:T(1,128)} %bitcast.1, bf16[16,1024,512]{2,1,0:T(8,128)(2,1)} %series_ref.3), custom_call_target="tpu_custom_call" | custom-call | flops 1000 | bytes 1000 | tf_op jit(solution)/shard_map/forward_first/pallas_call | solution.py:114
  3.7 3.0 %collective-permute-start = (bf16[4,64,512]{2,1,0:T(8,128)(2,1)S(1)}, bf16[4,64,512]{2,1,0:T(8,128)(2,1)S(1)}, u32[]{:S(2)}, u32[]{:S(2)}) collective-permute-start(bf16[4,64,512]{2,1,0:T(8,128)(2,1)S(1)} %get-tuple-element.49), channel_id=1, source_target_pairs={{0,2},{1,5},{2,0},{3,7},{4,6},{5,1},{6,4},{7,3},{8,10},{9,13},{10,... | collective-permute-start | bytes 786440 | tf_op jit(solution)/shard_map/ppermute | solution.py:372
  6.8 3.1 %forward_second.1 = (bf16[4,64,512]{2,1,0:T(8,128)(2,1)S(1)}, bf16[4,64,512]{2,1,0:T(8,128)(2,1)S(1)}, f32[4,128,512]{2,1,0:T(8,128)S(1)}) custom-call(bf16[256,1024]{1,0:T(8,128)(2,1)S(1)} %get-tuple-element.42.extra_ref.table_ref, bf16[16,1024,512]{2,1,0:T(8,128)(2,1)} %series_ref.3), custom_call_target="tpu_custom_call" | custom-call | flops 1000 | bytes 1000 | tf_op jit(solution)/shard_map/forward_second/pallas_call | solution.py:114
  9.9 2.0 %collective-permute-start.2 = (bf16[4,64,512]{2,1,0:T(8,128)(2,1)S(1)}, bf16[4,64,512]{2,1,0:T(8,128)(2,1)S(1)}, u32[]{:S(2)}, u32[]{:S(2)}) collective-permute-start(bf16[4,64,512]{2,1,0:T(8,128)(2,1)S(1)} %get-tuple-element.53), channel_id=1, source_target_pairs={{0,2},{1,5},{2,0},{3,7},{4,6},{5,1},{6,4},{7,3},{8,10},{9,13},{10,... | collective-permute-start | bytes 786440 | tf_op jit(solution)/shard_map/ppermute | solution.py:372
  13.8 2.0 %collective-permute-start.6 = (bf16[4,64,512]{2,1,0:T(8,128)(2,1)S(1)}, bf16[4,64,512]{2,1,0:T(8,128)(2,1)S(1)}, u32[]{:S(2)}, u32[]{:S(2)}) collective-permute-start(bf16[4,64,512]{2,1,0:T(8,128)(2,1)S(1)} %sum_onward.2), channel_id=1, source_target_pairs={{0,4},{1,3},{2,6},{3,1},{4,0},{5,7},{6,2},{7,5},{8,12},{9,11},{10,... | collective-permute-start | bytes 786440 | tf_op jit(solution)/shard_map/ppermute | solution.py:372
  15.9 1.4 %collective-permute-done.2.arrived_ref = bf16[4,64,512]{2,1,0:T(8,128)(2,1)S(1)} collective-permute-done((bf16[4,64,512]{2,1,0:T(8,128)(2,1)S(1)}, bf16[4,64,512]{2,1,0:T(8,128)(2,1)S(1)}, u32[]{:S(2)}, u32[]{:S(2)}) %collective-permute-start.2) | collective-permute-done | bytes 262176 | tf_op jit(solution)/shard_map/ppermute | solution.py:372
  17.4 2.5 %collective-permute-start.7 = (bf16[4,64,512]{2,1,0:T(8,128)(2,1)S(1)}, bf16[4,64,512]{2,1,0:T(8,128)(2,1)S(1)}, u32[]{:S(2)}, u32[]{:S(2)}) collective-permute-start(bf16[4,64,512]{2,1,0:T(8,128)(2,1)S(1)} %get-tuple-element.58), channel_id=1, source_target_pairs={{0,2},{1,5},{2,0},{3,7},{4,6},{5,1},{6,4},{7,3},{8,10},{9,13},{10,... | collective-permute-start | bytes 786440 | tf_op jit(solution)/shard_map/ppermute | solution.py:372
  20.0 1.5 %collective-permute-start.8 = (bf16[4,64,512]{2,1,0:T(8,128)(2,1)S(1)}, bf16[4,64,512]{2,1,0:T(8,128)(2,1)S(1)}, u32[]{:S(2)}, u32[]{:S(2)}) collective-permute-start(bf16[4,64,512]{2,1,0:T(8,128)(2,1)S(1)} %sum_onward.3), channel_id=1, source_target_pairs={{0,4},{1,3},{2,6},{3,1},{4,0},{5,7},{6,2},{7,5},{8,12},{9,11},{10,... | collective-permute-start | bytes 786440 | tf_op jit(solution)/shard_map/ppermute | solution.py:372
  21.9 4.5 %collective-permute-start.9 = (bf16[4,16,512]{2,1,0:T(8,128)(2,1)S(1)}, bf16[4,16,512]{2,1,0:T(8,128)(2,1)S(1)}, u32[]{:S(2)}, u32[]{:S(2)}) collective-permute-start(bf16[4,16,512]{2,1,0:T(8,128)(2,1)S(1)} %get-tuple-element.61), channel_id=1, source_target_pairs={{0,24},{1,25},{2,26},{3,27},{4,28},{5,29},{6,30},{7,31},{8,16},{9,... | collective-permute-start | bytes 196616 | tf_op jit(solution)/shard_map/ppermute | solution.py:372
  27.1 3.8 %collective-permute-start.13 = (bf16[4,16,512]{2,1,0:T(8,128)(2,1)S(1)}, bf16[4,16,512]{2,1,0:T(8,128)(2,1)S(1)}, u32[]{:S(2)}, u32[]{:S(2)}) collective-permute-start(bf16[4,16,512]{2,1,0:T(8,128)(2,1)S(1)} %get-tuple-element.67), channel_id=1, source_target_pairs={{0,24},{1,25},{2,26},{3,27},{4,28},{5,29},{6,30},{7,31},{8,16},{9,... | collective-permute-start | bytes 196616 | tf_op jit(solution)/shard_map/ppermute | solution.py:372
  35.5 2.4 %collective-permute-start.24 = (bf16[8,16,256]{2,1,0:T(8,128)(2,1)S(1)}, bf16[8,16,256]{2,1,0:T(8,128)(2,1)S(1)}, u32[]{:S(2)}, u32[]{:S(2)}) collective-permute-start(bf16[8,16,256]{2,1,0:T(8,128)(2,1)S(1)} %constant_dynamic-update-slice_fusion.refs_0_), channel_id=1, source_target_pairs={{0,24},{1,25},{2,26},{3,27},{4,28},{5,29},{6,30},{7,31},{8,16},{9,... | collective-permute-start | bytes 196616 | tf_op jit(solution)/shard_map/ppermute | solution.py:372
  37.9 2.0 %collective-permute-start.22 = (bf16[8,16,256]{2,1,0:T(8,128)(2,1)S(1)}, bf16[8,16,256]{2,1,0:T(8,128)(2,1)S(1)}, u32[]{:S(2)}, u32[]{:S(2)}) collective-permute-start(bf16[8,16,256]{2,1,0:T(8,128)(2,1)S(1)} %constant_dynamic-update-slice_fusion.refs_0_), channel_id=1, source_target_pairs={{0,8},{1,9},{2,10},{3,11},{4,12},{5,13},{6,14},{7,15},{8,0},{9,1},... | collective-permute-start | bytes 196616 | tf_op jit(solution)/shard_map/ppermute | solution.py:372
  42.4 2.4 %collective-permute-start.19 = (bf16[8,16,256]{2,1,0:T(8,128)(2,1)S(1)}, bf16[8,16,256]{2,1,0:T(8,128)(2,1)S(1)}, u32[]{:S(2)}, u32[]{:S(2)}) collective-permute-start(bf16[8,16,256]{2,1,0:T(8,128)(2,1)S(1)} %constant_dynamic-update-slice_fusion.2.refs_0_), channel_id=1, source_target_pairs={{0,24},{1,25},{2,26},{3,27},{4,28},{5,29},{6,30},{7,31},{8,16},{9,... | collective-permute-start | bytes 196616 | tf_op jit(solution)/shard_map/ppermute | solution.py:372
  44.8 2.0 %collective-permute-start.17 = (bf16[8,16,256]{2,1,0:T(8,128)(2,1)S(1)}, bf16[8,16,256]{2,1,0:T(8,128)(2,1)S(1)}, u32[]{:S(2)}, u32[]{:S(2)}) collective-permute-start(bf16[8,16,256]{2,1,0:T(8,128)(2,1)S(1)} %constant_dynamic-update-slice_fusion.2.refs_0_), channel_id=1, source_target_pairs={{0,8},{1,9},{2,10},{3,11},{4,12},{5,13},{6,14},{7,15},{8,0},{9,1},... | collective-permute-start | bytes 196616 | tf_op jit(solution)/shard_map/ppermute | solution.py:372
  46.8 1.8 %collective-permute-start.28 = (bf16[8,64,256]{2,1,0:T(8,128)(2,1)S(1)}, bf16[8,64,256]{2,1,0:T(8,128)(2,1)S(1)}, u32[]{:S(2)}, u32[]{:S(2)}) collective-permute-start(bf16[8,64,256]{2,1,0:T(8,128)(2,1)S(1)} %join_rows.3.refs_0_), channel_id=1, source_target_pairs={{0,4},{1,3},{2,6},{3,1},{4,0},{5,7},{6,2},{7,5},{8,12},{9,11},{10,... | collective-permute-start | bytes 786440 | tf_op jit(solution)/shard_map/ppermute | solution.py:372
  48.6 1.5 %collective-permute-start.25 = (bf16[8,64,256]{2,1,0:T(8,128)(2,1)S(1)}, bf16[8,64,256]{2,1,0:T(8,128)(2,1)S(1)}, u32[]{:S(2)}, u32[]{:S(2)}) collective-permute-start(bf16[8,64,256]{2,1,0:T(8,128)(2,1)S(1)} %join_rows.3.refs_0_), channel_id=1, source_target_pairs={{0,2},{1,5},{2,0},{3,7},{4,6},{5,1},{6,4},{7,3},{8,10},{9,13},{10,... | collective-permute-start | bytes 786440 | tf_op jit(solution)/shard_map/ppermute | solution.py:372
  51.2 1.8 %collective-permute-start.20 = (bf16[8,64,256]{2,1,0:T(8,128)(2,1)S(1)}, bf16[8,64,256]{2,1,0:T(8,128)(2,1)S(1)}, u32[]{:S(2)}, u32[]{:S(2)}) collective-permute-start(bf16[8,64,256]{2,1,0:T(8,128)(2,1)S(1)} %join_rows.2.refs_0_), channel_id=1, source_target_pairs={{0,4},{1,3},{2,6},{3,1},{4,0},{5,7},{6,2},{7,5},{8,12},{9,11},{10,... | collective-permute-start | bytes 786440 | tf_op jit(solution)/shard_map/ppermute | solution.py:372
  53.0 1.5 %collective-permute-start.21 = (bf16[8,64,256]{2,1,0:T(8,128)(2,1)S(1)}, bf16[8,64,256]{2,1,0:T(8,128)(2,1)S(1)}, u32[]{:S(2)}, u32[]{:S(2)}) collective-permute-start(bf16[8,64,256]{2,1,0:T(8,128)(2,1)S(1)} %join_rows.2.refs_0_), channel_id=1, source_target_pairs={{0,2},{1,5},{2,0},{3,7},{4,6},{5,1},{6,4},{7,3},{8,10},{9,13},{10,... | collective-permute-start | bytes 786440 | tf_op jit(solution)/shard_map/ppermute | solution.py:372
  54.5 1.6 %collective-permute-done.28.refs_1_ = bf16[8,64,256]{2,1,0:T(8,128)(2,1)S(1)} collective-permute-done((bf16[8,64,256]{2,1,0:T(8,128)(2,1)S(1)}, bf16[8,64,256]{2,1,0:T(8,128)(2,1)S(1)}, u32[]{:S(2)}, u32[]{:S(2)}) %collective-permute-start.28) | collective-permute-done | bytes 262176 | tf_op jit(solution)/shard_map/ppermute | solution.py:372
  56.7 5.0 %collective-permute-done.20.refs_1_ = bf16[8,64,256]{2,1,0:T(8,128)(2,1)S(1)} collective-permute-done((bf16[8,64,256]{2,1,0:T(8,128)(2,1)S(1)}, bf16[8,64,256]{2,1,0:T(8,128)(2,1)S(1)}, u32[]{:S(2)}, u32[]{:S(2)}) %collective-permute-start.20) | collective-permute-done | bytes 262176 | tf_op jit(solution)/shard_map/ppermute | solution.py:372
  62.4 1.4 %collective-permute-start.26 = (bf16[4,64,256]{2,1,0:T(8,128)(2,1)S(1)}, bf16[4,64,256]{2,1,0:T(8,128)(2,1)S(1)}, u32[]{:S(2)}, u32[]{:S(2)}) collective-permute-start(bf16[4,64,256]{2,1,0:T(8,128)(2,1)S(1)} %get-tuple-element.76), channel_id=1, source_target_pairs={{0,2},{1,5},{2,0},{3,7},{4,6},{5,1},{6,4},{7,3},{8,10},{9,13},{10,... | collective-permute-start | bytes 393224 | tf_op jit(solution)/shard_map/ppermute | solution.py:372
  63.8 2.5 %inverse_first.1.refs_4_ = bf16[16,1024,256]{2,1,0:T(8,128)(2,1)} custom-call(bf16[1024,256]{1,0:T(8,128)(2,1)S(1)} %get-tuple-element.43.table_ref, bf16[8,64,256]{2,1,0:T(8,128)(2,1)S(1)} %join_rows.3.refs_0_, bf16[8,64,256]{2,1,0:T(8,128)(2,1)S(1)} %collective-permute-done.28.refs_1_, bf16[8,64,256]{2,1,0:T(8,128)(2,1)S(1)} %collective-permute-done.25.refs_2_, ...), custom_call_target="tpu_custom_call" | custom-call | flops 1000 | bytes 1000 | tf_op jit(solution)/shard_map/inverse_first/pallas_call | solution.py:357
  66.8 1.8 %inverse_next.2.refs_4_ = bf16[16,1024,256]{2,1,0:T(8,128)(2,1)} custom-call(bf16[1024,256]{1,0:T(8,128)(2,1)S(1)} %get-tuple-element.43.table_ref, bf16[8,64,256]{2,1,0:T(8,128)(2,1)S(1)} %join_rows.2.refs_0_, bf16[8,64,256]{2,1,0:T(8,128)(2,1)S(1)} %collective-permute-done.20.refs_1_, ...), custom_call_target="tpu_custom_call", output_to_operand_aliasing={{}: (5, {})} | custom-call | flops 1000 | bytes 1000 | tf_op jit(solution)/shard_map/inverse_next/pallas_call | solution.py:357
  68.5 1.8 %inverse_next.3 = bf16[16,1024,256]{2,1,0:T(8,128)(2,1)} custom-call(bf16[1024,256]{1,0:T(8,128)(2,1)S(1)} %get-tuple-element.43.table_ref, bf16[8,64,256]{2,1,0:T(8,128)(2,1)S(1)} %join_rows.2.refs_0_, bf16[8,64,256]{2,1,0:T(8,128)(2,1)S(1)} %collective-permute-done.20.refs_1_, ...), custom_call_target="tpu_custom_call", output_to_operand_aliasing={{}: (5, {})} | custom-call | flops 1000 | bytes 1000 | tf_op jit(solution)/shard_map/inverse_next/pallas_call | solution.py:357
  (63 shorter events, 13.1 us)
Async XLA Ops:
  3.7 9.4 %collective-permute-start = (bf16[4,64,512]{2,1,0:T(8,128)(2,1)S(1)}, bf16[4,64,512]{2,1,0:T(8,128)(2,1)S(1)}, u32[]{:S(2)}, u32[]{:S(2)}) collective-permute-start(bf16[4,64,512]{2,1,0:T(8,128)(2,1)S(1)} %get-tuple-element.49), channel_id=1, source_target_pairs={{0,2},{1,5},{2,0},{3,7},{4,6},{5,1},{6,4},{7,3},{8,10},{9,13},{10,... | collective-permute-start | bytes 786440 | tf_op jit(solution)/shard_map/ppermute | solution.py:372
  6.7 7.2 %collective-permute-start.1 = (bf16[4,64,512]{2,1,0:T(8,128)(2,1)S(1)}, bf16[4,64,512]{2,1,0:T(8,128)(2,1)S(1)}, u32[]{:S(2)}, u32[]{:S(2)}) collective-permute-start(bf16[4,64,512]{2,1,0:T(8,128)(2,1)S(1)} %get-tuple-element.51), channel_id=1, source_target_pairs={{0,2},{1,5},{2,0},{3,7},{4,6},{5,1},{6,4},{7,3},{8,10},{9,13},{10,... | collective-permute-start | bytes 786440 | tf_op jit(solution)/shard_map/ppermute | solution.py:372
  9.9 7.5 %collective-permute-start.2 = (bf16[4,64,512]{2,1,0:T(8,128)(2,1)S(1)}, bf16[4,64,512]{2,1,0:T(8,128)(2,1)S(1)}, u32[]{:S(2)}, u32[]{:S(2)}) collective-permute-start(bf16[4,64,512]{2,1,0:T(8,128)(2,1)S(1)} %get-tuple-element.53), channel_id=1, source_target_pairs={{0,2},{1,5},{2,0},{3,7},{4,6},{5,1},{6,4},{7,3},{8,10},{9,13},{10,... | collective-permute-start | bytes 786440 | tf_op jit(solution)/shard_map/ppermute | solution.py:372
  12.5 7.5 %collective-permute-start.3 = (bf16[2048,128]{1,0:T(8,128)(2,1)S(1)}, bf16[2048,128]{1,0:T(8,128)(2,1)S(1)}, u32[]{:S(2)}, u32[]{:S(2)}) collective-permute-start(bf16[2048,128]{1,0:T(8,128)(2,1)S(1)} %get-tuple-element.45.refs_3_), channel_id=1, source_target_pairs={{0,1},{1,0},{2,3},{3,2},{4,5},{5,4},{6,7},{7,6},{8,9},{9,8},{10,11... | collective-permute-start | bytes 1572872 | tf_op jit(solution)/shard_map/ppermute | solution.py:379
  12.5 9.0 %collective-permute-start.4 = (bf16[2048,128]{1,0:T(8,128)(2,1)S(1)}, bf16[2048,128]{1,0:T(8,128)(2,1)S(1)}, u32[]{:S(2)}, u32[]{:S(2)}) collective-permute-start(bf16[2048,128]{1,0:T(8,128)(2,1)S(1)} %get-tuple-element.46.refs_4_), channel_id=1, source_target_pairs={{0,1},{1,0},{2,3},{3,2},{4,5},{5,4},{6,7},{7,6},{8,9},{9,8},{10,11... | collective-permute-start | bytes 1572872 | tf_op jit(solution)/shard_map/ppermute | solution.py:379
  13.0 8.5 %collective-permute-start.5 = (bf16[2048,128]{1,0:T(8,128)(2,1)S(1)}, bf16[2048,128]{1,0:T(8,128)(2,1)S(1)}, u32[]{:S(2)}, u32[]{:S(2)}) collective-permute-start(bf16[2048,128]{1,0:T(8,128)(2,1)S(1)} %get-tuple-element.47.refs_5_), channel_id=1, source_target_pairs={{0,1},{1,0},{2,3},{3,2},{4,5},{5,4},{6,7},{7,6},{8,9},{9,8},{10,11... | collective-permute-start | bytes 1572872 | tf_op jit(solution)/shard_map/ppermute | solution.py:379
  13.8 8.0 %collective-permute-start.6 = (bf16[4,64,512]{2,1,0:T(8,128)(2,1)S(1)}, bf16[4,64,512]{2,1,0:T(8,128)(2,1)S(1)}, u32[]{:S(2)}, u32[]{:S(2)}) collective-permute-start(bf16[4,64,512]{2,1,0:T(8,128)(2,1)S(1)} %sum_onward.2), channel_id=1, source_target_pairs={{0,4},{1,3},{2,6},{3,1},{4,0},{5,7},{6,2},{7,5},{8,12},{9,11},{10,... | collective-permute-start | bytes 786440 | tf_op jit(solution)/shard_map/ppermute | solution.py:372
  17.4 9.6 %collective-permute-start.7 = (bf16[4,64,512]{2,1,0:T(8,128)(2,1)S(1)}, bf16[4,64,512]{2,1,0:T(8,128)(2,1)S(1)}, u32[]{:S(2)}, u32[]{:S(2)}) collective-permute-start(bf16[4,64,512]{2,1,0:T(8,128)(2,1)S(1)} %get-tuple-element.58), channel_id=1, source_target_pairs={{0,2},{1,5},{2,0},{3,7},{4,6},{5,1},{6,4},{7,3},{8,10},{9,13},{10,... | collective-permute-start | bytes 786440 | tf_op jit(solution)/shard_map/ppermute | solution.py:372
  20.0 7.1 %collective-permute-start.8 = (bf16[4,64,512]{2,1,0:T(8,128)(2,1)S(1)}, bf16[4,64,512]{2,1,0:T(8,128)(2,1)S(1)}, u32[]{:S(2)}, u32[]{:S(2)}) collective-permute-start(bf16[4,64,512]{2,1,0:T(8,128)(2,1)S(1)} %sum_onward.3), channel_id=1, source_target_pairs={{0,4},{1,3},{2,6},{3,1},{4,0},{5,7},{6,2},{7,5},{8,12},{9,11},{10,... | collective-permute-start | bytes 786440 | tf_op jit(solution)/shard_map/ppermute | solution.py:372
  21.9 9.1 %collective-permute-start.9 = (bf16[4,16,512]{2,1,0:T(8,128)(2,1)S(1)}, bf16[4,16,512]{2,1,0:T(8,128)(2,1)S(1)}, u32[]{:S(2)}, u32[]{:S(2)}) collective-permute-start(bf16[4,16,512]{2,1,0:T(8,128)(2,1)S(1)} %get-tuple-element.61), channel_id=1, source_target_pairs={{0,24},{1,25},{2,26},{3,27},{4,28},{5,29},{6,30},{7,31},{8,16},{9,... | collective-permute-start | bytes 196616 | tf_op jit(solution)/shard_map/ppermute | solution.py:372
  26.4 6.6 %collective-permute-start.10 = (bf16[4,16,512]{2,1,0:T(8,128)(2,1)S(1)}, bf16[4,16,512]{2,1,0:T(8,128)(2,1)S(1)}, u32[]{:S(2)}, u32[]{:S(2)}) collective-permute-start(bf16[4,16,512]{2,1,0:T(8,128)(2,1)S(1)} %get-tuple-element.62), channel_id=1, source_target_pairs={{0,16},{1,17},{2,18},{3,19},{4,20},{5,21},{6,22},{7,23},{8,24},{9,... | collective-permute-start | bytes 196616 | tf_op jit(solution)/shard_map/ppermute | solution.py:372
  26.4 6.6 %collective-permute-start.11 = (bf16[4,16,512]{2,1,0:T(8,128)(2,1)S(1)}, bf16[4,16,512]{2,1,0:T(8,128)(2,1)S(1)}, u32[]{:S(2)}, u32[]{:S(2)}) collective-permute-start(bf16[4,16,512]{2,1,0:T(8,128)(2,1)S(1)} %get-tuple-element.63), channel_id=1, source_target_pairs={{0,8},{1,9},{2,10},{3,11},{4,12},{5,13},{6,14},{7,15},{8,0},{9,1},... | collective-permute-start | bytes 196616 | tf_op jit(solution)/shard_map/ppermute | solution.py:372
  27.1 10.8 %collective-permute-start.13 = (bf16[4,16,512]{2,1,0:T(8,128)(2,1)S(1)}, bf16[4,16,512]{2,1,0:T(8,128)(2,1)S(1)}, u32[]{:S(2)}, u32[]{:S(2)}) collective-permute-start(bf16[4,16,512]{2,1,0:T(8,128)(2,1)S(1)} %get-tuple-element.67), channel_id=1, source_target_pairs={{0,24},{1,25},{2,26},{3,27},{4,28},{5,29},{6,30},{7,31},{8,16},{9,... | collective-permute-start | bytes 196616 | tf_op jit(solution)/shard_map/ppermute | solution.py:372
  30.9 9.0 %collective-permute-start.14 = (bf16[4,16,512]{2,1,0:T(8,128)(2,1)S(1)}, bf16[4,16,512]{2,1,0:T(8,128)(2,1)S(1)}, u32[]{:S(2)}, u32[]{:S(2)}) collective-permute-start(bf16[4,16,512]{2,1,0:T(8,128)(2,1)S(1)} %get-tuple-element.68), channel_id=1, source_target_pairs={{0,16},{1,17},{2,18},{3,19},{4,20},{5,21},{6,22},{7,23},{8,24},{9,... | collective-permute-start | bytes 196616 | tf_op jit(solution)/shard_map/ppermute | solution.py:372
  30.9 8.9 %collective-permute-start.15 = (bf16[4,16,512]{2,1,0:T(8,128)(2,1)S(1)}, bf16[4,16,512]{2,1,0:T(8,128)(2,1)S(1)}, u32[]{:S(2)}, u32[]{:S(2)}) collective-permute-start(bf16[4,16,512]{2,1,0:T(8,128)(2,1)S(1)} %get-tuple-element.69), channel_id=1, source_target_pairs={{0,8},{1,9},{2,10},{3,11},{4,12},{5,13},{6,14},{7,15},{8,0},{9,1},... | collective-permute-start | bytes 196616 | tf_op jit(solution)/shard_map/ppermute | solution.py:372
  35.5 9.3 %collective-permute-start.24 = (bf16[8,16,256]{2,1,0:T(8,128)(2,1)S(1)}, bf16[8,16,256]{2,1,0:T(8,128)(2,1)S(1)}, u32[]{:S(2)}, u32[]{:S(2)}) collective-permute-start(bf16[8,16,256]{2,1,0:T(8,128)(2,1)S(1)} %constant_dynamic-update-slice_fusion.refs_0_), channel_id=1, source_target_pairs={{0,24},{1,25},{2,26},{3,27},{4,28},{5,29},{6,30},{7,31},{8,16},{9,... | collective-permute-start | bytes 196616 | tf_op jit(solution)/shard_map/ppermute | solution.py:372
  37.9 8.9 %collective-permute-start.23 = (bf16[8,16,256]{2,1,0:T(8,128)(2,1)S(1)}, bf16[8,16,256]{2,1,0:T(8,128)(2,1)S(1)}, u32[]{:S(2)}, u32[]{:S(2)}) collective-permute-start(bf16[8,16,256]{2,1,0:T(8,128)(2,1)S(1)} %constant_dynamic-update-slice_fusion.refs_0_), channel_id=1, source_target_pairs={{0,16},{1,17},{2,18},{3,19},{4,20},{5,21},{6,22},{7,23},{8,24},{9,... | collective-permute-start | bytes 196616 | tf_op jit(solution)/shard_map/ppermute | solution.py:372
  37.9 8.9 %collective-permute-start.22 = (bf16[8,16,256]{2,1,0:T(8,128)(2,1)S(1)}, bf16[8,16,256]{2,1,0:T(8,128)(2,1)S(1)}, u32[]{:S(2)}, u32[]{:S(2)}) collective-permute-start(bf16[8,16,256]{2,1,0:T(8,128)(2,1)S(1)} %constant_dynamic-update-slice_fusion.refs_0_), channel_id=1, source_target_pairs={{0,8},{1,9},{2,10},{3,11},{4,12},{5,13},{6,14},{7,15},{8,0},{9,1},... | collective-permute-start | bytes 196616 | tf_op jit(solution)/shard_map/ppermute | solution.py:372
  42.4 7.7 %collective-permute-start.19 = (bf16[8,16,256]{2,1,0:T(8,128)(2,1)S(1)}, bf16[8,16,256]{2,1,0:T(8,128)(2,1)S(1)}, u32[]{:S(2)}, u32[]{:S(2)}) collective-permute-start(bf16[8,16,256]{2,1,0:T(8,128)(2,1)S(1)} %constant_dynamic-update-slice_fusion.2.refs_0_), channel_id=1, source_target_pairs={{0,24},{1,25},{2,26},{3,27},{4,28},{5,29},{6,30},{7,31},{8,16},{9,... | collective-permute-start | bytes 196616 | tf_op jit(solution)/shard_map/ppermute | solution.py:372
  46.8 9.2 %collective-permute-start.28 = (bf16[8,64,256]{2,1,0:T(8,128)(2,1)S(1)}, bf16[8,64,256]{2,1,0:T(8,128)(2,1)S(1)}, u32[]{:S(2)}, u32[]{:S(2)}) collective-permute-start(bf16[8,64,256]{2,1,0:T(8,128)(2,1)S(1)} %join_rows.3.refs_0_), channel_id=1, source_target_pairs={{0,4},{1,3},{2,6},{3,1},{4,0},{5,7},{6,2},{7,5},{8,12},{9,11},{10,... | collective-permute-start | bytes 786440 | tf_op jit(solution)/shard_map/ppermute | solution.py:372
  48.6 8.1 %collective-permute-start.25 = (bf16[8,64,256]{2,1,0:T(8,128)(2,1)S(1)}, bf16[8,64,256]{2,1,0:T(8,128)(2,1)S(1)}, u32[]{:S(2)}, u32[]{:S(2)}) collective-permute-start(bf16[8,64,256]{2,1,0:T(8,128)(2,1)S(1)} %join_rows.3.refs_0_), channel_id=1, source_target_pairs={{0,2},{1,5},{2,0},{3,7},{4,6},{5,1},{6,4},{7,3},{8,10},{9,13},{10,... | collective-permute-start | bytes 786440 | tf_op jit(solution)/shard_map/ppermute | solution.py:372
  51.2 10.5 %collective-permute-start.20 = (bf16[8,64,256]{2,1,0:T(8,128)(2,1)S(1)}, bf16[8,64,256]{2,1,0:T(8,128)(2,1)S(1)}, u32[]{:S(2)}, u32[]{:S(2)}) collective-permute-start(bf16[8,64,256]{2,1,0:T(8,128)(2,1)S(1)} %join_rows.2.refs_0_), channel_id=1, source_target_pairs={{0,4},{1,3},{2,6},{3,1},{4,0},{5,7},{6,2},{7,5},{8,12},{9,11},{10,... | collective-permute-start | bytes 786440 | tf_op jit(solution)/shard_map/ppermute | solution.py:372
  53.0 13.3 %collective-permute-start.21 = (bf16[8,64,256]{2,1,0:T(8,128)(2,1)S(1)}, bf16[8,64,256]{2,1,0:T(8,128)(2,1)S(1)}, u32[]{:S(2)}, u32[]{:S(2)}) collective-permute-start(bf16[8,64,256]{2,1,0:T(8,128)(2,1)S(1)} %join_rows.2.refs_0_), channel_id=1, source_target_pairs={{0,2},{1,5},{2,0},{3,7},{4,6},{5,1},{6,4},{7,3},{8,10},{9,13},{10,... | collective-permute-start | bytes 786440 | tf_op jit(solution)/shard_map/ppermute | solution.py:372
  56.1 7.7 %collective-permute-start.29 = (bf16[8,64,256]{2,1,0:T(8,128)(2,1)S(1)}, bf16[8,64,256]{2,1,0:T(8,128)(2,1)S(1)}, u32[]{:S(2)}, u32[]{:S(2)}) collective-permute-start(bf16[8,64,256]{2,1,0:T(8,128)(2,1)S(1)} %collective-permute-done.28.refs_1_), channel_id=1, source_target_pairs={{0,2},{1,5},{2,0},{3,7},{4,6},{5,1},{6,4},{7,3},{8,10},{9,13},{10,... | collective-permute-start | bytes 786440 | tf_op jit(solution)/shard_map/ppermute | solution.py:372
  (9 other events, 42.0 us)
